TPU v7x, 32 devices: a whole 2x2x4 slice. The times are simulated.
32 devices in a mesh: dp: 8 (over z, y), head: 4 (over x, core).
Axes of the slice: x: 2, y: 2, z: 4, core: 2. Of those that a mesh axis runs over, the one named last changes fastest.
Arguments:
- queries: bfloat16 [2048, 1536], P(('dp', 'head')), may hold values from -100 to 100
- fresh_keyvals: bfloat16 [2048, 512], P(('dp', 'head')), may hold values from -4.1 to 4.1
- ssm_input: bfloat16 [2048, 3072], P(('dp', 'head')), may hold values from -4 to 4
- gate_input: bfloat16 [2048, 3072], P(('dp', 'head')), may hold values from -40 to 40
- state_maps: bfloat16 [2048, 512], P(('dp', 'head')), may hold values from -4 to 4
- step_logit: bfloat16 [2048, 24], P(('dp', 'head')), may hold values from -6 to 8
- slot_mask: int32 [2048], P(('dp', 'head')), may hold values 0 or 1
- cache_pool: bfloat16 [64, 32, 256], P('dp', 'head'), may hold values from -4 to 4
- page_map: int32 [8, 8], P('dp'), may hold values from 0 to 7, each once within a row
- cached_lengths: int32 [8], P('dp'), may hold values from 1 to 128, 512 in all
- prior_state: bfloat16 [8, 24, 128, 256], P('dp', 'head'), may hold values from -0.8984375 to 0.8984375
- decay_log: float32 [24], P('head'), may hold values from -4.61 to 0.7
- step_bias: float32 [24], P('head'), may hold values from -1 to 1
- skip_gain: float32 [24], P('head'), may hold values from 0.5 to 1.5
- norm_gain: float32 [3072], replicated, may hold values from 0.1 to 1.9
Outputs:
- mixed: bfloat16 [2048, 4608], P(('dp', 'head'))
Inputs may be any that keep to these rules, and one draw needn't show every extreme that they name: `page_map`: each row is a permutation of 0 to 7. `cached_lengths`: the lengths sum to 512; the largest is exactly 128.
All inputs are finite; a program needn't handle non-finite values. No bound on the sum of `slot_mask` or of `cached_lengths` on one device may be relied on, other than what follows from the above.
Results may differ from a plain program's by a relative error of at most 0.012.
Values may be sent and summed in bfloat16 or wider, within the bound.
No kernel may reach another device: no remote copies, remote signals or barrier semaphores. Data moves between devices by JAX's collectives and lax.ppermute only.
A program may use at most 64 MiB of HBM per device.

v0:
```python
import math

import jax
import jax.numpy as jnp
from jax import lax
from jax.sharding import PartitionSpec as P

HD = 128
STATE = 256
MI = 3072


HIGHEST = lax.Precision.HIGHEST
EPSILON = 1e-05


def swapped(block, axis, distance):
    count = lax.axis_size(axis)
    route = []
    for low in range(count):
        high = low | 1 << distance
        if high != low and high < count:
            route += [(low, high), (high, low)]
    return lax.ppermute(block, axis, route)


def attention(query_rows, all_keys, all_values, cached_count, valid_rows):
    length = query_rows.shape[0]
    key_count = all_keys.shape[0]
    cached_positions = key_count - length
    row_block = min(512, length)
    inv_scale = 1.0 / math.sqrt(HD)
    key_slots = jnp.arange(key_count, dtype=jnp.int32)
    new_index = key_slots - cached_positions
    live_new = jnp.concatenate([jnp.zeros((cached_positions,), dtype=bool), valid_rows])
    key_live = jnp.where(key_slots < cached_positions, key_slots < cached_count, live_new)
    results = []
    for head_num in range(query_rows.shape[1] // HD):
        block_query = query_rows[0:row_block, head_num * HD : (head_num + 1) * HD]
        row_ids = 0 + jnp.arange(row_block, dtype=jnp.int32)
        allowed = key_live[None, :] & (
            (key_slots[None, :] < cached_positions) | (new_index[None, :] <= row_ids[:, None])
        )
        scores = jnp.dot(block_query, all_keys.T, preferred_element_type=jnp.float32) * inv_scale
        scores = jnp.where(allowed, scores, -jnp.inf)
        row_max = jnp.max(scores, axis=1, keepdims=True)
        exp_terms = jnp.exp(scores - row_max)
        row_total = jnp.sum(exp_terms, axis=1, keepdims=True)
        weighted_values = jnp.dot(
            exp_terms.astype(jnp.bfloat16), all_values, preferred_element_type=jnp.float32
        )
        pieces = weighted_values / row_total
        results.append(pieces)
    joined = jnp.concatenate(results, axis=1) * valid_rows[:, None].astype(jnp.float32)
    return joined.astype(jnp.bfloat16)


def block_scan(inputs, in_raw, out_raw, steps, log_decay, carried):
    length = inputs.shape[0]
    block_len = min(128, length)
    causal = jnp.arange(block_len)[:, None] >= jnp.arange(block_len)[None, :]
    outputs = []
    for offset in range(0, length, block_len):
        block_input = inputs[offset : offset + block_len]
        block_in_raw = in_raw[offset : offset + block_len]
        block_out_raw = out_raw[offset : offset + block_len]
        block_in_map = block_in_raw.astype(jnp.float32)
        block_out_map = block_out_raw.astype(jnp.float32)
        block_steps = steps[offset : offset + block_len]
        cumulative = jnp.cumsum(log_decay[offset : offset + block_len], axis=0)
        log_gaps = cumulative[:, None, :] - cumulative[None, :, :]
        decays = jnp.exp(jnp.where(causal[:, :, None], log_gaps, -jnp.inf))
        intersections = jnp.dot(block_out_raw, block_in_raw.T, preferred_element_type=jnp.float32)
        weights = intersections[:, :, None] * decays * block_steps[None, :, :]
        within = jnp.einsum("tsh,shp->thp", weights, block_input, precision=HIGHEST)
        from_state = (
            jnp.einsum("tn,hpn->thp", block_out_map, carried, precision=HIGHEST)
            * jnp.exp(cumulative)[:, :, None]
        )
        outputs.append(within + from_state)
        tail_weight = jnp.exp(cumulative[-1:, :] - cumulative) * block_steps
        carried = carried * jnp.exp(cumulative[-1])[:, None, None] + jnp.einsum(
            "shp,sn->hpn", block_input * tail_weight[:, :, None], block_in_map, precision=HIGHEST
        )
    return jnp.concatenate(outputs, axis=0)


def state_space(inputs, maps, step_rows, valid_rows, decay_log, step_bias, skip_gain, prior):
    length = inputs.shape[0]
    head_count = decay_log.shape[0]
    valid_float = valid_rows.astype(jnp.float32)
    steps = (
        jax.nn.softplus(step_rows.astype(jnp.float32) + step_bias[None, :]) * valid_float[:, None]
    )
    log_decay = -jnp.exp(decay_log)[None, :] * steps
    input_float = inputs.astype(jnp.float32).reshape(length, head_count, -1)
    in_raw = maps[:, :STATE]
    out_raw = maps[:, STATE:]
    result = block_scan(input_float, in_raw, out_raw, steps, log_decay, prior.astype(jnp.float32))
    result = (result + skip_gain[None, :, None] * input_float) * valid_float[:, None, None]
    return result.reshape(length, -1).astype(jnp.bfloat16)


def local(
    queries,
    fresh_keyvals,
    ssm_input,
    gate_input,
    state_maps,
    step_logit,
    slot_mask,
    cache_pool,
    page_map,
    cached_lengths,
    prior_state,
    decay_log,
    step_bias,
    skip_gain,
    norm_gain,
):
    owner_index = lax.axis_index("head")
    is_even = owner_index % 2 == 0
    own_queries, own_keyval, own_input, own_steps, own_gate = (
        lax.all_to_all(queries, "head", split_axis=1, concat_axis=0, tiled=True),
        lax.all_to_all(fresh_keyvals, "head", split_axis=1, concat_axis=0, tiled=True),
        lax.all_to_all(ssm_input, "head", split_axis=1, concat_axis=0, tiled=True),
        lax.all_to_all(step_logit, "head", split_axis=1, concat_axis=0, tiled=True),
        lax.all_to_all(gate_input, "head", split_axis=1, concat_axis=0, tiled=True),
    )
    all_maps, all_mask = (
        lax.all_gather(state_maps, "head", axis=0, tiled=True),
        lax.all_gather(slot_mask.astype(jnp.bfloat16), "head", axis=0, tiled=True),
    )
    valid_rows = all_mask.astype(jnp.float32) > 0.5
    arrived = lax.all_to_all(cache_pool, "dp", split_axis=0, concat_axis=0, tiled=True)
    page_rows = jnp.take(arrived, page_map[0], axis=0)
    other_pages, other_keyval = swapped((page_rows, own_keyval), "head", 0)
    lower_half = jnp.where(is_even, page_rows, other_pages)
    upper_half = jnp.where(is_even, other_pages, page_rows)
    cache_rows = jnp.stack([lower_half, upper_half], axis=1).reshape(-1, 2 * HD)
    new_keys = jnp.where(is_even, own_keyval, other_keyval)
    new_values = jnp.where(is_even, other_keyval, own_keyval)
    all_keys = jnp.concatenate([cache_rows[:, :HD], new_keys], axis=0)
    all_values = jnp.concatenate([cache_rows[:, HD:], new_values], axis=0)
    attended = attention(own_queries, all_keys, all_values, cached_lengths[0], valid_rows)
    scanned = state_space(
        own_input, all_maps, own_steps, valid_rows, decay_log, step_bias, skip_gain, prior_state[0]
    )
    gated = scanned.astype(jnp.float32) * jax.nn.silu(own_gate.astype(jnp.float32))
    square_sums = lax.psum(jnp.sum(gated * gated, axis=1), "head")
    part_width = gated.shape[1]
    gain_part = lax.dynamic_slice_in_dim(norm_gain, owner_index * part_width, part_width)
    normed = (gated * lax.rsqrt(square_sums / MI + EPSILON)[:, None] * gain_part[None, :]).astype(
        jnp.bfloat16
    )
    attention_rows, normed_rows = (
        lax.all_to_all(attended, "head", split_axis=0, concat_axis=1, tiled=True),
        lax.all_to_all(normed, "head", split_axis=0, concat_axis=1, tiled=True),
    )
    result = jnp.concatenate([attention_rows, normed_rows], axis=1)
    return result


def solution(mesh):
    in_specs = (
        P(("dp", "head"), None),
        P(("dp", "head"), None),
        P(("dp", "head"), None),
        P(("dp", "head"), None),
        P(("dp", "head"), None),
        P(("dp", "head"), None),
        P(("dp", "head")),
        P("dp", "head", None),
        P("dp", None),
        P("dp"),
        P("dp", "head", None, None),
        P("head"),
        P("head"),
        P("head"),
        P(),
    )
    out_specs = P(("dp", "head"), None)
    return jax.shard_map(local, mesh=mesh, in_specs=in_specs, out_specs=out_specs, check_vma=False)
```

profile of v0, /device:TPU:0, one launch (start us, length us, event | category | flops | bytes accessed | tf_op | source)
XLA Modules:
  0.0 101.8 jit_solution(9935204021642409191)
XLA Ops:
  0.0 0.8 all_to_all.99
  0.8 0.7 reshape.191
  1.5 4.2 %all-to-all-start.4 = ((bf16[4,2,192]{2,1,0:T(2,128)(2,1)}), bf16[4,2,192]{2,1,0:T(2,128)(2,1)S(1)}, u32[]{:S(2)}, u32[]{:S(2)}) async-start(bf16[4,2,192]{2,1,0:T(2,128)(2,1)} %reshape.191), calls=%async_computation.4 | async-start | bytes 8192 | tf_op jit(solution)/shard_map/all_to_all | solution.py:127
  5.7 0.7 fusion.71
  6.4 0.7 compare_and_fusion
  7.1 6.5 %all_gather.7 = bf16[256,512]{1,0:T(8,128)(2,1)S(1)} all-gather(bf16[64,512]{1,0:T(8,128)(2,1)} %param.19), channel_id=1, replica_groups=mesh['dp'=8,'head'=4] {'head'}, dimensions={0}, use_global_device_ids=true | all-gather | bytes 327680 | tf_op jit(solution)/shard_map/all_gather | solution.py:131
  13.9 0.6 copy_bitcast_fusion.3
  16.0 7.1 %all-reduce.1 = bf16[256]{0:T(256)(128)(2,1)S(1)} all-reduce(bf16[256]{0:T(256)(128)(2,1)S(1)} %dynamic-update-slice), channel_id=1, replica_groups=mesh['dp'=8,'head'=4] {'head'}, use_global_device_ids=true, to_apply=%add.1 | all-reduce | flops 256 | bytes 1024
  23.9 0.7 copy.179
  24.7 0.8 copy.178
  25.5 0.8 copy.177
  26.3 0.8 dynamic_slice.3
  27.0 6.3 %all-to-all-start = ((bf16[8,8,256]{2,1,0:T(8,128)(2,1)}), bf16[8,8,256]{2,1,0:T(8,128)(2,1)S(1)}, u32[]{:S(2)}, u32[]{:S(2)}) async-start(bf16[8,8,256]{2,1,0:T(8,128)(2,1)} %param.22), calls=%async_computation | async-start | bytes 65536 | tf_op jit(solution)/shard_map/all_to_all | solution.py:135
  34.4 5.6 %all-to-all-done = bf16[8,8,256]{2,1,0:T(8,128)(2,1)S(1)} async-done(((bf16[8,8,256]{2,1,0:T(8,128)(2,1)}), bf16[8,8,256]{2,1,0:T(8,128)(2,1)S(1)}, u32[]{:S(2)}, u32[]{:S(2)}) %all-to-all-start) | async-done | bytes 32800 | tf_op jit(solution)/shard_map/all_to_all | solution.py:135
  40.0 3.3 %all-to-all-start.1 = ((bf16[64,4,128]{2,0,1:T(8,128)(2,1)}), bf16[64,4,128]{2,0,1:T(8,128)(2,1)S(1)}, u32[]{:S(2)}, u32[]{:S(2)}) async-start(bf16[64,4,128]{2,0,1:T(8,128)(2,1)} %copy_bitcast_fusion.3), calls=%async_computation.1 | async-start | bytes 131072 | tf_op jit(solution)/shard_map/all_to_all | solution.py:125
  45.0 2.4 %all-to-all-done.1 = bf16[64,4,128]{2,0,1:T(8,128)(2,1)S(1)} async-done(((bf16[64,4,128]{2,0,1:T(8,128)(2,1)}), bf16[64,4,128]{2,0,1:T(8,128)(2,1)S(1)}, u32[]{:S(2)}, u32[]{:S(2)}) %all-to-all-start.1) | async-done | bytes 65568 | tf_op jit(solution)/shard_map/all_to_all | solution.py:125
  47.4 3.4 %all-to-all-start.2 = ((bf16[64,4,384]{2,0,1:T(8,128)(2,1)}), bf16[64,4,384]{2,0,1:T(8,128)(2,1)S(1)}, u32[]{:S(2)}, u32[]{:S(2)}) async-start(bf16[64,4,384]{2,0,1:T(8,128)(2,1)} %bitcast.121), calls=%async_computation.2 | async-start | bytes 393216 | tf_op jit(solution)/shard_map/all_to_all | solution.py:124
  51.3 0.8 collective-permute-done.1
  52.1 3.9 %all-to-all-done.2 = bf16[64,4,384]{2,0,1:T(8,128)(2,1)S(1)} async-done(((bf16[64,4,384]{2,0,1:T(8,128)(2,1)}), bf16[64,4,384]{2,0,1:T(8,128)(2,1)S(1)}, u32[]{:S(2)}, u32[]{:S(2)}) %all-to-all-start.2) | async-done | bytes 196640 | tf_op jit(solution)/shard_map/all_to_all | solution.py:124
  56.1 3.5 %all-to-all-start.5 = ((bf16[64,4,768]{2,0,1:T(8,128)(2,1)}), bf16[64,4,768]{2,0,1:T(8,128)(2,1)S(1)}, u32[]{:S(2)}, u32[]{:S(2)}) async-start(bf16[64,4,768]{2,0,1:T(8,128)(2,1)} %bitcast.120), calls=%async_computation.5 | async-start | bytes 786432 | tf_op jit(solution)/shard_map/all_to_all | solution.py:126
  61.4 0.8 fusion.13
  62.2 4.7 %all-to-all-done.5 = bf16[64,4,768]{2,0,1:T(8,128)(2,1)S(1)} async-done(((bf16[64,4,768]{2,0,1:T(8,128)(2,1)}), bf16[64,4,768]{2,0,1:T(8,128)(2,1)S(1)}, u32[]{:S(2)}, u32[]{:S(2)}) %all-to-all-start.5) | async-done | bytes 393248 | tf_op jit(solution)/shard_map/all_to_all | solution.py:126
  66.9 3.5 %all-to-all-start.6 = ((bf16[64,4,768]{2,0,1:T(8,128)(2,1)}), bf16[64,4,768]{2,0,1:T(8,128)(2,1)S(1)}, u32[]{:S(2)}, u32[]{:S(2)}) async-start(bf16[64,4,768]{2,0,1:T(8,128)(2,1)} %bitcast.119), calls=%async_computation.6 | async-start | bytes 786432 | tf_op jit(solution)/shard_map/all_to_all | solution.py:128
  72.2 0.7 fusion.7
  73.0 0.7 fusion.6
  73.9 3.9 %all-to-all-done.6 = bf16[64,4,768]{2,0,1:T(8,128)(2,1)S(1)} async-done(((bf16[64,4,768]{2,0,1:T(8,128)(2,1)}), bf16[64,4,768]{2,0,1:T(8,128)(2,1)S(1)}, u32[]{:S(2)}, u32[]{:S(2)}) %all-to-all-start.6) | async-done | bytes 393248 | tf_op jit(solution)/shard_map/all_to_all | solution.py:128
  77.8 3.4 %all-to-all-start.3 = ((bf16[4,64,384]{2,1,0:T(8,128)(2,1)}), bf16[4,64,384]{2,1,0:T(8,128)(2,1)S(1)}, u32[]{:S(2)}, u32[]{:S(2)}) async-start(bf16[4,64,384]{2,1,0:T(8,128)(2,1)} %fusion.13), calls=%async_computation.3 | async-start | bytes 393216 | tf_op jit(solution)/shard_map/all_to_all | solution.py:157
  81.7 7.4 %psum.7 = f32[256]{0:T(256)S(1)} all-reduce(f32[256]{0:T(256)S(1)} %reduce_sum.42), channel_id=1, replica_groups=mesh['dp'=8,'head'=4] {'head'}, use_global_device_ids=true, to_apply=%region_9.10 | all-reduce | flops 256 | bytes 2048 | tf_op jit(solution)/shard_map/psum | solution.py:150
  89.2 0.9 multiply_convert_fusion
  90.1 3.5 %all-to-all-start.7 = ((bf16[4,64,768]{2,1,0:T(8,128)(2,1)}), bf16[4,64,768]{2,1,0:T(8,128)(2,1)S(1)}, u32[]{:S(2)}, u32[]{:S(2)}) async-start(bf16[4,64,768]{2,1,0:T(8,128)(2,1)} %multiply_convert_fusion), calls=%async_computation.7 | async-start | bytes 786432 | tf_op jit(solution)/shard_map/all_to_all | solution.py:158
  93.6 7.4 %all-to-all-done.7 = bf16[4,64,768]{2,1,0:T(8,128)(2,1)S(1)} async-done(((bf16[4,64,768]{2,1,0:T(8,128)(2,1)}), bf16[4,64,768]{2,1,0:T(8,128)(2,1)S(1)}, u32[]{:S(2)}, u32[]{:S(2)}) %all-to-all-start.7) | async-done | bytes 393248 | tf_op jit(solution)/shard_map/all_to_all | solution.py:158
  101.0 0.9 pad_maximum_fusion.1
  (90 shorter events, 9.5 us)
Async XLA Ops:
  0.0 13.9 %copy-start = (bf16[64,512]{1,0:T(8,128)(2,1)S(1)}, bf16[64,512]{1,0:T(8,128)(2,1)}, u32[]{:S(2)}) copy-start(bf16[64,512]{1,0:T(8,128)(2,1)} %param.16) | copy-start | bytes 196612
  0.0 14.6 %copy-start.9 = (u32[32]{0:T(128)S(1)}, u32[32]{0:T(128)}, u32[]{:S(2)}) copy-start(u32[32]{0:T(128)} %constant.76) | copy-start | bytes 388
  0.0 14.5 %copy-start.7 = (s32[64]{0:T(128)S(1)}, s32[64]{0:T(128)}, u32[]{:S(2)}) copy-start(s32[64]{0:T(128)} %param.21) | copy-start | bytes 772
  0.0 23.8 %copy-start.8 = (f32[6]{0:T(128)S(1)}, f32[6]{0:T(128)}, u32[]{:S(2)}) copy-start(f32[6]{0:T(128)} %param.26) | copy-start | bytes 76
  0.0 23.8 %copy-start.5 = (f32[6]{0:T(128)S(1)}, f32[6]{0:T(128)}, u32[]{:S(2)}) copy-start(f32[6]{0:T(128)} %param.28) | copy-start | bytes 76
  0.0 23.9 %copy-start.4 = (bf16[64,1536]{1,0:T(8,128)(2,1)S(1)}, bf16[64,1536]{1,0:T(8,128)(2,1)}, u32[]{:S(2)}) copy-start(bf16[64,1536]{1,0:T(8,128)(2,1)} %param.15) | copy-start | bytes 589828
  0.0 24.7 %copy-start.2 = (bf16[64,3072]{1,0:T(8,128)(2,1)S(1)}, bf16[64,3072]{1,0:T(8,128)(2,1)}, u32[]{:S(2)}) copy-start(bf16[64,3072]{1,0:T(8,128)(2,1)} %param.17) | copy-start | bytes 1179652
  1.5 25.5 %all-to-all-start.4 = ((bf16[4,2,192]{2,1,0:T(2,128)(2,1)}), bf16[4,2,192]{2,1,0:T(2,128)(2,1)S(1)}, u32[]{:S(2)}, u32[]{:S(2)}) async-start(bf16[4,2,192]{2,1,0:T(2,128)(2,1)} %reshape.191), calls=%async_computation.4 | async-start | bytes 8192 | tf_op jit(solution)/shard_map/all_to_all | solution.py:127
  13.7 11.8 %copy-start.3 = (bf16[64,3072]{1,0:T(8,128)(2,1)S(1)}, bf16[64,3072]{1,0:T(8,128)(2,1)}, u32[]{:S(2)}) copy-start(bf16[64,3072]{1,0:T(8,128)(2,1)} %param.18) | copy-start | bytes 1179652
  24.7 8.8 %copy-start.6 = (f32[6]{0:T(128)S(1)}, f32[6]{0:T(128)}, u32[]{:S(2)}) copy-start(f32[6]{0:T(128)} %param.27) | copy-start | bytes 76
  25.5 8.6 %copy-start.1 = (bf16[1,6,128,256]{3,2,1,0:T(8,128)(2,1)S(1)}, bf16[1,6,128,256]{3,2,1,0:T(8,128)(2,1)}, u32[]{:S(2)}) copy-start(bf16[1,6,128,256]{3,2,1,0:T(8,128)(2,1)} %param.25) | copy-start | bytes 1179652
  27.0 13.0 %all-to-all-start = ((bf16[8,8,256]{2,1,0:T(8,128)(2,1)}), bf16[8,8,256]{2,1,0:T(8,128)(2,1)S(1)}, u32[]{:S(2)}, u32[]{:S(2)}) async-start(bf16[8,8,256]{2,1,0:T(8,128)(2,1)} %param.22), calls=%async_computation | async-start | bytes 65536 | tf_op jit(solution)/shard_map/all_to_all | solution.py:135
  40.0 7.4 %all-to-all-start.1 = ((bf16[64,4,128]{2,0,1:T(8,128)(2,1)}), bf16[64,4,128]{2,0,1:T(8,128)(2,1)S(1)}, u32[]{:S(2)}, u32[]{:S(2)}) async-start(bf16[64,4,128]{2,0,1:T(8,128)(2,1)} %copy_bitcast_fusion.3), calls=%async_computation.1 | async-start | bytes 131072 | tf_op jit(solution)/shard_map/all_to_all | solution.py:125
  43.9 7.3 %collective-permute-start = (bf16[8,8,256]{2,1,0:T(8,128)(2,1)S(1)}, bf16[8,8,256]{2,1,0:T(8,128)(2,1)S(1)}, u32[]{:S(2)}, u32[]{:S(2)}) collective-permute-start(bf16[8,8,256]{2,1,0:T(8,128)(2,1)S(1)} %broadcast_select_fusion.2), channel_id=1, source_target_pairs={{0,1},{1,0},{2,3},{3,2},{4,5},{5,4},{6,7},{7,6},{8,9},{9,8},{10,11... | collective-permute-start | bytes 98312 | tf_op jit(solution)/shard_map/ppermute | solution.py:24
  47.4 8.7 %all-to-all-start.2 = ((bf16[64,4,384]{2,0,1:T(8,128)(2,1)}), bf16[64,4,384]{2,0,1:T(8,128)(2,1)S(1)}, u32[]{:S(2)}, u32[]{:S(2)}) async-start(bf16[64,4,384]{2,0,1:T(8,128)(2,1)} %bitcast.121), calls=%async_computation.2 | async-start | bytes 393216 | tf_op jit(solution)/shard_map/all_to_all | solution.py:124
  50.8 1.4 %collective-permute-start.1 = (bf16[256,128]{1,0:T(8,128)(2,1)S(1)}, bf16[256,128]{1,0:T(8,128)(2,1)S(1)}, u32[]{:S(2)}, u32[]{:S(2)}) collective-permute-start(bf16[256,128]{1,0:T(8,128)(2,1)S(1)} %bitcast.134), channel_id=1, source_target_pairs={{0,1},{1,0},{2,3},{3,2},{4,5},{5,4},{6,7},{7,6},{8,9},{9,8},{10,11... | collective-permute-start | bytes 196616 | tf_op jit(solution)/shard_map/ppermute | solution.py:24
  56.1 10.9 %all-to-all-start.5 = ((bf16[64,4,768]{2,0,1:T(8,128)(2,1)}), bf16[64,4,768]{2,0,1:T(8,128)(2,1)S(1)}, u32[]{:S(2)}, u32[]{:S(2)}) async-start(bf16[64,4,768]{2,0,1:T(8,128)(2,1)} %bitcast.120), calls=%async_computation.5 | async-start | bytes 786432 | tf_op jit(solution)/shard_map/all_to_all | solution.py:126
  66.9 10.9 %all-to-all-start.6 = ((bf16[64,4,768]{2,0,1:T(8,128)(2,1)}), bf16[64,4,768]{2,0,1:T(8,128)(2,1)S(1)}, u32[]{:S(2)}, u32[]{:S(2)}) async-start(bf16[64,4,768]{2,0,1:T(8,128)(2,1)} %bitcast.119), calls=%async_computation.6 | async-start | bytes 786432 | tf_op jit(solution)/shard_map/all_to_all | solution.py:128
  77.8 12.3 %all-to-all-start.3 = ((bf16[4,64,384]{2,1,0:T(8,128)(2,1)}), bf16[4,64,384]{2,1,0:T(8,128)(2,1)S(1)}, u32[]{:S(2)}, u32[]{:S(2)}) async-start(bf16[4,64,384]{2,1,0:T(8,128)(2,1)} %fusion.13), calls=%async_computation.3 | async-start | bytes 393216 | tf_op jit(solution)/shard_map/all_to_all | solution.py:157
  90.1 10.9 %all-to-all-start.7 = ((bf16[4,64,768]{2,1,0:T(8,128)(2,1)}), bf16[4,64,768]{2,1,0:T(8,128)(2,1)S(1)}, u32[]{:S(2)}, u32[]{:S(2)}) async-start(bf16[4,64,768]{2,1,0:T(8,128)(2,1)} %multiply_convert_fusion), calls=%async_computation.7 | async-start | bytes 786432 | tf_op jit(solution)/shard_map/all_to_all | solution.py:158
where the time goes:
time: 103 us; the launch traced here: 102 us
  starting transfers between devices  31.9 us (31%)
  waiting for transfers between devices  28.6 us (28%)
  blocking collectives  21 us (20%)
  local copies, waits for them, and re-layouts  8.61 us (8%)
  other arithmetic  5.66 us (5%)
  matrix products  4.46 us (4%)
  between operations  1.67 us (2%)
    all_to_all x1, waiting for transfers between devices, local(): lax.all_to_all(normed, 'head', split_axis=0, concat_axis=1, tiled=True)  7.38 us
    psum x1, blocking collectives, local(): square_sums = lax.psum(jnp.sum(gated * gated, axis=1), 'head')  7.36 us
    unnamed x1, blocking collectives  7.11 us
    all_gather x1, blocking collectives, local(): lax.all_gather(state_maps, 'head', axis=0, tiled=True)  6.49 us
    all_to_all x1, starting transfers between devices, local(): lax.all_to_all(cache_pool, 'dp', split_axis=0, concat_axis=0, tiled=True)  6.27 us
    all_to_all x1, waiting for transfers between devices, local(): lax.all_to_all(cache_pool, 'dp', split_axis=0, concat_axis=0, tiled=True)  5.58 us
    all_to_all x1, waiting for transfers between devices, local(): lax.all_to_all(ssm_input, 'head', split_axis=1, concat_axis=0, tiled=True)  4.71 us
    all_to_all x1, starting transfers between devices, local(): lax.all_to_all(step_logit, 'head', split_axis=1, concat_axis=0, tiled=True)  4.21 us
  transfers between devices with their start and end apart: 10, of which 7 were waited for; matrix products, arithmetic and copies ran while one was open for 16% of the time, Pallas kernels for 0%

commit v1 on v0

v1 whole, which is shorter than its diff:
```python
import math

import jax
import jax.numpy as jnp
from jax import lax
from jax.experimental import pallas as pl
from jax.experimental.pallas import tpu as pltpu
from jax.sharding import PartitionSpec as P

HD = 128
QH = 12
KVH = 2
GROUP = QH // KVH
STATE = 256
MI = 3072
PAGE = 16
LANES = 128
EPSILON = 1e-05
BF16 = jnp.bfloat16
F32 = jnp.float32
HIGHEST = lax.Precision.HIGHEST
VMEM = pl.BlockSpec(memory_space=pltpu.VMEM)
SMEM = pl.BlockSpec(memory_space=pltpu.SMEM)


def call(kernel, outs, specs, scratch=(), limit=24 << 20):
    return pl.pallas_call(
        kernel,
        out_shape=[jax.ShapeDtypeStruct(shape, dtype) for shape, dtype in outs],
        in_specs=specs,
        out_specs=[VMEM] * len(outs),
        scratch_shapes=list(scratch),
        compiler_params=pltpu.CompilerParams(vmem_limit_bytes=limit),
    )


def columns(ref, owner, width):
    return ref[:, pl.ds(pl.multiple_of(owner * width, LANES), width)]


def iota(shape, dim):
    return lax.broadcasted_iota(jnp.int32, shape, dim)


def nt_dot(a, b, precision=None):
    return lax.dot_general(
        a, b, (((1,), (1,)), ((), ())), preferred_element_type=F32, precision=precision
    )


def pack_kernel(x_ref, maps_ref, logit_ref, mask_ref, small_ref, x1_ref, x2_ref, x3_ref):
    me = lax.axis_index("head")
    rows = x_ref.shape[0]
    width = x1_ref.shape[1]
    maps_width = maps_ref.shape[1]
    heads = logit_ref.shape[1]
    small_ref[:, :maps_width] = maps_ref[...]
    diagonal = iota((rows, rows), 0) == iota((rows, rows), 1)
    mask_row = jnp.broadcast_to(mask_ref[...], (rows, rows))
    mask_column = jnp.sum(
        jnp.where(diagonal & (mask_row > 0), 1.0, 0.0), axis=1, keepdims=True
    )
    small_ref[:, maps_width:] = jnp.broadcast_to(mask_column, (rows, LANES)).astype(BF16)
    small_ref[:, maps_width : maps_width + heads] = logit_ref[...]
    for hop, ref in ((1, x1_ref), (2, x2_ref), (3, x3_ref)):
        ref[...] = columns(x_ref, me ^ hop, width)


def scan_kernel(
    log_rate_ref, bias_ref, skip_ref,
    small0, small1, small2, small3, x_ref, x1, x2, x3, prior_ref,
    y0, y1, y2, y3,
    small, xs, ys,
):
    me = lax.axis_index("head")
    rows, width = x1.shape
    span = 4 * rows
    head_count = width // HD
    maps_width = 2 * STATE
    every_head = 4 * head_count
    def at(hop):
        return pl.ds(pl.multiple_of((me ^ hop) * rows, rows), rows)
    for hop, ref in enumerate((small0, small1, small2, small3)):
        small[at(hop), :] = ref[...]
    xs[at(0), :] = columns(x_ref, me, width)
    for hop, ref in ((1, x1), (2, x2), (3, x3)):
        xs[at(hop), :] = ref[...]

    logits = small[:, maps_width:]
    first = me * head_count
    pick_row, pick_lane = iota((8, LANES), 0), iota((8, LANES), 1)
    picked = jnp.where(pick_row < head_count, pick_row + first, every_head)
    by_row = jnp.where(picked == pick_lane, 1.0, 0.0).astype(BF16)
    pick_lane, pick_row = iota((LANES, LANES), 0), iota((LANES, LANES), 1)
    picked = jnp.where(pick_row < head_count, pick_row + first, every_head)
    by_lane = jnp.where(picked == pick_lane, 1.0, 0.0).astype(BF16)
    row_logits = nt_dot(by_row, logits)
    lane_logits = jnp.dot(logits, by_lane, preferred_element_type=F32)
    row_mask = row_logits[head_count : head_count + 1, :]
    lane_mask = lane_logits[:, head_count : head_count + 1]

    row_head, lane_head = iota((8, 1), 0), iota((1, LANES), 1)
    row_bias = row_rate = jnp.zeros((8, 1), F32)
    lane_bias = lane_rate = jnp.zeros((1, LANES), F32)
    for head in range(head_count):
        bias, log_rate = bias_ref[head], log_rate_ref[head]
        row_bias = jnp.where(row_head == head, bias, row_bias)
        row_rate = jnp.where(row_head == head, log_rate, row_rate)
        lane_bias = jnp.where(lane_head == head, bias, lane_bias)
        lane_rate = jnp.where(lane_head == head, log_rate, lane_rate)
    row_steps = jnp.log(1.0 + jnp.exp(row_logits + row_bias)) * row_mask
    lane_steps = jnp.log(1.0 + jnp.exp(lane_logits + lane_bias)) * lane_mask
    row_decay = -jnp.exp(row_rate) * row_steps
    lane_decay = -jnp.exp(lane_rate) * lane_steps
    token, source = iota((span, span), 0), iota((span, span), 1)
    upto = jnp.where(source <= token, 1.0, 0.0)
    row_sum = nt_dot(row_decay, upto, HIGHEST)
    lane_sum = jnp.dot(upto, lane_decay, preferred_element_type=F32, precision=HIGHEST)
    row_shift = row_sum - jnp.log(row_steps)

    in_map, out_map = small[:, :STATE], small[:, STATE : 2 * STATE]
    products = nt_dot(out_map, in_map)
    prior = prior_ref[0].reshape(width, STATE)
    from_prior = nt_dot(out_map, prior)
    causal = source <= token
    for head in range(head_count):
        cols = slice(head * HD, (head + 1) * HD)
        total = lane_sum[:, head : head + 1]
        gaps = jnp.where(causal, total - row_shift[head : head + 1, :], -jnp.inf)
        weights = (jnp.exp(gaps) * products).astype(BF16)
        x = xs[:, cols]
        y = jnp.dot(weights, x, preferred_element_type=F32)
        y = y + from_prior[:, cols] * jnp.exp(total) + skip_ref[head] * x.astype(F32)
        ys[:, cols] = (y * lane_mask).astype(BF16)
    for hop, ref in enumerate((y0, y1, y2, y3)):
        ref[...] = ys[at(hop), :]


def attention_kernel(
    page_map_ref, length_ref, query_ref, pages_ref, kv0, kv1, kv2, kv3, small0, small1, small2, small3, out_ref
):
    me = lax.axis_index("head")
    rows = query_ref.shape[0]
    slots = page_map_ref.shape[1]
    cached = slots * PAGE
    inv_scale = 1.0 / math.sqrt(HD)
    maps_width = 2 * STATE
    lane = iota((1, cached), 1)

    def place(page, base):
        return jnp.where(lane // PAGE == page_map_ref[0, page], page * PAGE, base)

    position = lax.fori_loop(0, slots, place, jnp.zeros((1, cached), jnp.int32), unroll=slots <= 8)
    position = position + lane % PAGE
    shut = [jnp.broadcast_to(jnp.where(position < length_ref[0], 0.0, -jnp.inf), (rows, cached))]
    ones = jnp.where(iota((8, LANES), 1) == LANES - 1, 1.0, 0.0).astype(BF16)
    token, source = iota((rows, rows), 0), iota((rows, rows), 1)
    own_mask = None
    for hop, ref in enumerate((small0, small1, small2, small3)):
        real = nt_dot(ones, ref[:, maps_width:])[0:1, :] > 0.5
        limit = token if hop == 0 else jnp.where((me ^ hop) < me, rows, -1)
        shut.append(jnp.where(real & (source <= limit), 0.0, -jnp.inf))
    shut = jnp.concatenate(shut, axis=1)
    shut = jnp.concatenate([shut] * GROUP, axis=0)
    keep = small0[:, maps_width + LANES - 1 :].astype(F32)
    pages = pages_ref[...].reshape(slots, KVH, PAGE, 2 * HD)
    for group in range(KVH):
        queries = jnp.concatenate(
            [query_ref[:, (group * GROUP + h) * HD : (group * GROUP + h + 1) * HD] for h in range(GROUP)],
            axis=0,
        )
        old = pages[:, group].reshape(cached, 2 * HD)
        base = 2 * group * HD
        keys = jnp.concatenate(
            [old[:, :HD]] + [ref[:, base : base + HD] for ref in (kv0, kv1, kv2, kv3)], axis=0
        )
        values = jnp.concatenate(
            [old[:, HD:]] + [ref[:, base + HD : base + 2 * HD] for ref in (kv0, kv1, kv2, kv3)], axis=0
        )
        scores = nt_dot(queries, keys) * inv_scale + shut
        top = jnp.max(scores, axis=1, keepdims=True)
        terms = jnp.exp(scores - top)
        total = jnp.sum(terms, axis=1, keepdims=True)
        mixed = jnp.dot(terms.astype(BF16), values, preferred_element_type=F32) / total
        for h in range(GROUP):
            head = group * GROUP + h
            out_ref[:, head * HD : (head + 1) * HD] = (mixed[h * rows : (h + 1) * rows] * keep).astype(BF16)


def final_kernel(attended_ref, gate_ref, gain_ref, y0, y1, y2, y3, out_ref, gated):
    me = lax.axis_index("head")
    rows, width = y0.shape
    heads_width = attended_ref.shape[1]
    out_ref[:, :heads_width] = attended_ref[...]
    squares = jnp.zeros((rows, 1), F32)
    for hop, ref in enumerate((y0, y1, y2, y3)):
        gate = columns(gate_ref, me ^ hop, width).astype(F32)
        part = ref[...].astype(F32) * (gate / (1.0 + jnp.exp(-gate)))
        gated[:, hop * width : (hop + 1) * width] = part
        squares = squares + jnp.sum(part * part, axis=1, keepdims=True)
    scale = lax.rsqrt(squares / MI + EPSILON)
    for hop in range(4):
        gain = columns(gain_ref, me ^ hop, width)
        part = gated[:, hop * width : (hop + 1) * width] * scale * gain
        start = pl.multiple_of(heads_width + (me ^ hop) * width, LANES)
        out_ref[:, pl.ds(start, width)] = part.astype(BF16)


def hopped(block, hop):
    return lax.ppermute(block, "head", [(i, i ^ hop) for i in range(4)])


def local(
    queries,
    fresh_keyvals,
    ssm_input,
    gate_input,
    state_maps,
    step_logit,
    slot_mask,
    cache_pool,
    page_map,
    cached_lengths,
    prior_state,
    decay_log,
    step_bias,
    skip_gain,
    norm_gain,
):
    rows = ssm_input.shape[0]
    width = MI // 4
    small_width = state_maps.shape[1] + LANES
    small, x1, x2, x3 = call(
        pack_kernel,
        [((rows, small_width), BF16)] + [((rows, width), BF16)] * 3,
        [VMEM] * 4,
    )(ssm_input, state_maps, step_logit, slot_mask.reshape(1, rows))
    small2 = hopped(small, 2)
    small1 = hopped(small, 1)
    x2 = hopped(x2, 2)
    x3 = hopped(x3, 3)
    x1 = hopped(x1, 1)
    kv2 = hopped(fresh_keyvals, 2)
    kv1 = hopped(fresh_keyvals, 1)
    small3 = hopped(small2, 1)
    kv3 = hopped(kv2, 1)

    slots, half = cache_pool.shape[0], cache_pool.shape[1]
    copies = jnp.broadcast_to(cache_pool[:, None], (slots, 4, half, 2 * HD)).reshape(slots * 4 * half, 2 * HD)
    pages = lax.all_to_all(copies, ("dp", "head"), split_axis=0, concat_axis=0, tiled=True)

    span = 4 * rows
    y0, y1, y2, y3 = call(
        scan_kernel,
        [((rows, width), BF16)] * 4,
        [SMEM] * 3 + [VMEM] * 9,
        [pltpu.VMEM((span, small_width), BF16), pltpu.VMEM((span, width), BF16), pltpu.VMEM((span, width), BF16)],
    )(
        decay_log, step_bias, skip_gain,
        small, small1, small2, small3, ssm_input, x1, x2, x3, prior_state,
    )
    y2 = hopped(y2, 2)
    y3 = hopped(y3, 3)
    y1 = hopped(y1, 1)
    (attended,) = call(
        attention_kernel, [((rows, QH * HD), BF16)], [SMEM] * 2 + [VMEM] * 10
    )(
        page_map, cached_lengths, queries, pages,
        fresh_keyvals, kv1, kv2, kv3, small, small1, small2, small3,
    )
    (result,) = call(
        final_kernel,
        [((rows, QH * HD + MI), BF16)],
        [VMEM] * 7,
        [pltpu.VMEM((rows, MI), F32)],
    )(attended, gate_input, norm_gain.reshape(1, MI), y0, y1, y2, y3)
    return result


def solution(mesh):
    in_specs = (
        P(("dp", "head"), None),
        P(("dp", "head"), None),
        P(("dp", "head"), None),
        P(("dp", "head"), None),
        P(("dp", "head"), None),
        P(("dp", "head"), None),
        P(("dp", "head")),
        P("dp", "head", None),
        P("dp", None),
        P("dp"),
        P("dp", "head", None, None),
        P("head"),
        P("head"),
        P("head"),
        P(),
    )
    out_specs = P(("dp", "head"), None)
    return jax.shard_map(local, mesh=mesh, in_specs=in_specs, out_specs=out_specs, check_vma=False)
```

time: 103 us -> 32 us (0.31)
  waiting for transfers between devices: 28.6 us -> 6.21 us
  blocking collectives: 21 us -> 0 us
  starting transfers between devices: 31.9 us -> 15.1 us
  other arithmetic: 5.66 us -> 0 us
  Pallas kernels: 0 us -> 4.78 us
  matrix products: 4.46 us -> 0 us
  local copies, waits for them, and re-layouts: 8.61 us -> 4.78 us
    all_to_all x8 -> x1, waiting for transfers between devices: 27.8 us -> 0.01 us  [local(): lax.all_to_all(copies, ('dp', 'head'), split_axis=0, concat_axis=0, tiled...]
    all_to_all x8 -> x1, starting transfers between devices: 30.9 us -> 4.92 us  [local(): lax.all_to_all(copies, ('dp', 'head'), split_axis=0, concat_axis=0, tiled...]
    ppermute x2 -> x12, starting transfers between devices: 1 us -> 10.2 us  [hopped(): return lax.ppermute(block, 'head', [(i, i ^ hop) for i in range(4)])]
    psum x1 -> x0, blocking collectives: 7.36 us -> none  [local(): square_sums = lax.psum(jnp.sum(gated * gated, axis=1), 'head')]
    unnamed x1 -> x0, blocking collectives: 7.11 us -> none
    all_gather x1 -> x0, blocking collectives: 6.49 us -> none  [local(): lax.all_gather(state_maps, 'head', axis=0, tiled=True)]
    ppermute x2 -> x12, waiting for transfers between devices: 0.78 us -> 6.2 us  [hopped(): return lax.ppermute(block, 'head', [(i, i ^ hop) for i in range(4)])]
    pallas_call x0 -> x4, Pallas kernels: none -> 4.78 us  [the longest x1 1.99 us: local(): call(scan_kernel, [((rows, width), BF16)] * 4, [SMEM] * 3 + [VMEM] * 9, [...]
  transfers between devices with their start and end apart: 10 -> 13, of which waited for: 7 -> 6; matrix products, arithmetic and copies ran while one was open for 16% -> 4% of each run, Pallas kernels for 0% -> 11%
where the time goes in v1:
time: 32 us; the launch traced here: 31.6 us
  starting transfers between devices  15.1 us (47%)
  waiting for transfers between devices  6.21 us (19%)
  local copies, waits for them, and re-layouts  4.78 us (15%)
  Pallas kernels  4.78 us (15%)
  between operations  0.75 us (2%)
    ppermute x12, starting transfers between devices, hopped(): return lax.ppermute(block, 'head', [(i, i ^ hop) for i in range(4)])  10.2 us
    ppermute x12, waiting for transfers between devices, hopped(): return lax.ppermute(block, 'head', [(i, i ^ hop) for i in range(4)])  6.2 us
    all_to_all x1, starting transfers between devices, local(): lax.all_to_all(copies, ('dp', 'head'), split_axis=0, concat_axis=0, tiled...  4.92 us
    unnamed x27, local copies, waits for them, and re-layouts  3.36 us
    pallas_call x1, Pallas kernels, local(): call(scan_kernel, [((rows, width), BF16)] * 4, [SMEM] * 3 + [VMEM] * 9, [...  1.99 us
    pallas_call x1, Pallas kernels, local(): call(attention_kernel, [((rows, QH * HD), BF16)], [SMEM] * 2 + [VMEM] * 10)  1.46 us
    broadcast_in_dim x1, local copies, waits for them, and re-layouts, local(): jnp.broadcast_to(cache_pool[:, None], (slots, 4, half, 2 * HD))  1.42 us
    pallas_call x1, Pallas kernels, local(): call(final_kernel, [((rows, QH * HD + MI), BF16)], [VMEM] * 7, [pltpu.VME...  1.25 us
  transfers between devices with their start and end apart: 13, of which 6 were waited for; matrix products, arithmetic and copies ran while one was open for 4% of the time, Pallas kernels for 11%

profile of v1, /device:TPU:0, one launch (start us, length us, event | category | flops | bytes accessed | tf_op | source)
XLA Modules:
  0.0 31.6 jit_solution(478954235491100449)
XLA Ops:
  0.0 0.8 %copy.16.logit_ref = bf16[64,24]{1,0:T(8,128)(2,1)S(1)} copy(bf16[64,24]{0,1:T(8,128)(2,1)} %param.20) | data formatting | bytes 6144 | tf_op args[5]
  0.8 0.7 %copy-done.9 = s32[64]{0:T(128)S(1)} copy-done((s32[64]{0:T(128)S(1)}, s32[64]{0:T(128)}, u32[]{:S(2)}) %copy-start.9) | copy-done | bytes 280
  1.4 1.0 %copy-done = bf16[64,3072]{1,0:T(8,128)(2,1)S(1)} copy-done((bf16[64,3072]{1,0:T(8,128)(2,1)S(1)}, bf16[64,3072]{1,0:T(8,128)(2,1)}, u32[]{:S(2)}) %copy-start) | copy-done | bytes 393240
  2.4 0.8 %copy-done.6 = bf16[64,512]{1,0:T(8,128)(2,1)S(1)} copy-done((bf16[64,512]{1,0:T(8,128)(2,1)S(1)}, bf16[64,512]{1,0:T(8,128)(2,1)}, u32[]{:S(2)}) %copy-start.6) | copy-done | bytes 65560
  3.3 0.1 shard_map.145
  3.4 3.0 %collective-permute-start.4 = (bf16[64,640]{1,0:T(8,128)(2,1)S(1)}, bf16[64,640]{1,0:T(8,128)(2,1)S(1)}, u32[]{:S(2)}, u32[]{:S(2)}) collective-permute-start(bf16[64,640]{1,0:T(8,128)(2,1)S(1)} %get-tuple-element.13.small0), channel_id=1, source_target_pairs={{0,2},{1,3},{2,0},{3,1},{4,6},{5,7},{6,4},{7,5},{8,10},{9,11},{10,... | collective-permute-start | bytes 245768 | tf_op jit(solution)/shard_map/ppermute | solution.py:210
  6.4 1.4 %broadcast_in_dim.2 = bf16[8,4,8,256]{3,2,1,0:T(8,128)(2,1)} broadcast(bf16[8,8,256]{2,1,0:T(8,128)(2,1)} %param.22), dimensions={0,2,3} | broadcast | bytes 163840 | tf_op jit(solution)/shard_map/broadcast_in_dim | solution.py:249
  7.8 4.9 %all-to-all-start = ((bf16[32,8,256]{2,1,0:T(8,128)(2,1)}), bf16[32,8,256]{2,1,0:T(8,128)(2,1)S(1)}, u32[]{:S(2)}, u32[]{:S(2)}) async-start(bf16[32,8,256]{2,1,0:T(8,128)(2,1)} %bitcast), calls=%async_computation | async-start | bytes 262144 | tf_op jit(solution)/shard_map/all_to_all | solution.py:250
  12.7 0.3 collective-permute-start.3
  13.0 0.3 collective-permute-start.6
  13.3 1.8 %collective-permute-start.7 = (bf16[64,768]{1,0:T(8,128)(2,1)S(1)}, bf16[64,768]{1,0:T(8,128)(2,1)S(1)}, u32[]{:S(2)}, u32[]{:S(2)}) collective-permute-start(bf16[64,768]{1,0:T(8,128)(2,1)S(1)} %get-tuple-element.15), channel_id=1, source_target_pairs={{0,2},{1,3},{2,0},{3,1},{4,6},{5,7},{6,4},{7,5},{8,10},{9,11},{10,... | collective-permute-start | bytes 294920 | tf_op jit(solution)/shard_map/ppermute | solution.py:210
  15.1 0.0 collective-permute-start.8
  15.1 0.0 collective-permute-done.4.small2
  15.1 0.4 %collective-permute-start.5 = (bf16[64,640]{1,0:T(8,128)(2,1)S(1)}, bf16[64,640]{1,0:T(8,128)(2,1)S(1)}, u32[]{:S(2)}, u32[]{:S(2)}) collective-permute-start(bf16[64,640]{1,0:T(8,128)(2,1)S(1)} %collective-permute-done.4.small2), channel_id=1, source_target_pairs={{0,1},{1,0},{2,3},{3,2},{4,5},{5,4},{6,7},{7,6},{8,9},{9,8},{10,11... | collective-permute-start | bytes 245768 | tf_op jit(solution)/shard_map/ppermute | solution.py:210
  15.5 0.0 collective-permute-done.3.small1
  15.5 1.8 %collective-permute-start.1 = (bf16[64,512]{1,0:T(8,128)(2,1)S(1)}, bf16[64,512]{1,0:T(8,128)(2,1)S(1)}, u32[]{:S(2)}, u32[]{:S(2)}) collective-permute-start(bf16[64,512]{1,0:T(8,128)(2,1)S(1)} %copy-done.5), channel_id=1, source_target_pairs={{0,2},{1,3},{2,0},{3,1},{4,6},{5,7},{6,4},{7,5},{8,10},{9,11},{10,... | collective-permute-start | bytes 196616 | tf_op jit(solution)/shard_map/ppermute | solution.py:210
  17.2 2.5 %collective-permute-done.7.x2 = bf16[64,768]{1,0:T(8,128)(2,1)S(1)} collective-permute-done((bf16[64,768]{1,0:T(8,128)(2,1)S(1)}, bf16[64,768]{1,0:T(8,128)(2,1)S(1)}, u32[]{:S(2)}, u32[]{:S(2)}) %collective-permute-start.7) | collective-permute-done | bytes 98336 | tf_op jit(solution)/shard_map/ppermute | solution.py:210
  19.7 1.5 %collective-permute-done.8.x3 = bf16[64,768]{1,0:T(8,128)(2,1)S(1)} collective-permute-done((bf16[64,768]{1,0:T(8,128)(2,1)S(1)}, bf16[64,768]{1,0:T(8,128)(2,1)S(1)}, u32[]{:S(2)}, u32[]{:S(2)}) %collective-permute-start.8) | collective-permute-done | bytes 98336 | tf_op jit(solution)/shard_map/ppermute | solution.py:210
  21.3 2.0 %shard_map.147 = (bf16[64,768]{1,0:T(8,128)(2,1)S(1)}, bf16[64,768]{1,0:T(8,128)(2,1)S(1)}, bf16[64,768]{1,0:T(8,128)(2,1)S(1)}, bf16[64,768]{1,0:T(8,128)(2,1)S(1)}) custom-call(f32[6]{0:T(128)S(1)} %copy-done.10, f32[6]{0:T(128)S(1)} %copy-done.11, f32[6]{0:T(128)S(1)} %copy-done.12, bf16[64,640]{1,0:T(8,128)(2,1)S(1)} %get-tuple-element.13.small0, ...), custom_call_target="tpu_custom_call" | custom-call | tf_op jit(solution)/shard_map/pallas_call | solution.py:253
  23.3 0.6 %collective-permute-start.9 = (bf16[64,768]{1,0:T(8,128)(2,1)S(1)}, bf16[64,768]{1,0:T(8,128)(2,1)S(1)}, u32[]{:S(2)}, u32[]{:S(2)}) collective-permute-start(bf16[64,768]{1,0:T(8,128)(2,1)S(1)} %get-tuple-element.18), channel_id=1, source_target_pairs={{0,1},{1,0},{2,3},{3,2},{4,5},{5,4},{6,7},{7,6},{8,9},{9,8},{10,11... | collective-permute-start | bytes 294920 | tf_op jit(solution)/shard_map/ppermute | solution.py:210
  23.8 1.5 %collective-permute-start.10 = (bf16[64,768]{1,0:T(8,128)(2,1)S(1)}, bf16[64,768]{1,0:T(8,128)(2,1)S(1)}, u32[]{:S(2)}, u32[]{:S(2)}) collective-permute-start(bf16[64,768]{1,0:T(8,128)(2,1)S(1)} %get-tuple-element.19), channel_id=1, source_target_pairs={{0,2},{1,3},{2,0},{3,1},{4,6},{5,7},{6,4},{7,5},{8,10},{9,11},{10,... | collective-permute-start | bytes 294920 | tf_op jit(solution)/shard_map/ppermute | solution.py:210
  25.3 0.0 collective-permute-start.11
  25.3 0.7 %collective-permute-start = (bf16[64,512]{1,0:T(8,128)(2,1)S(1)}, bf16[64,512]{1,0:T(8,128)(2,1)S(1)}, u32[]{:S(2)}, u32[]{:S(2)}) collective-permute-start(bf16[64,512]{1,0:T(8,128)(2,1)S(1)} %copy-done.5), channel_id=1, source_target_pairs={{0,1},{1,0},{2,3},{3,2},{4,5},{5,4},{6,7},{7,6},{8,9},{9,8},{10,11... | collective-permute-start | bytes 196616 | tf_op jit(solution)/shard_map/ppermute | solution.py:210
  26.0 0.0 collective-permute-start.2
  26.6 0.0 copy-start.8
  26.6 0.2 collective-permute-done.kv1
  26.9 0.4 %collective-permute-done.2.kv3 = bf16[64,512]{1,0:T(8,128)(2,1)S(1)} collective-permute-done((bf16[64,512]{1,0:T(8,128)(2,1)S(1)}, bf16[64,512]{1,0:T(8,128)(2,1)S(1)}, u32[]{:S(2)}, u32[]{:S(2)}) %collective-permute-start.2) | collective-permute-done | bytes 65568 | tf_op jit(solution)/shard_map/ppermute | solution.py:210
  27.2 0.1 copy-done.8
  27.3 1.5 %shard_map.146.attended_ref = bf16[64,1536]{1,0:T(8,128)(2,1)S(1)} custom-call(s32[1,8]{1,0:T(1,128)S(1)} %copy-done.8, s32[1]{0:T(128)S(6)} %copy.17.length_ref, bf16[64,1536]{1,0:T(8,128)(2,1)S(1)} %copy-done.4, bf16[256,256]{1,0:T(8,128)(2,1)S(1)} %bitcast.4, bf16[64,512]{1,0:T(8,128)(2,1)S(1)} %copy-done.5, ...), custom_call_target="tpu_custom_call" | custom-call | tf_op jit(solution)/shard_map/pallas_call | solution.py:265
  28.8 0.2 collective-permute-done.10.y2
  28.9 1.4 %collective-permute-done.11.y3 = bf16[64,768]{1,0:T(8,128)(2,1)S(1)} collective-permute-done((bf16[64,768]{1,0:T(8,128)(2,1)S(1)}, bf16[64,768]{1,0:T(8,128)(2,1)S(1)}, u32[]{:S(2)}, u32[]{:S(2)}) %collective-permute-start.11) | collective-permute-done | bytes 98336 | tf_op jit(solution)/shard_map/ppermute | solution.py:210
  30.4 1.3 %shard_map.148 = bf16[64,4608]{1,0:T(8,128)(2,1)} custom-call(bf16[64,1536]{1,0:T(8,128)(2,1)S(1)} %shard_map.146.attended_ref, bf16[64,3072]{1,0:T(8,128)(2,1)S(1)} %copy-done.3, f32[1,3072]{1,0:T(1,128)S(1)} %bitcast.5, bf16[64,768]{1,0:T(8,128)(2,1)S(1)} %get-tuple-element.17.y0, bf16[64,768]{1,0:T(8,128)(2,1)S(1)} %collective-permute-done.9.y1, ...), custom_call_target="tpu_custom_call" | custom-call | tf_op jit(solution)/shard_map/pallas_call | solution.py:271
  (26 shorter events, 0.1 us)
Async XLA Ops:
  0.8 0.7 %copy-start.9 = (s32[64]{0:T(128)S(1)}, s32[64]{0:T(128)}, u32[]{:S(2)}) copy-start(s32[64]{0:T(128)} %param.21) | copy-start | bytes 772
  1.4 1.0 %copy-start = (bf16[64,3072]{1,0:T(8,128)(2,1)S(1)}, bf16[64,3072]{1,0:T(8,128)(2,1)}, u32[]{:S(2)}) copy-start(bf16[64,3072]{1,0:T(8,128)(2,1)} %x_ref.3) | copy-start | bytes 1179652
  2.4 0.8 %copy-start.6 = (bf16[64,512]{1,0:T(8,128)(2,1)S(1)}, bf16[64,512]{1,0:T(8,128)(2,1)}, u32[]{:S(2)}) copy-start(bf16[64,512]{1,0:T(8,128)(2,1)} %maps_ref.1) | copy-start | bytes 196612
  3.3 18.0 %copy-start.1 = (bf16[64,3072]{1,0:T(8,128)(2,1)S(1)}, bf16[64,3072]{1,0:T(8,128)(2,1)}, u32[]{:S(2)}) copy-start(bf16[64,3072]{1,0:T(8,128)(2,1)} %x_ref.3) | copy-start | bytes 1179652
  3.3 18.0 %copy-start.2 = (bf16[1,6,128,256]{3,2,1,0:T(8,128)(2,1)S(1)}, bf16[1,6,128,256]{3,2,1,0:T(8,128)(2,1)}, u32[]{:S(2)}) copy-start(bf16[1,6,128,256]{3,2,1,0:T(8,128)(2,1)} %prior_ref.1) | copy-start | bytes 1179652
  3.4 11.7 %collective-permute-start.4 = (bf16[64,640]{1,0:T(8,128)(2,1)S(1)}, bf16[64,640]{1,0:T(8,128)(2,1)S(1)}, u32[]{:S(2)}, u32[]{:S(2)}) collective-permute-start(bf16[64,640]{1,0:T(8,128)(2,1)S(1)} %get-tuple-element.13.small0), channel_id=1, source_target_pairs={{0,2},{1,3},{2,0},{3,1},{4,6},{5,7},{6,4},{7,5},{8,10},{9,11},{10,... | collective-permute-start | bytes 245768 | tf_op jit(solution)/shard_map/ppermute | solution.py:210
  7.8 7.7 %copy-start.5 = (bf16[64,512]{1,0:T(8,128)(2,1)S(1)}, bf16[64,512]{1,0:T(8,128)(2,1)}, u32[]{:S(2)}) copy-start(bf16[64,512]{1,0:T(8,128)(2,1)} %kv0.1) | copy-start | bytes 196612
  7.8 19.4 %all-to-all-start = ((bf16[32,8,256]{2,1,0:T(8,128)(2,1)}), bf16[32,8,256]{2,1,0:T(8,128)(2,1)S(1)}, u32[]{:S(2)}, u32[]{:S(2)}) async-start(bf16[32,8,256]{2,1,0:T(8,128)(2,1)} %bitcast), calls=%async_computation | async-start | bytes 262144 | tf_op jit(solution)/shard_map/all_to_all | solution.py:250
  12.7 2.7 %collective-permute-start.3 = (bf16[64,640]{1,0:T(8,128)(2,1)S(1)}, bf16[64,640]{1,0:T(8,128)(2,1)S(1)}, u32[]{:S(2)}, u32[]{:S(2)}) collective-permute-start(bf16[64,640]{1,0:T(8,128)(2,1)S(1)} %get-tuple-element.13.small0), channel_id=1, source_target_pairs={{0,1},{1,0},{2,3},{3,2},{4,5},{5,4},{6,7},{7,6},{8,9},{9,8},{10,11... | collective-permute-start | bytes 245768 | tf_op jit(solution)/shard_map/ppermute | solution.py:210
  13.0 4.2 %collective-permute-start.6 = (bf16[64,768]{1,0:T(8,128)(2,1)S(1)}, bf16[64,768]{1,0:T(8,128)(2,1)S(1)}, u32[]{:S(2)}, u32[]{:S(2)}) collective-permute-start(bf16[64,768]{1,0:T(8,128)(2,1)S(1)} %get-tuple-element.14), channel_id=1, source_target_pairs={{0,1},{1,0},{2,3},{3,2},{4,5},{5,4},{6,7},{7,6},{8,9},{9,8},{10,11... | collective-permute-start | bytes 294920 | tf_op jit(solution)/shard_map/ppermute | solution.py:210
  13.3 7.9 %copy-start.10 = (f32[6]{0:T(128)S(1)}, f32[6]{0:T(128)}, u32[]{:S(2)}) copy-start(f32[6]{0:T(128)} %log_rate_ref.1) | copy-start | bytes 76
  13.3 7.9 %copy-start.11 = (f32[6]{0:T(128)S(1)}, f32[6]{0:T(128)}, u32[]{:S(2)}) copy-start(f32[6]{0:T(128)} %bias_ref.1) | copy-start | bytes 76
  13.3 8.0 %copy-start.12 = (f32[6]{0:T(128)S(1)}, f32[6]{0:T(128)}, u32[]{:S(2)}) copy-start(f32[6]{0:T(128)} %skip_ref.1) | copy-start | bytes 76
  13.3 6.4 %collective-permute-start.7 = (bf16[64,768]{1,0:T(8,128)(2,1)S(1)}, bf16[64,768]{1,0:T(8,128)(2,1)S(1)}, u32[]{:S(2)}, u32[]{:S(2)}) collective-permute-start(bf16[64,768]{1,0:T(8,128)(2,1)S(1)} %get-tuple-element.15), channel_id=1, source_target_pairs={{0,2},{1,3},{2,0},{3,1},{4,6},{5,7},{6,4},{7,5},{8,10},{9,11},{10,... | collective-permute-start | bytes 294920 | tf_op jit(solution)/shard_map/ppermute | solution.py:210
  15.1 12.2 %copy-start.4 = (bf16[64,1536]{1,0:T(8,128)(2,1)S(1)}, bf16[64,1536]{1,0:T(8,128)(2,1)}, u32[]{:S(2)}) copy-start(bf16[64,1536]{1,0:T(8,128)(2,1)} %query_ref.1) | copy-start | bytes 589828
  15.1 6.2 %collective-permute-start.8 = (bf16[64,768]{1,0:T(8,128)(2,1)S(1)}, bf16[64,768]{1,0:T(8,128)(2,1)S(1)}, u32[]{:S(2)}, u32[]{:S(2)}) collective-permute-start(bf16[64,768]{1,0:T(8,128)(2,1)S(1)} %get-tuple-element.16), channel_id=1, source_target_pairs={{0,3},{1,2},{2,1},{3,0},{4,7},{5,6},{6,5},{7,4},{8,11},{9,10},{10,... | collective-permute-start | bytes 294920 | tf_op jit(solution)/shard_map/ppermute | solution.py:210
  15.1 6.1 %collective-permute-start.5 = (bf16[64,640]{1,0:T(8,128)(2,1)S(1)}, bf16[64,640]{1,0:T(8,128)(2,1)S(1)}, u32[]{:S(2)}, u32[]{:S(2)}) collective-permute-start(bf16[64,640]{1,0:T(8,128)(2,1)S(1)} %collective-permute-done.4.small2), channel_id=1, source_target_pairs={{0,1},{1,0},{2,3},{3,2},{4,5},{5,4},{6,7},{7,6},{8,9},{9,8},{10,11... | collective-permute-start | bytes 245768 | tf_op jit(solution)/shard_map/ppermute | solution.py:210
  15.5 10.5 %collective-permute-start.1 = (bf16[64,512]{1,0:T(8,128)(2,1)S(1)}, bf16[64,512]{1,0:T(8,128)(2,1)S(1)}, u32[]{:S(2)}, u32[]{:S(2)}) collective-permute-start(bf16[64,512]{1,0:T(8,128)(2,1)S(1)} %copy-done.5), channel_id=1, source_target_pairs={{0,2},{1,3},{2,0},{3,1},{4,6},{5,7},{6,4},{7,5},{8,10},{9,11},{10,... | collective-permute-start | bytes 196616 | tf_op jit(solution)/shard_map/ppermute | solution.py:210
  23.3 5.5 %collective-permute-start.9 = (bf16[64,768]{1,0:T(8,128)(2,1)S(1)}, bf16[64,768]{1,0:T(8,128)(2,1)S(1)}, u32[]{:S(2)}, u32[]{:S(2)}) collective-permute-start(bf16[64,768]{1,0:T(8,128)(2,1)S(1)} %get-tuple-element.18), channel_id=1, source_target_pairs={{0,1},{1,0},{2,3},{3,2},{4,5},{5,4},{6,7},{7,6},{8,9},{9,8},{10,11... | collective-permute-start | bytes 294920 | tf_op jit(solution)/shard_map/ppermute | solution.py:210
  23.8 5.1 %collective-permute-start.10 = (bf16[64,768]{1,0:T(8,128)(2,1)S(1)}, bf16[64,768]{1,0:T(8,128)(2,1)S(1)}, u32[]{:S(2)}, u32[]{:S(2)}) collective-permute-start(bf16[64,768]{1,0:T(8,128)(2,1)S(1)} %get-tuple-element.19), channel_id=1, source_target_pairs={{0,2},{1,3},{2,0},{3,1},{4,6},{5,7},{6,4},{7,5},{8,10},{9,11},{10,... | collective-permute-start | bytes 294920 | tf_op jit(solution)/shard_map/ppermute | solution.py:210
  25.3 5.1 %collective-permute-start.11 = (bf16[64,768]{1,0:T(8,128)(2,1)S(1)}, bf16[64,768]{1,0:T(8,128)(2,1)S(1)}, u32[]{:S(2)}, u32[]{:S(2)}) collective-permute-start(bf16[64,768]{1,0:T(8,128)(2,1)S(1)} %get-tuple-element.20), channel_id=1, source_target_pairs={{0,3},{1,2},{2,1},{3,0},{4,7},{5,6},{6,5},{7,4},{8,11},{9,10},{10,... | collective-permute-start | bytes 294920 | tf_op jit(solution)/shard_map/ppermute | solution.py:210
  25.3 1.6 %collective-permute-start = (bf16[64,512]{1,0:T(8,128)(2,1)S(1)}, bf16[64,512]{1,0:T(8,128)(2,1)S(1)}, u32[]{:S(2)}, u32[]{:S(2)}) collective-permute-start(bf16[64,512]{1,0:T(8,128)(2,1)S(1)} %copy-done.5), channel_id=1, source_target_pairs={{0,1},{1,0},{2,3},{3,2},{4,5},{5,4},{6,7},{7,6},{8,9},{9,8},{10,11... | collective-permute-start | bytes 196616 | tf_op jit(solution)/shard_map/ppermute | solution.py:210
  26.0 1.3 %collective-permute-start.2 = (bf16[64,512]{1,0:T(8,128)(2,1)S(1)}, bf16[64,512]{1,0:T(8,128)(2,1)S(1)}, u32[]{:S(2)}, u32[]{:S(2)}) collective-permute-start(bf16[64,512]{1,0:T(8,128)(2,1)S(1)} %collective-permute-done.1.kv2), channel_id=1, source_target_pairs={{0,1},{1,0},{2,3},{3,2},{4,5},{5,4},{6,7},{7,6},{8,9},{9,8},{10,11... | collective-permute-start | bytes 196616 | tf_op jit(solution)/shard_map/ppermute | solution.py:210
  26.6 0.7 %copy-start.8 = (s32[1,8]{1,0:T(1,128)S(1)}, s32[1,8]{1,0:T(1,128)}, u32[]{:S(2)}) copy-start(s32[1,8]{1,0:T(1,128)} %page_map_ref.1) | copy-start | bytes 100
  27.3 3.1 %copy-start.3 = (bf16[64,3072]{1,0:T(8,128)(2,1)S(1)}, bf16[64,3072]{1,0:T(8,128)(2,1)}, u32[]{:S(2)}) copy-start(bf16[64,3072]{1,0:T(8,128)(2,1)} %gate_ref.1) | copy-start | bytes 1179652
  27.3 3.1 %copy-start.7 = (f32[3072]{0:T(1024)S(1)}, f32[3072]{0:T(1024)}, u32[]{:S(2)}) copy-start(f32[3072]{0:T(1024)} %param.29) | copy-start | bytes 36868

commit v2 on v1

v2 whole, which is shorter than its diff:
```python
import math

import jax
import jax.numpy as jnp
from jax import lax
from jax.experimental import pallas as pl
from jax.experimental.pallas import tpu as pltpu
from jax.sharding import PartitionSpec as P

HD = 128
QH = 12
KVH = 2
GROUP = QH // KVH
STATE = 256
MI = 3072
PAGE = 16
LANES = 128
EPSILON = 1e-05
BF16 = jnp.bfloat16
F32 = jnp.float32
HIGHEST = lax.Precision.HIGHEST
VMEM = pl.BlockSpec(memory_space=pltpu.VMEM)
SMEM = pl.BlockSpec(memory_space=pltpu.SMEM)
ANY = pl.BlockSpec(memory_space=pl.ANY)
MAPS = 2 * STATE
NOTES = slice(MAPS, MAPS + LANES)
TOLD = MAPS + LANES
KEYVALS = 2 * KVH * HD
MASK_LANE = 24
PARAM_LANE = 32
ALL_HEADS = 24


def call(kernel, outs, specs, scratch=(), limit=24):
    return pl.pallas_call(
        kernel,
        out_shape=[jax.ShapeDtypeStruct(shape, dtype) for shape, dtype in outs],
        in_specs=specs,
        out_specs=[VMEM] * len(outs),
        scratch_shapes=list(scratch),
        compiler_params=pltpu.CompilerParams(vmem_limit_bytes=limit << 20),
    )


def columns(ref, owner, width):
    return ref[:, pl.ds(pl.multiple_of(owner * width, LANES), width)]


def iota(shape, dim):
    return lax.broadcasted_iota(jnp.int32, shape, dim)


def rolled(array, first, axis):
    size = array.shape[axis]
    return pltpu.roll(array, lax.rem(size - first, size), axis)


def nt_dot(a, b, precision=None):
    return lax.dot_general(
        a, b, (((1,), (1,)), ((), ())), preferred_element_type=F32, precision=precision
    )


def pack_kernel(
    log_rate_ref, bias_ref, skip_ref, x_ref, maps_ref, logit_ref, mask_ref, keyval_ref, told_ref, far_ref,
):
    me = lax.axis_index("head")
    rows, width = x_ref.shape[0], x_ref.shape[1] // 4
    far_ref[:, :width] = columns(x_ref, me ^ 2, width)
    far_ref[:, width : 2 * width] = columns(x_ref, me ^ 3, width)
    far_ref[:, 2 * width :] = keyval_ref[...]
    told_ref[:, :MAPS] = maps_ref[...]
    heads, head_count = logit_ref.shape[0], log_rate_ref.shape[0]
    pick = (iota((heads, LANES), 0) == iota((heads, LANES), 1)).astype(F32).astype(BF16)
    notes = lax.dot_general(logit_ref[...], pick, (((0,), (0,)), ((), ())), preferred_element_type=F32)
    diagonal = iota((rows, rows), 0) == iota((rows, rows), 1)
    real = jnp.broadcast_to(mask_ref[...], (rows, rows)) > 0
    real = jnp.sum(jnp.where(diagonal & real, 1.0, 0.0), axis=1, keepdims=True)
    lane, row = iota((1, LANES), 1), iota((rows, 1), 0)
    params = jnp.zeros((rows, LANES), F32)
    for kind, ref in enumerate((log_rate_ref, bias_ref, skip_ref)):
        value = jnp.zeros((1, LANES), F32)
        for head in range(head_count):
            value = jnp.where(lane == PARAM_LANE + me * head_count + head, ref[head], value)
        high = value.astype(BF16).astype(F32)
        middle = (value - high).astype(BF16).astype(F32)
        for part, piece in enumerate((high, middle, value - high - middle)):
            params = jnp.where(row == 3 * kind + part, piece, params)
    in_params = (lane >= PARAM_LANE) & (lane < PARAM_LANE + ALL_HEADS)
    notes = jnp.where(lane < heads, notes, jnp.where(in_params, params, real))
    told_ref[:, NOTES] = notes.astype(BF16)


def order_kernel(pool_ref, even_ref, odd_ref):
    request = lax.axis_index("dp")
    half_slots = even_ref.shape[0]

    def place(at, carry):
        distance, rest, bit = 0, at, half_slots
        while bit > 1:
            distance, rest, bit = distance + (rest % 2) * bit, rest // 2, bit // 2
        even_ref[at] = pool_ref[request ^ distance]
        odd_ref[at] = pool_ref[request ^ distance ^ 1]
        return carry

    lax.fori_loop(0, half_slots, place, 0, unroll=half_slots <= 8)


def copy_kernel(from_ref, to_ref):
    to_ref[...] = from_ref[...]


def token_at(index, rows, me):
    return (me ^ (index // rows)) * rows + index % rows


def head_sums(tolds, me):
    rows = tolds[0].shape[0]
    span = 4 * rows
    notes = jnp.concatenate([ref[:, NOTES] for ref in tolds], axis=0)
    params = sum(ref[0:16, NOTES].astype(F32) for ref in tolds).astype(BF16)
    head, lane = iota((32, LANES), 0), iota((32, LANES), 1)
    by_row = jnp.where(head == lane, 1.0, 0.0).astype(BF16)
    by_row_params = jnp.where(head + PARAM_LANE == lane, 1.0, 0.0).astype(BF16)
    source, target = iota((LANES, LANES), 0), iota((LANES, LANES), 1)
    by_lane_params = jnp.where((source == target + PARAM_LANE) & (target < ALL_HEADS), 1.0, 0.0).astype(BF16)
    row_params = nt_dot(by_row_params, params)
    lane_params = jnp.dot(params, by_lane_params, preferred_element_type=F32)

    def row_param(kind):
        return sum(row_params[:, 3 * kind + part : 3 * kind + part + 1] for part in range(3))

    def lane_param(kind):
        return sum(lane_params[3 * kind + part : 3 * kind + part + 1, :] for part in range(3))

    row_logits = nt_dot(by_row, notes)
    lane_logits = notes.astype(F32)
    row_mask = row_logits[MASK_LANE : MASK_LANE + 1, :]
    lane_mask = lane_logits[:, MASK_LANE : MASK_LANE + 1]
    row_steps = jnp.log(1.0 + jnp.exp(row_logits + row_param(1))) * row_mask
    lane_steps = jnp.log(1.0 + jnp.exp(lane_logits + lane_param(1))) * lane_mask
    token = token_at(iota((span, span), 0), rows, me)
    source = token_at(iota((span, span), 1), rows, me)
    upto = jnp.where(source <= token, 1.0, 0.0)
    row_sum = nt_dot(-jnp.exp(row_param(0)) * row_steps, upto, HIGHEST)
    lane_sum = jnp.dot(upto, -jnp.exp(lane_param(0)) * lane_steps, preferred_element_type=F32, precision=HIGHEST)
    return row_sum - jnp.log(row_steps), lane_sum, lane_param(2), lane_mask


def remote_kernel(
    told0, told1, told2, told3, x0_ref, x1_ref, prior_ref,
    y_ref, shift_ref, total_ref, skip_ref,
):
    me = lax.axis_index("head")
    rows, width = told0.shape[0], y_ref.shape[1]
    near, head_count = 2 * rows, width // HD
    shift, total, skip, mask = head_sums((told0, told1, told2, told3), me)
    shift_ref[...] = shift
    total_ref[...] = total
    skip_ref[...] = jnp.broadcast_to(skip, skip_ref.shape)
    own_shift = rolled(shift, me * head_count, 0)
    own_total = rolled(total, me * head_count, 1)
    in_map = jnp.concatenate([told0[:, :STATE], told1[:, :STATE]], axis=0)
    out_map = jnp.concatenate([told2[:, STATE:MAPS], told3[:, STATE:MAPS]], axis=0)
    products = nt_dot(out_map, in_map)
    from_prior = nt_dot(out_map, prior_ref[0].reshape(width, STATE))
    x = jnp.concatenate([columns(x0_ref, me, width), columns(x1_ref, me, width)], axis=0)
    earlier = jnp.where(jnp.broadcast_to(me, (near, near)) < 2, 0.0, -jnp.inf)
    for head in range(head_count):
        cols = slice(head * HD, (head + 1) * HD)
        sums = own_total[near:, head : head + 1]
        weights = (jnp.exp(sums - own_shift[head : head + 1, :near] + earlier) * products).astype(BF16)
        y = jnp.dot(weights, x[:, cols], preferred_element_type=F32) + from_prior[:, cols] * jnp.exp(sums)
        y_ref[:, cols] = (y * mask[near:]).astype(BF16)


def near_kernel(
    shift_ref, total_ref, skip_ref, told0, told1, told2, told3, x0_ref, x1_ref, far_ref, relayed_ref,
    prior0_ref, prior1_ref, y_ref,
):
    me = lax.axis_index("head")
    rows, width = told0.shape[0], x0_ref.shape[1] // 4
    near, span, head_count = 2 * rows, 4 * rows, width // HD
    in_map = jnp.concatenate([ref[:, :STATE] for ref in (told0, told1, told2, told3)], axis=0)
    out_map = told0[:, STATE:MAPS]
    products = nt_dot(out_map, in_map)
    token = token_at(iota((rows, span), 0), rows, me)
    source = token_at(iota((rows, span), 1), rows, me)
    causal = jnp.where(source <= token, 0.0, -jnp.inf)
    mask = told0[:, MAPS + MASK_LANE : MAPS + MASK_LANE + 1].astype(F32)
    shift, total, skip = shift_ref[...], total_ref[:rows, :], skip_ref[...]
    for hop in range(4):
        block = me ^ hop
        block_shift = rolled(shift, block * head_count, 0)
        block_total = rolled(total, block * head_count, 1)
        block_skip = rolled(skip, block * head_count, 1)[0:1, :]
        own = columns(x0_ref, block, width)
        sources = [own, columns(x1_ref, block, width)]
        reach = near
        if hop < 2:
            reach = span
            place = (hop, 1 - hop)
            sources += [ref[:, at * width : (at + 1) * width] for ref, at in zip((far_ref, relayed_ref), place)]
            from_prior = nt_dot(out_map, (prior0_ref, prior1_ref)[hop][0].reshape(width, STATE))
        sources = jnp.concatenate(sources, axis=0)
        for head in range(head_count):
            cols = slice(head * HD, (head + 1) * HD)
            sums = block_total[:, head : head + 1]
            weights = jnp.exp(sums - block_shift[head : head + 1, :reach] + causal[:, :reach]) * products[:, :reach]
            y = jnp.dot(weights.astype(BF16), sources[:, cols], preferred_element_type=F32)
            y = y + block_skip[:, head : head + 1] * own[:, cols].astype(F32)
            if hop < 2:
                y = y + from_prior[:, cols] * jnp.exp(sums)
            y_ref[:, hop * width + head * HD : hop * width + (head + 1) * HD] = y * mask


def attention_kernel(
    page_map_ref, length_ref, query_ref, pages0, pages1,
    kv0, kv1, far_ref, relayed_ref, told0, told1, told2, told3, out_ref,
):
    me = lax.axis_index("head")
    request = lax.axis_index("dp")
    rows = query_ref.shape[0]
    slots, half = pages0.shape[1], pages0.shape[2]
    part = slots * half
    cached = 2 * part
    inv_scale = 1.0 / math.sqrt(HD)
    lane = iota((1, cached), 1)

    def place(page, base):
        return jnp.where(lane % part // half == (page_map_ref[0, page] ^ request), page * PAGE, base)

    position = lax.fori_loop(0, slots, place, jnp.zeros((1, cached), jnp.int32), unroll=slots <= 8)
    position = position + ((me ^ (lane // part)) % 2) * half + lane % half
    shut = [jnp.broadcast_to(jnp.where(position < length_ref[0], 0.0, -jnp.inf), (rows, cached))]
    ones = jnp.where(iota((8, LANES), 1) == MASK_LANE, 1.0, 0.0).astype(BF16)
    token, source = iota((rows, rows), 0), iota((rows, rows), 1)
    for hop, ref in enumerate((told0, told1, told2, told3)):
        real = nt_dot(ones, ref[:, NOTES])[0:1, :] > 0.5
        limit = token if hop == 0 else jnp.where((me ^ hop) < me, rows, -1)
        shut.append(jnp.where(real & (source <= limit), 0.0, -jnp.inf))
    shut = jnp.concatenate(shut, axis=1)
    shut = jnp.concatenate([shut] * GROUP, axis=0)
    keep = told0[:, MAPS + MASK_LANE : MAPS + MASK_LANE + 1].astype(F32)
    pages = [ref[chip].reshape(part, 2 * HD) for chip in range(2) for ref in (pages0, pages1)]
    for group in range(KVH):
        queries = jnp.concatenate(
            [query_ref[:, (group * GROUP + h) * HD : (group * GROUP + h + 1) * HD] for h in range(GROUP)],
            axis=0,
        )
        here = jnp.broadcast_to(me // 2, (part, 2 * HD)) == group
        old = [jnp.where(here, pages[core], pages[core ^ 2]) for core in range(2)]
        base = 2 * group * HD
        fresh = []
        for ref in (kv0, kv1, far_ref, relayed_ref):
            start = ref.shape[1] - KEYVALS + base
            fresh.append(ref[:, start : start + 2 * HD])
        every = jnp.concatenate(old + fresh, axis=0)
        keys, values = every[:, :HD], every[:, HD:]
        scores = nt_dot(queries, keys) * inv_scale + shut
        top = jnp.max(scores, axis=1, keepdims=True)
        terms = jnp.exp(scores - top)
        total = jnp.sum(terms, axis=1, keepdims=True)
        mixed = jnp.dot(terms.astype(BF16), values, preferred_element_type=F32) / total
        for h in range(GROUP):
            head = group * GROUP + h
            out_ref[:, head * HD : (head + 1) * HD] = (mixed[h * rows : (h + 1) * rows] * keep).astype(BF16)


def final_kernel(attended_ref, gate_ref, gain_ref, y_ref, y2_ref, y3_ref, out_ref, gated):
    me = lax.axis_index("head")
    rows, width = y_ref.shape[0], y2_ref.shape[1]
    heads_width = attended_ref.shape[1]
    out_ref[:, :heads_width] = attended_ref[...]
    squares = jnp.zeros((rows, 1), F32)
    for hop, far in enumerate((None, None, y2_ref[:rows, :], y3_ref[rows:, :])):
        gate = columns(gate_ref, me ^ hop, width).astype(F32)
        part = y_ref[:, hop * width : (hop + 1) * width]
        if far is not None:
            part = part + far.astype(F32)
        part = part.astype(BF16).astype(F32) * (gate / (1.0 + jnp.exp(-gate)))
        gated[:, hop * width : (hop + 1) * width] = part
        squares = squares + jnp.sum(part * part, axis=1, keepdims=True)
    scale = lax.rsqrt(squares / MI + EPSILON)
    for hop in range(4):
        gain = columns(gain_ref, me ^ hop, width)
        part = gated[:, hop * width : (hop + 1) * width] * scale * gain
        start = pl.multiple_of(heads_width + (me ^ hop) * width, LANES)
        out_ref[:, pl.ds(start, width)] = part.astype(BF16)


def behind(block, earlier):
    return block if earlier is None else lax.optimization_barrier((block, earlier))[0]


def hopped(block, hop):
    return lax.ppermute(block, "head", [(i, i ^ hop) for i in range(4)])


def local(
    queries,
    fresh_keyvals,
    ssm_input,
    gate_input,
    state_maps,
    step_logit,
    slot_mask,
    cache_pool,
    page_map,
    cached_lengths,
    prior_state,
    decay_log,
    step_bias,
    skip_gain,
    norm_gain,
):
    rows = ssm_input.shape[0]
    width = MI // 4
    slots, half = cache_pool.shape[0], cache_pool.shape[1]
    pages, sent = call(order_kernel, [((slots // 2, half, 2 * HD), BF16)] * 2, [VMEM])(cache_pool)
    told, far = call(
        pack_kernel,
        [((rows, TOLD), BF16), ((rows, 2 * width + KEYVALS), BF16)],
        [SMEM] * 3 + [VMEM] * 5,
        limit=60,
    )(
        decay_log, step_bias, skip_gain,
        ssm_input, behind(state_maps, sent), step_logit.T, slot_mask.reshape(1, rows), fresh_keyvals,
    )
    prior1 = hopped(prior_state, 1)
    x1 = hopped(ssm_input, 1)
    kv1 = hopped(fresh_keyvals, 1)
    told1 = hopped(told, 1)
    told2 = hopped(told, 2)
    far = hopped(far, 2)
    told3 = hopped(told2, 1)
    (prior0,) = call(copy_kernel, [(prior_state.shape, BF16)], [VMEM])(behind(prior_state, told1))

    parts, bit, came, earlier = [pages], 1, None, None
    while bit < slots:
        if bit > 1:
            keep = parts[0].shape[0] // 2
            sent = jnp.concatenate([part[keep:] for part in parts])
            parts = [part[:keep] for part in parts]
        if bit == 2:
            sent = behind(sent, told1)
        if 2 * bit == slots:
            sent = behind(sent, prior0)
        came, earlier = lax.ppermute(sent, "dp", [(i, i ^ bit) for i in range(slots)]), came
        keep = parts[0].shape[0]
        parts = parts + [came[i * keep : (i + 1) * keep] for i in range(len(parts))]
        bit *= 2
    pages = jnp.concatenate(parts)

    y2, shift, total, skip = call(
        remote_kernel,
        [((2 * rows, width), BF16), ((32, 4 * rows), F32), ((4 * rows, LANES), F32), ((8, LANES), F32)],
        [VMEM] * 7,
    )(told, told1, told2, behind(behind(told3, earlier), prior1), ssm_input, x1, prior0)
    relayed = hopped(behind(far, y2), 1)
    pages = jnp.stack([pages, hopped(pages, 2)])
    pages1 = hopped(pages, 1)
    y2 = hopped(y2, 2)
    y3 = hopped(y2, 1)
    (y,) = call(near_kernel, [((rows, MI), F32)], [VMEM] * 13)(
        shift, total, skip, told, told1, told2, told3, ssm_input, x1, far, relayed, prior0, prior1
    )
    (attended,) = call(attention_kernel, [((rows, QH * HD), BF16)], [SMEM] * 2 + [VMEM] * 11)(
        page_map, cached_lengths, queries, pages, pages1,
        fresh_keyvals, kv1, far, relayed, told, told1, told2, told3,
    )
    (result,) = call(
        final_kernel,
        [((rows, QH * HD + MI), BF16)],
        [VMEM] * 6,
        [pltpu.VMEM((rows, MI), F32)],
    )(attended, gate_input, norm_gain.reshape(1, MI), y, y2, y3)
    return result


def solution(mesh):
    in_specs = (
        P(("dp", "head"), None),
        P(("dp", "head"), None),
        P(("dp", "head"), None),
        P(("dp", "head"), None),
        P(("dp", "head"), None),
        P(("dp", "head"), None),
        P(("dp", "head")),
        P("dp", "head", None),
        P("dp", None),
        P("dp"),
        P("dp", "head", None, None),
        P("head"),
        P("head"),
        P("head"),
        P(),
    )
    out_specs = P(("dp", "head"), None)
    return jax.shard_map(local, mesh=mesh, in_specs=in_specs, out_specs=out_specs, check_vma=False)
```

time: 32 us -> 28.7 us (0.90)
  local copies, waits for them, and re-layouts: 4.78 us -> 1.85 us
  starting transfers between devices: 15.1 us -> 12.5 us
  Pallas kernels: 4.78 us -> 6.82 us
    ppermute x0 -> x3, starting transfers between devices: none -> 7.2 us  [local(): lax.ppermute(sent, 'dp', [(i, i ^ bit) for i in range(slots)])]
    ppermute x12, starting transfers between devices: 10.2 us -> 5.26 us  [hopped(): return lax.ppermute(block, 'head', [(i, i ^ hop) for i in range(4)])]
    all_to_all x1 -> x0, starting transfers between devices: 4.92 us -> none  [local(): lax.all_to_all(copies, ('dp', 'head'), split_axis=0, concat_axis=0, tiled...]
    ppermute x0 -> x3, waiting for transfers between devices: none -> 3.18 us  [local(): lax.ppermute(sent, 'dp', [(i, i ^ bit) for i in range(slots)])]
    ppermute x12, waiting for transfers between devices: 6.2 us -> 3.27 us  [hopped(): return lax.ppermute(block, 'head', [(i, i ^ hop) for i in range(4)])]
    pallas_call x4 -> x7, Pallas kernels: 4.78 us -> 6.82 us  [the longest x1 1.87 us: local(): call(pack_kernel, [((rows, TOLD), BF16), ((rows, 2 * width + KEYVALS), BF...]
    unnamed x27 -> x19, local copies, waits for them, and re-layouts: 3.36 us -> 1.84 us
    broadcast_in_dim x1 -> x0, local copies, waits for them, and re-layouts: 1.42 us -> none  [local(): jnp.broadcast_to(cache_pool[:, None], (slots, 4, half, 2 * HD))]
  transfers between devices with their start and end apart: 13 -> 15, of which waited for: 6 -> 5; matrix products, arithmetic and copies ran while one was open for 4% -> 0% of each run, Pallas kernels for 11% -> 19%
where the time goes in v2:
time: 28.7 us; the launch traced here: 28.4 us
  starting transfers between devices  12.5 us (44%)
  Pallas kernels  6.82 us (24%)
  waiting for transfers between devices  6.46 us (23%)
  local copies, waits for them, and re-layouts  1.85 us (6%)
  between operations  0.82 us (3%)
    ppermute x3, starting transfers between devices, local(): lax.ppermute(sent, 'dp', [(i, i ^ bit) for i in range(slots)])  7.2 us
    ppermute x12, starting transfers between devices, hopped(): return lax.ppermute(block, 'head', [(i, i ^ hop) for i in range(4)])  5.26 us
    ppermute x12, waiting for transfers between devices, hopped(): return lax.ppermute(block, 'head', [(i, i ^ hop) for i in range(4)])  3.27 us
    ppermute x3, waiting for transfers between devices, local(): lax.ppermute(sent, 'dp', [(i, i ^ bit) for i in range(slots)])  3.18 us
    pallas_call x1, Pallas kernels, local(): call(pack_kernel, [((rows, TOLD), BF16), ((rows, 2 * width + KEYVALS), BF...  1.87 us
    unnamed x19, local copies, waits for them, and re-layouts  1.84 us
    pallas_call x1, Pallas kernels, local(): call(attention_kernel, [((rows, QH * HD), BF16)], [SMEM] * 2 + [VMEM] * 11)  1.47 us
    pallas_call x1, Pallas kernels, local(): call(final_kernel, [((rows, QH * HD + MI), BF16)], [VMEM] * 6, [pltpu.VME...  1.3 us
  transfers between devices with their start and end apart: 15, of which 5 were waited for; matrix products, arithmetic and copies ran while one was open for 0% of the time, Pallas kernels for 19%

profile of v2, /device:TPU:0, one launch (start us, length us, event | category | flops | bytes accessed | tf_op | source)
XLA Modules:
  0.0 28.4 jit_solution(13034613188542333879)
XLA Ops:
  0.0 0.8 %copy-done.6 = bf16[8,8,256]{2,1,0:T(8,128)(2,1)S(1)} copy-done((bf16[8,8,256]{2,1,0:T(8,128)(2,1)S(1)}, bf16[8,8,256]{2,1,0:T(8,128)(2,1)}, u32[]{:S(2)}) %copy-start.6) | copy-done | bytes 32792
  0.8 3.0 %collective-permute-start = (bf16[4,8,256]{2,1,0:T(8,128)(2,1)S(1)}, bf16[4,8,256]{2,1,0:T(8,128)(2,1)S(1)}, u32[]{:S(2)}, u32[]{:S(2)}) collective-permute-start(bf16[4,8,256]{2,1,0:T(8,128)(2,1)S(1)} %get-tuple-element.21), channel_id=1, source_target_pairs={{0,4},{4,0},{8,12},{12,8},{16,20},{20,16},{24,28},{28,24},{1,5},{5... | collective-permute-start | bytes 49160 | tf_op jit(solution)/shard_map/ppermute | solution.py:349
  3.8 1.9 %shard_map.146 = (bf16[64,640]{1,0:T(8,128)(2,1)}, bf16[64,2048]{1,0:T(8,128)(2,1)}) custom-call(f32[6]{0:T(128)} %log_rate_ref.1, f32[6]{0:T(128)} %bias_ref.1, f32[6]{0:T(128)} %skip_ref.1, bf16[64,3072]{1,0:T(8,128)(2,1)} %x0_ref.3, bf16[64,512]{1,0:T(8,128)(2,1)} %maps_ref, bf16[24,64]{1,0:T(8,128)(2,1)} %bitcast.8, s32[1,64]{1,0:T(1,128)} %bitcast.9, ...), custom_call_target="tpu_custom_call" | custom-call | tf_op jit(solution)/shard_map/pallas_call | solution.py:321
  5.7 1.5 %collective-permute-start.8 = (bf16[64,640]{1,0:T(8,128)(2,1)}, bf16[64,640]{1,0:T(8,128)(2,1)S(1)}, u32[]{:S(2)}, u32[]{:S(2)}) collective-permute-start(bf16[64,640]{1,0:T(8,128)(2,1)} %get-tuple-element.23.told0), channel_id=1, source_target_pairs={{0,2},{1,3},{2,0},{3,1},{4,6},{5,7},{6,4},{7,5},{8,10},{9,11},{10,... | collective-permute-start | bytes 245768 | tf_op jit(solution)/shard_map/ppermute | solution.py:297
  7.2 0.2 collective-permute-start.11
  7.4 0.3 collective-permute-start.10
  7.7 0.0 collective-permute-done
  7.7 0.5 %collective-permute-start.7 = (bf16[64,2048]{1,0:T(8,128)(2,1)}, bf16[64,2048]{1,0:T(8,128)(2,1)S(1)}, u32[]{:S(2)}, u32[]{:S(2)}) collective-permute-start(bf16[64,2048]{1,0:T(8,128)(2,1)} %get-tuple-element.27), channel_id=1, source_target_pairs={{0,2},{1,3},{2,0},{3,1},{4,6},{5,7},{6,4},{7,5},{8,10},{9,11},{10,... | collective-permute-start | bytes 786440 | tf_op jit(solution)/shard_map/ppermute | solution.py:297
  8.2 0.0 collective-permute-done.1.told1
  8.2 1.6 %collective-permute-start.2 = (bf16[4,8,256]{2,1,0:T(8,128)(2,1)S(1)}, bf16[4,8,256]{2,1,0:T(8,128)(2,1)S(1)}, u32[]{:S(2)}, u32[]{:S(2)}) collective-permute-start(bf16[4,8,256]{2,1,0:T(8,128)(2,1)S(1)} %pad_maximum_fusion.1), channel_id=1, source_target_pairs={{0,8},{4,12},{8,0},{12,4},{16,24},{20,28},{24,16},{28,20},{1,9},{5... | collective-permute-start | bytes 49160 | tf_op jit(solution)/shard_map/ppermute | solution.py:349
  9.9 1.0 %copy-done.3 = bf16[1,6,128,256]{3,2,1,0:T(8,128)(2,1)S(1)} copy-done((bf16[1,6,128,256]{3,2,1,0:T(8,128)(2,1)S(1)}, bf16[1,6,128,256]{3,2,1,0:T(8,128)(2,1)}, u32[]{:S(2)}) %copy-start.3) | copy-done | bytes 393240
  10.9 0.0 collective-permute-done.8.told2
  10.9 0.1 collective-permute-start.9
  11.0 1.0 %collective-permute-done.2 = bf16[4,8,256]{2,1,0:T(8,128)(2,1)S(1)} collective-permute-done((bf16[4,8,256]{2,1,0:T(8,128)(2,1)S(1)}, bf16[4,8,256]{2,1,0:T(8,128)(2,1)S(1)}, u32[]{:S(2)}, u32[]{:S(2)}) %collective-permute-start.2) | collective-permute-done | bytes 16416 | tf_op jit(solution)/shard_map/ppermute | solution.py:349
  12.0 0.2 collective-permute-done.9.told3
  12.3 1.2 %shard_map.148 = (bf16[128,768]{1,0:T(8,128)(2,1)S(1)}, f32[32,256]{1,0:T(8,128)S(1)}, f32[256,128]{1,0:T(8,128)S(1)}, f32[8,128]{1,0:T(8,128)S(1)}) custom-call(bf16[64,640]{1,0:T(8,128)(2,1)S(1)} %copy-done.1, bf16[64,640]{1,0:T(8,128)(2,1)S(1)} %collective-permute-done.1.told1, bf16[64,640]{1,0:T(8,128)(2,1)S(1)} %collective-permute-done.8.told2, ...), custom_call_target="tpu_custom_call" | custom-call | tf_op jit(solution)/shard_map/pallas_call | solution.py:355
  13.5 0.0 copy-start.4
  13.5 1.7 %collective-permute-start.13 = (bf16[128,768]{1,0:T(8,128)(2,1)S(1)}, bf16[128,768]{1,0:T(8,128)(2,1)S(1)}, u32[]{:S(2)}, u32[]{:S(2)}) collective-permute-start(bf16[128,768]{1,0:T(8,128)(2,1)S(1)} %get-tuple-element.30), channel_id=1, source_target_pairs={{0,2},{1,3},{2,0},{3,1},{4,6},{5,7},{6,4},{7,5},{8,10},{9,11},{10,... | collective-permute-start | bytes 589832 | tf_op jit(solution)/shard_map/ppermute | solution.py:297
  15.2 2.6 %collective-permute-start.3 = (bf16[4,8,256]{2,1,0:T(8,128)(2,1)S(1)}, bf16[4,8,256]{2,1,0:T(8,128)(2,1)S(1)}, u32[]{:S(2)}, u32[]{:S(2)}) collective-permute-start(bf16[4,8,256]{2,1,0:T(8,128)(2,1)S(1)} %pad_maximum_fusion.2), channel_id=1, source_target_pairs={{0,16},{4,20},{8,24},{12,28},{16,0},{20,4},{24,8},{28,12},{1,17},{... | collective-permute-start | bytes 49160 | tf_op jit(solution)/shard_map/ppermute | solution.py:349
  17.8 2.1 %collective-permute-done.3 = bf16[4,8,256]{2,1,0:T(8,128)(2,1)S(1)} collective-permute-done((bf16[4,8,256]{2,1,0:T(8,128)(2,1)S(1)}, bf16[4,8,256]{2,1,0:T(8,128)(2,1)S(1)}, u32[]{:S(2)}, u32[]{:S(2)}) %collective-permute-start.3) | collective-permute-done | bytes 16416 | tf_op jit(solution)/shard_map/ppermute | solution.py:349
  19.9 0.4 %collective-permute-start.4 = (bf16[8,8,256]{2,1,0:T(8,128)(2,1)S(1)}, bf16[8,8,256]{2,1,0:T(8,128)(2,1)S(1)}, u32[]{:S(2)}, u32[]{:S(2)}) collective-permute-start(bf16[8,8,256]{2,1,0:T(8,128)(2,1)S(1)} %constant_dynamic-update-slice_fusion), channel_id=1, source_target_pairs={{0,2},{1,3},{2,0},{3,1},{4,6},{5,7},{6,4},{7,5},{8,10},{9,11},{10,... | collective-permute-start | bytes 98312 | tf_op jit(solution)/shard_map/ppermute | solution.py:297
  20.3 0.3 collective-permute-done.13.y2_ref
  20.6 0.5 %collective-permute-start.6 = (bf16[64,512]{1,0:T(8,128)(2,1)S(1)}, bf16[64,512]{1,0:T(8,128)(2,1)S(1)}, u32[]{:S(2)}, u32[]{:S(2)}) collective-permute-start(bf16[64,512]{1,0:T(8,128)(2,1)S(1)} %copy-done.4), channel_id=1, source_target_pairs={{0,1},{1,0},{2,3},{3,2},{4,5},{5,4},{6,7},{7,6},{8,9},{9,8},{10,11... | collective-permute-start | bytes 196616 | tf_op jit(solution)/shard_map/ppermute | solution.py:297
  21.1 2.8 %collective-permute-done.4 = bf16[8,8,256]{2,1,0:T(8,128)(2,1)S(1)} collective-permute-done((bf16[8,8,256]{2,1,0:T(8,128)(2,1)S(1)}, bf16[8,8,256]{2,1,0:T(8,128)(2,1)S(1)}, u32[]{:S(2)}, u32[]{:S(2)}) %collective-permute-start.4) | collective-permute-done | bytes 32800 | tf_op jit(solution)/shard_map/ppermute | solution.py:297
  23.9 0.1 collective-permute-start.5
  24.6 0.0 copy-start.5
  24.6 0.0 copy-start.8
  24.6 0.9 %shard_map.150.y_ref = f32[64,3072]{1,0:T(8,128)S(1)} custom-call(f32[32,256]{1,0:T(8,128)S(1)} %get-tuple-element.32.shift_ref, f32[256,128]{1,0:T(8,128)S(1)} %get-tuple-element.33.total_ref, f32[8,128]{1,0:T(8,128)S(1)} %get-tuple-element.34.skip_ref, bf16[64,640]{1,0:T(8,128)(2,1)S(1)} %copy-done.1, bf16[64,640]{1,0:T(8,128)(2,1)S(1)} %collective-permute-done.1.told1, ...), custom_call_target="tpu_custom_call" | custom-call | tf_op jit(solution)/shard_map/pallas_call | solution.py:365
  25.6 0.0 copy-start.2
  25.6 0.0 copy-start.7
  25.6 1.5 %shard_map.149.attended_ref = bf16[64,1536]{1,0:T(8,128)(2,1)S(1)} custom-call(s32[1,8]{1,0:T(1,128)S(1)} %copy-done.8, s32[1]{0:T(128)S(6)} %copy.20.length_ref, bf16[64,1536]{1,0:T(8,128)(2,1)S(1)} %copy-done.5, bf16[2,8,8,256]{3,2,1,0:T(8,128)(2,1)S(1)} %pad_maximum_fusion.pages0, bf16[2,8,8,256]{3,2,1,0:T(8,128)(2,1)S(1)} %collective-permute-done.5.pages1, ...), custom_call_target="tpu_custom_call" | custom-call | tf_op jit(solution)/shard_map/pallas_call | solution.py:368
  27.1 1.3 %shard_map.151 = bf16[64,4608]{1,0:T(8,128)(2,1)} custom-call(bf16[64,1536]{1,0:T(8,128)(2,1)S(1)} %shard_map.149.attended_ref, bf16[64,3072]{1,0:T(8,128)(2,1)S(1)} %copy-done.2, f32[1,3072]{1,0:T(1,128)S(1)} %bitcast.5, f32[64,3072]{1,0:T(8,128)S(1)} %shard_map.150.y_ref, bf16[128,768]{1,0:T(8,128)(2,1)S(1)} %collective-permute-done.13.y2_ref, ...), custom_call_target="tpu_custom_call" | custom-call | tf_op jit(solution)/shard_map/pallas_call | solution.py:372
  (33 shorter events, 0.1 us)
Async XLA Ops:
  0.0 7.2 %copy-start = (bf16[64,3072]{1,0:T(8,128)(2,1)S(1)}, bf16[64,3072]{1,0:T(8,128)(2,1)}, u32[]{:S(2)}) copy-start(bf16[64,3072]{1,0:T(8,128)(2,1)} %x0_ref.3) | copy-start | bytes 1179652
  0.0 0.8 %copy-start.6 = (bf16[8,8,256]{2,1,0:T(8,128)(2,1)S(1)}, bf16[8,8,256]{2,1,0:T(8,128)(2,1)}, u32[]{:S(2)}) copy-start(bf16[8,8,256]{2,1,0:T(8,128)(2,1)} %pool_ref.1) | copy-start | bytes 98308
  0.8 6.9 %collective-permute-start = (bf16[4,8,256]{2,1,0:T(8,128)(2,1)S(1)}, bf16[4,8,256]{2,1,0:T(8,128)(2,1)S(1)}, u32[]{:S(2)}, u32[]{:S(2)}) collective-permute-start(bf16[4,8,256]{2,1,0:T(8,128)(2,1)S(1)} %get-tuple-element.21), channel_id=1, source_target_pairs={{0,4},{4,0},{8,12},{12,8},{16,20},{20,16},{24,28},{28,24},{1,5},{5... | collective-permute-start | bytes 49160 | tf_op jit(solution)/shard_map/ppermute | solution.py:349
  5.7 2.6 %collective-permute-start.1 = (bf16[64,640]{1,0:T(8,128)(2,1)}, bf16[64,640]{1,0:T(8,128)(2,1)S(1)}, u32[]{:S(2)}, u32[]{:S(2)}) collective-permute-start(bf16[64,640]{1,0:T(8,128)(2,1)} %get-tuple-element.23.told0), channel_id=1, source_target_pairs={{0,1},{1,0},{2,3},{3,2},{4,5},{5,4},{6,7},{7,6},{8,9},{9,8},{10,11... | collective-permute-start | bytes 245768 | tf_op jit(solution)/shard_map/ppermute | solution.py:297
  5.7 5.2 %collective-permute-start.8 = (bf16[64,640]{1,0:T(8,128)(2,1)}, bf16[64,640]{1,0:T(8,128)(2,1)S(1)}, u32[]{:S(2)}, u32[]{:S(2)}) collective-permute-start(bf16[64,640]{1,0:T(8,128)(2,1)} %get-tuple-element.23.told0), channel_id=1, source_target_pairs={{0,2},{1,3},{2,0},{3,1},{4,6},{5,7},{6,4},{7,5},{8,10},{9,11},{10,... | collective-permute-start | bytes 245768 | tf_op jit(solution)/shard_map/ppermute | solution.py:297
  7.2 5.1 %collective-permute-start.11 = (bf16[64,3072]{1,0:T(8,128)(2,1)S(1)}, bf16[64,3072]{1,0:T(8,128)(2,1)S(1)}, u32[]{:S(2)}, u32[]{:S(2)}) collective-permute-start(bf16[64,3072]{1,0:T(8,128)(2,1)S(1)} %copy-done), channel_id=1, source_target_pairs={{0,1},{1,0},{2,3},{3,2},{4,5},{5,4},{6,7},{7,6},{8,9},{9,8},{10,11... | collective-permute-start | bytes 1179656 | tf_op jit(solution)/shard_map/ppermute | solution.py:297
  7.4 4.9 %collective-permute-start.10 = (bf16[1,6,128,256]{3,2,1,0:T(8,128)(2,1)}, bf16[1,6,128,256]{3,2,1,0:T(8,128)(2,1)S(1)}, u32[]{:S(2)}, u32[]{:S(2)}) collective-permute-start(bf16[1,6,128,256]{3,2,1,0:T(8,128)(2,1)} %from_ref), channel_id=1, source_target_pairs={{0,1},{1,0},{2,3},{3,2},{4,5},{5,4},{6,7},{7,6},{8,9},{9,8},{10,11... | collective-permute-start | bytes 1179656 | tf_op jit(solution)/shard_map/ppermute | solution.py:297
  7.7 10.1 %collective-permute-start.7 = (bf16[64,2048]{1,0:T(8,128)(2,1)}, bf16[64,2048]{1,0:T(8,128)(2,1)S(1)}, u32[]{:S(2)}, u32[]{:S(2)}) collective-permute-start(bf16[64,2048]{1,0:T(8,128)(2,1)} %get-tuple-element.27), channel_id=1, source_target_pairs={{0,2},{1,3},{2,0},{3,1},{4,6},{5,7},{6,4},{7,5},{8,10},{9,11},{10,... | collective-permute-start | bytes 786440 | tf_op jit(solution)/shard_map/ppermute | solution.py:297
  8.2 3.8 %collective-permute-start.2 = (bf16[4,8,256]{2,1,0:T(8,128)(2,1)S(1)}, bf16[4,8,256]{2,1,0:T(8,128)(2,1)S(1)}, u32[]{:S(2)}, u32[]{:S(2)}) collective-permute-start(bf16[4,8,256]{2,1,0:T(8,128)(2,1)S(1)} %pad_maximum_fusion.1), channel_id=1, source_target_pairs={{0,8},{4,12},{8,0},{12,4},{16,24},{20,28},{24,16},{28,20},{1,9},{5... | collective-permute-start | bytes 49160 | tf_op jit(solution)/shard_map/ppermute | solution.py:349
  9.9 1.0 %copy-start.3 = (bf16[1,6,128,256]{3,2,1,0:T(8,128)(2,1)S(1)}, bf16[1,6,128,256]{3,2,1,0:T(8,128)(2,1)}, u32[]{:S(2)}) copy-start(bf16[1,6,128,256]{3,2,1,0:T(8,128)(2,1)} %from_ref) | copy-start | bytes 1179652
  10.9 1.4 %copy-start.1 = (bf16[64,640]{1,0:T(8,128)(2,1)S(1)}, bf16[64,640]{1,0:T(8,128)(2,1)}, u32[]{:S(2)}) copy-start(bf16[64,640]{1,0:T(8,128)(2,1)} %get-tuple-element.23.told0) | copy-start | bytes 245764
  10.9 1.3 %collective-permute-start.9 = (bf16[64,640]{1,0:T(8,128)(2,1)S(1)}, bf16[64,640]{1,0:T(8,128)(2,1)S(1)}, u32[]{:S(2)}, u32[]{:S(2)}) collective-permute-start(bf16[64,640]{1,0:T(8,128)(2,1)S(1)} %collective-permute-done.8.told2), channel_id=1, source_target_pairs={{0,1},{1,0},{2,3},{3,2},{4,5},{5,4},{6,7},{7,6},{8,9},{9,8},{10,11... | collective-permute-start | bytes 245768 | tf_op jit(solution)/shard_map/ppermute | solution.py:297
  13.5 7.1 %copy-start.4 = (bf16[64,512]{1,0:T(8,128)(2,1)S(1)}, bf16[64,512]{1,0:T(8,128)(2,1)}, u32[]{:S(2)}) copy-start(bf16[64,512]{1,0:T(8,128)(2,1)} %kv0.1) | copy-start | bytes 196612
  13.5 7.1 %collective-permute-start.13 = (bf16[128,768]{1,0:T(8,128)(2,1)S(1)}, bf16[128,768]{1,0:T(8,128)(2,1)S(1)}, u32[]{:S(2)}, u32[]{:S(2)}) collective-permute-start(bf16[128,768]{1,0:T(8,128)(2,1)S(1)} %get-tuple-element.30), channel_id=1, source_target_pairs={{0,2},{1,3},{2,0},{3,1},{4,6},{5,7},{6,4},{7,5},{8,10},{9,11},{10,... | collective-permute-start | bytes 589832 | tf_op jit(solution)/shard_map/ppermute | solution.py:297
  15.2 4.7 %collective-permute-start.3 = (bf16[4,8,256]{2,1,0:T(8,128)(2,1)S(1)}, bf16[4,8,256]{2,1,0:T(8,128)(2,1)S(1)}, u32[]{:S(2)}, u32[]{:S(2)}) collective-permute-start(bf16[4,8,256]{2,1,0:T(8,128)(2,1)S(1)} %pad_maximum_fusion.2), channel_id=1, source_target_pairs={{0,16},{4,20},{8,24},{12,28},{16,0},{20,4},{24,8},{28,12},{1,17},{... | collective-permute-start | bytes 49160 | tf_op jit(solution)/shard_map/ppermute | solution.py:349
  17.8 6.8 %collective-permute-start.12 = (bf16[64,2048]{1,0:T(8,128)(2,1)S(1)}, bf16[64,2048]{1,0:T(8,128)(2,1)S(1)}, u32[]{:S(2)}, u32[]{:S(2)}) collective-permute-start(bf16[64,2048]{1,0:T(8,128)(2,1)S(1)} %collective-permute-done.7.far_ref), channel_id=1, source_target_pairs={{0,1},{1,0},{2,3},{3,2},{4,5},{5,4},{6,7},{7,6},{8,9},{9,8},{10,11... | collective-permute-start | bytes 786440 | tf_op jit(solution)/shard_map/ppermute | solution.py:297
  19.9 3.9 %collective-permute-start.4 = (bf16[8,8,256]{2,1,0:T(8,128)(2,1)S(1)}, bf16[8,8,256]{2,1,0:T(8,128)(2,1)S(1)}, u32[]{:S(2)}, u32[]{:S(2)}) collective-permute-start(bf16[8,8,256]{2,1,0:T(8,128)(2,1)S(1)} %constant_dynamic-update-slice_fusion), channel_id=1, source_target_pairs={{0,2},{1,3},{2,0},{3,1},{4,6},{5,7},{6,4},{7,5},{8,10},{9,11},{10,... | collective-permute-start | bytes 98312 | tf_op jit(solution)/shard_map/ppermute | solution.py:297
  20.6 6.5 %collective-permute-start.14 = (bf16[128,768]{1,0:T(8,128)(2,1)S(1)}, bf16[128,768]{1,0:T(8,128)(2,1)S(1)}, u32[]{:S(2)}, u32[]{:S(2)}) collective-permute-start(bf16[128,768]{1,0:T(8,128)(2,1)S(1)} %collective-permute-done.13.y2_ref), channel_id=1, source_target_pairs={{0,1},{1,0},{2,3},{3,2},{4,5},{5,4},{6,7},{7,6},{8,9},{9,8},{10,11... | collective-permute-start | bytes 589832 | tf_op jit(solution)/shard_map/ppermute | solution.py:297
  20.6 5.0 %collective-permute-start.6 = (bf16[64,512]{1,0:T(8,128)(2,1)S(1)}, bf16[64,512]{1,0:T(8,128)(2,1)S(1)}, u32[]{:S(2)}, u32[]{:S(2)}) collective-permute-start(bf16[64,512]{1,0:T(8,128)(2,1)S(1)} %copy-done.4), channel_id=1, source_target_pairs={{0,1},{1,0},{2,3},{3,2},{4,5},{5,4},{6,7},{7,6},{8,9},{9,8},{10,11... | collective-permute-start | bytes 196616 | tf_op jit(solution)/shard_map/ppermute | solution.py:297
  23.9 1.7 %collective-permute-start.5 = (bf16[2,8,8,256]{3,2,1,0:T(8,128)(2,1)S(1)}, bf16[2,8,8,256]{3,2,1,0:T(8,128)(2,1)S(1)}, u32[]{:S(2)}, u32[]{:S(2)}) collective-permute-start(bf16[2,8,8,256]{3,2,1,0:T(8,128)(2,1)S(1)} %pad_maximum_fusion.pages0), channel_id=1, source_target_pairs={{0,1},{1,0},{2,3},{3,2},{4,5},{5,4},{6,7},{7,6},{8,9},{9,8},{10,11... | collective-permute-start | bytes 196616 | tf_op jit(solution)/shard_map/ppermute | solution.py:297
  24.6 1.0 %copy-start.5 = (bf16[64,1536]{1,0:T(8,128)(2,1)S(1)}, bf16[64,1536]{1,0:T(8,128)(2,1)}, u32[]{:S(2)}) copy-start(bf16[64,1536]{1,0:T(8,128)(2,1)} %query_ref.1) | copy-start | bytes 589828
  24.6 1.0 %copy-start.8 = (s32[1,8]{1,0:T(1,128)S(1)}, s32[1,8]{1,0:T(1,128)}, u32[]{:S(2)}) copy-start(s32[1,8]{1,0:T(1,128)} %page_map_ref.1) | copy-start | bytes 100
  25.6 1.5 %copy-start.2 = (bf16[64,3072]{1,0:T(8,128)(2,1)S(1)}, bf16[64,3072]{1,0:T(8,128)(2,1)}, u32[]{:S(2)}) copy-start(bf16[64,3072]{1,0:T(8,128)(2,1)} %gate_ref.1) | copy-start | bytes 1179652
  25.6 1.5 %copy-start.7 = (f32[3072]{0:T(1024)S(1)}, f32[3072]{0:T(1024)}, u32[]{:S(2)}) copy-start(f32[3072]{0:T(1024)} %param.29) | copy-start | bytes 36868

commit v3 on v2

v3 whole, which is shorter than its diff:
```python
import math

import jax
import jax.numpy as jnp
from jax import lax
from jax.experimental import pallas as pl
from jax.experimental.pallas import tpu as pltpu
from jax.sharding import PartitionSpec as P

HD = 128
QH = 12
KVH = 2
GROUP = QH // KVH
STATE = 256
MI = 3072
PAGE = 16
LANES = 128
EPSILON = 1e-05
BF16 = jnp.bfloat16
F32 = jnp.float32
HIGHEST = lax.Precision.HIGHEST
VMEM = pl.BlockSpec(memory_space=pltpu.VMEM)
SMEM = pl.BlockSpec(memory_space=pltpu.SMEM)
ANY = pl.BlockSpec(memory_space=pl.ANY)
NOTES = slice(STATE, STATE + LANES)
AHEAD = STATE + LANES
IN_MAP = slice(AHEAD, AHEAD + STATE)
TOLD = AHEAD + STATE
KEYVALS = 2 * KVH * HD
MASK_LANE = 24
PARAM_LANE = 32
ALL_HEADS = 24


def call(kernel, outs, specs, scratch=(), limit=24):
    return pl.pallas_call(
        kernel,
        out_shape=[jax.ShapeDtypeStruct(shape, dtype) for shape, dtype in outs],
        in_specs=specs,
        out_specs=[VMEM] * len(outs),
        scratch_shapes=list(scratch),
        compiler_params=pltpu.CompilerParams(vmem_limit_bytes=limit << 20),
    )


def columns(ref, owner, width):
    return ref[:, pl.ds(pl.multiple_of(owner * width, LANES), width)]


def iota(shape, dim):
    return lax.broadcasted_iota(jnp.int32, shape, dim)


def rolled(array, first, axis):
    size = array.shape[axis]
    return pltpu.roll(array, lax.rem(size - first, size), axis)


def nt_dot(a, b, precision=None):
    return lax.dot_general(
        a, b, (((1,), (1,)), ((), ())), preferred_element_type=F32, precision=precision
    )


def pack_kernel(
    log_rate_ref, bias_ref, skip_ref, x_ref, maps_ref, logit_ref, mask_ref, keyval_ref, told_ref, ahead_ref, far_ref,
):
    me = lax.axis_index("head")
    rows, width = x_ref.shape[0], x_ref.shape[1] // 4
    far_ref[:, :width] = columns(x_ref, me ^ 2, width)
    far_ref[:, width : 2 * width] = columns(x_ref, me ^ 3, width)
    far_ref[:, 2 * width : 2 * width + STATE] = maps_ref[:, :STATE]
    far_ref[:, 2 * width + STATE :] = keyval_ref[...]
    told_ref[:, IN_MAP] = maps_ref[:, :STATE]
    told_ref[:, :STATE] = maps_ref[:, STATE:]
    ahead_ref[:, :STATE] = maps_ref[:, STATE:]
    heads, head_count = logit_ref.shape[0], log_rate_ref.shape[0]
    pick = (iota((heads, LANES), 0) == iota((heads, LANES), 1)).astype(F32).astype(BF16)
    notes = lax.dot_general(logit_ref[...], pick, (((0,), (0,)), ((), ())), preferred_element_type=F32)
    diagonal = iota((rows, rows), 0) == iota((rows, rows), 1)
    real = jnp.broadcast_to(mask_ref[...], (rows, rows)) > 0
    real = jnp.sum(jnp.where(diagonal & real, 1.0, 0.0), axis=1, keepdims=True)
    lane, row = iota((1, LANES), 1), iota((rows, 1), 0)
    params = jnp.zeros((rows, LANES), F32)
    for kind, ref in enumerate((log_rate_ref, bias_ref, skip_ref)):
        value = jnp.zeros((1, LANES), F32)
        for head in range(head_count):
            value = jnp.where(lane == PARAM_LANE + me * head_count + head, ref[head], value)
        high = value.astype(BF16).astype(F32)
        middle = (value - high).astype(BF16).astype(F32)
        for part, piece in enumerate((high, middle, value - high - middle)):
            params = jnp.where(row == 3 * kind + part, piece, params)
    in_params = (lane >= PARAM_LANE) & (lane < PARAM_LANE + ALL_HEADS)
    notes = jnp.where(lane < heads, notes, jnp.where(in_params, params, real))
    told_ref[:, NOTES] = notes.astype(BF16)
    ahead_ref[:, NOTES] = notes.astype(BF16)


def order_kernel(pool_ref, far_pool_ref, even_ref, odd_ref):
    request = lax.axis_index("dp")
    half_slots = even_ref.shape[0]

    def place(at, carry):
        distance, rest, bit = 0, at, half_slots
        while bit > 1:
            distance, rest, bit = distance + (rest % 2) * bit, rest // 2, bit // 2
        for chip, ref in enumerate((pool_ref, far_pool_ref)):
            even_ref[at, chip] = ref[request ^ distance]
            odd_ref[at, chip] = ref[request ^ distance ^ 1]
        return carry

    lax.fori_loop(0, half_slots, place, 0, unroll=half_slots <= 8)


def token_at(index, rows, me):
    return (me ^ (index // rows)) * rows + index % rows


def head_sums(tolds, me):
    rows = tolds[0].shape[0]
    span = 4 * rows
    notes = jnp.concatenate([ref[:, NOTES] for ref in tolds], axis=0)
    params = sum(ref[0:16, NOTES].astype(F32) for ref in tolds).astype(BF16)
    head, lane = iota((32, LANES), 0), iota((32, LANES), 1)
    by_row = jnp.where(head == lane, 1.0, 0.0).astype(BF16)
    by_row_params = jnp.where(head + PARAM_LANE == lane, 1.0, 0.0).astype(BF16)
    row_params = nt_dot(by_row_params, params)
    source, target = iota((LANES, LANES), 0), iota((LANES, LANES), 1)
    by_lane_params = jnp.where((source == target + PARAM_LANE) & (target < ALL_HEADS), 1.0, 0.0).astype(BF16)
    skips = jnp.dot(params, by_lane_params, preferred_element_type=F32)
    skip = skips[6:7, :] + skips[7:8, :] + skips[8:9, :]

    def row_param(kind):
        return sum(row_params[:, 3 * kind + part : 3 * kind + part + 1] for part in range(3))

    logits = nt_dot(by_row, notes)
    steps = jnp.log(1.0 + jnp.exp(logits + row_param(1))) * logits[MASK_LANE : MASK_LANE + 1, :]
    token = token_at(iota((span, span), 0), rows, me)
    source = token_at(iota((span, span), 1), rows, me)
    upto = jnp.where(source <= token, 1.0, 0.0)
    sums = nt_dot(-jnp.exp(row_param(0)) * steps, upto, HIGHEST)
    by_token = jnp.concatenate([sums] * (LANES // 32), axis=0).T
    return sums - jnp.log(steps), by_token, skip


def remote_kernel(
    told0, told1, ahead2, ahead3, x0_ref, x1_ref, prior1_ref,
    y_ref, shift_ref, total_ref, skip_ref,
):
    me = lax.axis_index("head")
    rows, width = told0.shape[0], y_ref.shape[1]
    near, head_count = 2 * rows, width // HD
    shift, total, skip = head_sums((told0, told1, ahead2, ahead3), me)
    shift_ref[...] = shift
    total_ref[...] = total
    skip_ref[...] = jnp.broadcast_to(skip, skip_ref.shape)
    block = me ^ 1
    block_shift = rolled(shift, block * head_count, 0)
    block_total = rolled(total[near:], block * head_count, 1)
    mask = jnp.concatenate([ref[:, STATE + MASK_LANE : STATE + MASK_LANE + 1] for ref in (ahead2, ahead3)], axis=0)
    mask = mask.astype(F32)
    out_map = jnp.concatenate([ahead2[:, :STATE], ahead3[:, :STATE]], axis=0)
    from_prior = nt_dot(out_map, prior1_ref[0].reshape(width, STATE))

    def write(from_x):
        for head in range(head_count):
            cols = slice(head * HD, (head + 1) * HD)
            sums = block_total[:, head : head + 1]
            y = from_prior[:, cols] * jnp.exp(sums)
            if from_x is not None:
                y = y + from_x(cols, sums - block_shift[head : head + 1, :near])
            y_ref[:, cols] = (y * mask).astype(BF16)

    @pl.when(me < 2)
    def _():
        in_map = jnp.concatenate([told0[:, IN_MAP], told1[:, IN_MAP]], axis=0)
        products = nt_dot(out_map, in_map)
        x = jnp.concatenate([columns(x0_ref, block, width), columns(x1_ref, block, width)], axis=0)

        def from_x(cols, gaps):
            return jnp.dot((jnp.exp(gaps) * products).astype(BF16), x[:, cols], preferred_element_type=F32)

        write(from_x)

    @pl.when(me >= 2)
    def _():
        write(None)


def near_kernel(
    shift_ref, total_ref, skip_ref, told0, told1, x0_ref, x1_ref, far_ref, relayed_ref,
    prior0_ref, prior1_ref, y_ref,
):
    me = lax.axis_index("head")
    rows, width = told0.shape[0], x0_ref.shape[1] // 4
    near, span, head_count = 2 * rows, 4 * rows, width // HD
    far_map = slice(2 * width, 2 * width + STATE)
    out_map = told0[:, :STATE]
    mask = told0[:, STATE + MASK_LANE : STATE + MASK_LANE + 1].astype(F32)
    shift, total, skip = shift_ref[...], total_ref[:rows, :], skip_ref[...]

    def write(with_far):
        whole = span if with_far else near
        in_map = [told0[:, IN_MAP], told1[:, IN_MAP]]
        if with_far:
            in_map += [far_ref[:, far_map], relayed_ref[:, far_map]]
        products = nt_dot(out_map, jnp.concatenate(in_map, axis=0))
        token = token_at(iota((rows, whole), 0), rows, me)
        source = token_at(iota((rows, whole), 1), rows, me)
        causal = jnp.where(source <= token, 0.0, -jnp.inf)
        for hop in range(4):
            block = me ^ hop
            block_shift = rolled(shift, block * head_count, 0)
            block_total = rolled(total, block * head_count, 1)
            block_skip = rolled(skip, block * head_count, 1)[0:1, :]
            own = columns(x0_ref, block, width)
            sources = [own, columns(x1_ref, block, width)]
            reach = near
            if hop < 2:
                reach = whole
                from_prior = nt_dot(out_map, (prior0_ref, prior1_ref)[hop][0].reshape(width, STATE))
            if reach == span:
                place = (hop, 1 - hop)
                sources += [ref[:, at * width : (at + 1) * width] for ref, at in zip((far_ref, relayed_ref), place)]
            sources = jnp.concatenate(sources, axis=0)
            for head in range(head_count):
                cols = slice(head * HD, (head + 1) * HD)
                sums = block_total[:, head : head + 1]
                weights = jnp.exp(sums - block_shift[head : head + 1, :reach] + causal[:, :reach]) * products[:, :reach]
                y = jnp.dot(weights.astype(BF16), sources[:, cols], preferred_element_type=F32)
                y = y + block_skip[:, head : head + 1] * own[:, cols].astype(F32)
                if hop < 2:
                    y = y + from_prior[:, cols] * jnp.exp(sums)
                y_ref[:, hop * width + head * HD : hop * width + (head + 1) * HD] = y * mask

    @pl.when(me < 2)
    def _():
        write(False)

    @pl.when(me >= 2)
    def _():
        write(True)


def attention_kernel(
    page_map_ref, length_ref, query_ref, pages0, pages1,
    kv0, kv1, far_ref, relayed_ref, told0, told1, told2, told3, out_ref,
):
    me = lax.axis_index("head")
    request = lax.axis_index("dp")
    rows = query_ref.shape[0]
    slots, half = pages0.shape[0], pages0.shape[2]
    part = slots * half
    cached = 2 * part
    inv_scale = 1.0 / math.sqrt(HD)
    lane = iota((1, cached), 1)

    def place(page, base):
        return jnp.where(lane % part // half == (page_map_ref[0, page] ^ request), page * PAGE, base)

    position = lax.fori_loop(0, slots, place, jnp.zeros((1, cached), jnp.int32), unroll=slots <= 8)
    position = position + ((me ^ (lane // part)) % 2) * half + lane % half
    old_shut = jnp.broadcast_to(jnp.where(position < length_ref[0], 0.0, -jnp.inf), (rows, cached))
    ones = jnp.where(iota((8, LANES), 1) == MASK_LANE, 1.0, 0.0).astype(BF16)
    token, source = iota((rows, rows), 0), iota((rows, rows), 1)
    keep = told0[:, STATE + MASK_LANE : STATE + MASK_LANE + 1].astype(F32)
    pages = [ref[:, chip].reshape(part, 2 * HD) for chip in range(2) for ref in (pages0, pages1)]

    def write(reach):
        shut = [old_shut]
        for hop, ref in enumerate((told0, told1, told2, told3)[:reach]):
            real = nt_dot(ones, ref[:, NOTES])[0:1, :] > 0.5
            limit = token if hop == 0 else jnp.where((me ^ hop) < me, rows, -1)
            shut.append(jnp.where(real & (source <= limit), 0.0, -jnp.inf))
        shut = jnp.concatenate(shut, axis=1)
        shut = jnp.concatenate([shut] * GROUP, axis=0)
        for group in range(KVH):
            queries = jnp.concatenate(
                [query_ref[:, (group * GROUP + h) * HD : (group * GROUP + h + 1) * HD] for h in range(GROUP)],
                axis=0,
            )
            here = jnp.broadcast_to(me // 2, (part, 2 * HD)) == group
            every = [jnp.where(here, pages[core], pages[core ^ 2]) for core in range(2)]
            for ref in (kv0, kv1, far_ref, relayed_ref)[:reach]:
                start = ref.shape[1] - KEYVALS + 2 * group * HD
                every.append(ref[:, start : start + 2 * HD])
            every = jnp.concatenate(every, axis=0)
            keys, values = every[:, :HD], every[:, HD:]
            scores = nt_dot(queries, keys) * inv_scale + shut
            top = jnp.max(scores, axis=1, keepdims=True)
            terms = jnp.exp(scores - top)
            total = jnp.sum(terms, axis=1, keepdims=True)
            mixed = jnp.dot(terms.astype(BF16), values, preferred_element_type=F32) / total
            for h in range(GROUP):
                head = group * GROUP + h
                out_ref[:, head * HD : (head + 1) * HD] = (mixed[h * rows : (h + 1) * rows] * keep).astype(BF16)

    @pl.when(me < 2)
    def _():
        write(2)

    @pl.when(me >= 2)
    def _():
        write(4)


def final_kernel(attended_ref, gate_ref, gain_ref, y_ref, y2_ref, y3_ref, out_ref, gated):
    me = lax.axis_index("head")
    rows, width = y_ref.shape[0], y2_ref.shape[1]
    heads_width = attended_ref.shape[1]
    out_ref[:, :heads_width] = attended_ref[...]
    squares = jnp.zeros((rows, 1), F32)
    for hop, far in enumerate((None, None, y3_ref[rows:, :], y2_ref[:rows, :])):
        gate = columns(gate_ref, me ^ hop, width).astype(F32)
        part = y_ref[:, hop * width : (hop + 1) * width]
        if far is not None:
            part = part + far.astype(F32)
        part = part.astype(BF16).astype(F32) * (gate / (1.0 + jnp.exp(-gate)))
        gated[:, hop * width : (hop + 1) * width] = part
        squares = squares + jnp.sum(part * part, axis=1, keepdims=True)
    scale = lax.rsqrt(squares / MI + EPSILON)
    for hop in range(4):
        gain = columns(gain_ref, me ^ hop, width)
        part = gated[:, hop * width : (hop + 1) * width] * scale * gain
        start = pl.multiple_of(heads_width + (me ^ hop) * width, LANES)
        out_ref[:, pl.ds(start, width)] = part.astype(BF16)


def behind(block, earlier):
    return lax.optimization_barrier((block, earlier))[0]


def hopped(block, hop):
    return lax.ppermute(block, "head", [(i, i ^ hop) for i in range(4)])


def local(
    queries,
    fresh_keyvals,
    ssm_input,
    gate_input,
    state_maps,
    step_logit,
    slot_mask,
    cache_pool,
    page_map,
    cached_lengths,
    prior_state,
    decay_log,
    step_bias,
    skip_gain,
    norm_gain,
):
    rows = ssm_input.shape[0]
    width = MI // 4
    slots, half = cache_pool.shape[0], cache_pool.shape[1]
    far_pool = hopped(cache_pool, 2)
    pages, sent = call(order_kernel, [((slots // 2, 2, half, 2 * HD), BF16)] * 2, [VMEM] * 2)(cache_pool, far_pool)
    told, ahead, far = call(
        pack_kernel,
        [((rows, TOLD), BF16), ((rows, AHEAD), BF16), ((rows, 2 * width + STATE + KEYVALS), BF16)],
        [SMEM] * 3 + [VMEM] * 5,
        limit=60,
    )(
        decay_log, step_bias, skip_gain,
        ssm_input, state_maps, step_logit.T, slot_mask.reshape(1, rows), fresh_keyvals,
    )
    prior1 = hopped(prior_state, 1)
    x1 = hopped(ssm_input, 1)
    kv1 = hopped(fresh_keyvals, 1)
    told1 = hopped(told, 1)
    ahead2 = hopped(ahead, 2)
    far = hopped(far, 2)
    ahead3 = hopped(ahead2, 1)

    parts, bit = [pages], 1
    while bit < slots:
        if bit > 1:
            keep = parts[0].shape[0] // 2
            sent = jnp.concatenate([part[keep:] for part in parts])
            parts = [part[:keep] for part in parts]
        if bit == 2:
            sent = behind(sent, told1)
        came = lax.ppermute(sent, "dp", [(i, i ^ bit) for i in range(slots)])
        keep = parts[0].shape[0]
        parts = parts + [came[i * keep : (i + 1) * keep] for i in range(len(parts))]
        bit *= 2
    y2, shift, total, skip = call(
        remote_kernel,
        [((2 * rows, width), BF16), ((32, 4 * rows), F32), ((4 * rows, LANES), F32), ((8, LANES), F32)],
        [VMEM] * 7,
    )(told, told1, ahead2, ahead3, ssm_input, x1, prior1)
    relayed = hopped(behind(far, y2), 1)
    y2 = hopped(y2, 2)
    (y,) = call(near_kernel, [((rows, MI), F32)], [VMEM] * 11)(
        shift, total, skip, told, told1, ssm_input, x1, far, relayed, prior_state, prior1
    )
    y3 = hopped(behind(y2, y), 1)
    pages = jnp.concatenate(parts)
    pages1 = hopped(pages, 1)
    (attended,) = call(attention_kernel, [((rows, QH * HD), BF16)], [SMEM] * 2 + [VMEM] * 11)(
        page_map, cached_lengths, queries, pages, pages1,
        fresh_keyvals, kv1, far, relayed, told, told1, ahead2, ahead3,
    )
    (result,) = call(
        final_kernel,
        [((rows, QH * HD + MI), BF16)],
        [VMEM] * 6,
        [pltpu.VMEM((rows, MI), F32)],
    )(attended, gate_input, norm_gain.reshape(1, MI), y, y2, y3)
    return result


def solution(mesh):
    in_specs = (
        P(("dp", "head"), None),
        P(("dp", "head"), None),
        P(("dp", "head"), None),
        P(("dp", "head"), None),
        P(("dp", "head"), None),
        P(("dp", "head"), None),
        P(("dp", "head")),
        P("dp", "head", None),
        P("dp", None),
        P("dp"),
        P("dp", "head", None, None),
        P("head"),
        P("head"),
        P("head"),
        P(),
    )
    out_specs = P(("dp", "head"), None)
    return jax.shard_map(local, mesh=mesh, in_specs=in_specs, out_specs=out_specs, check_vma=False)
```

time: 28.7 us -> 26.7 us (0.930)
  local copies, waits for them, and re-layouts: 1.85 us -> 0.06 us
    unnamed x19, local copies, waits for them, and re-layouts: 1.84 us -> 0.04 us
    ppermute x3, waiting for transfers between devices: 3.18 us -> 2.05 us  [local(): came = lax.ppermute(sent, 'dp', [(i, i ^ bit) for i in range(slots)])]
    ppermute x12, waiting for transfers between devices: 3.27 us -> 4.26 us  [hopped(): return lax.ppermute(block, 'head', [(i, i ^ hop) for i in range(4)])]
    ppermute x12, starting transfers between devices: 5.26 us -> 5.76 us  [hopped(): return lax.ppermute(block, 'head', [(i, i ^ hop) for i in range(4)])]
    ppermute x3, starting transfers between devices: 7.2 us -> 6.88 us  [local(): came = lax.ppermute(sent, 'dp', [(i, i ^ bit) for i in range(slots)])]
    pallas_call x4 -> x3, Pallas kernels: 2.84 us -> 2.96 us  [the longest x1 2.05 us: local(): call(pack_kernel, [((rows, TOLD), BF16), ((rows, AHEAD), BF16), ((rows, 2...]
  transfers between devices with their start and end apart: 15 -> 15, of which waited for: 5 -> 6; matrix products, arithmetic and copies ran while one was open for 0% -> 0% of each run, Pallas kernels for 19% -> 20%
where the time goes in v3:
time: 26.7 us; the launch traced here: 26.6 us
  starting transfers between devices  12.6 us (47%)
  Pallas kernels  6.75 us (25%)
  waiting for transfers between devices  6.31 us (24%)
  between operations  0.82 us (3%)
    ppermute x3, starting transfers between devices, local(): came = lax.ppermute(sent, 'dp', [(i, i ^ bit) for i in range(slots)])  6.88 us
    ppermute x12, starting transfers between devices, hopped(): return lax.ppermute(block, 'head', [(i, i ^ hop) for i in range(4)])  5.76 us
    ppermute x12, waiting for transfers between devices, hopped(): return lax.ppermute(block, 'head', [(i, i ^ hop) for i in range(4)])  4.26 us
    ppermute x3, waiting for transfers between devices, local(): came = lax.ppermute(sent, 'dp', [(i, i ^ bit) for i in range(slots)])  2.05 us
    pallas_call x1, Pallas kernels, local(): call(pack_kernel, [((rows, TOLD), BF16), ((rows, AHEAD), BF16), ((rows, 2...  2.05 us
    pallas_call x1, Pallas kernels, local(): call(final_kernel, [((rows, QH * HD + MI), BF16)], [VMEM] * 6, [pltpu.VME...  1.3 us
    pallas_call x1, Pallas kernels, local(): call(remote_kernel, [((2 * rows, width), BF16), ((32, 4 * rows), F32), ((...  1.28 us
    pallas_call x1, Pallas kernels, local(): call(attention_kernel, [((rows, QH * HD), BF16)], [SMEM] * 2 + [VMEM] * 11)  1.21 us
  transfers between devices with their start and end apart: 15, of which 6 were waited for; matrix products, arithmetic and copies ran while one was open for 0% of the time, Pallas kernels for 20%

profile of v3, /device:TPU:0, one launch (start us, length us, event | category | flops | bytes accessed | tf_op | source)
XLA Modules:
  0.0 26.6 jit_solution(2066855257699131218)
XLA Ops:
  0.0 2.9 %collective-permute-start = (bf16[8,8,256]{2,1,0:T(8,128)(2,1)}, bf16[8,8,256]{2,1,0:T(8,128)(2,1)S(1)}, u32[]{:S(2)}, u32[]{:S(2)}) collective-permute-start(bf16[8,8,256]{2,1,0:T(8,128)(2,1)} %pool_ref.1), channel_id=1, source_target_pairs={{0,2},{1,3},{2,0},{3,1},{4,6},{5,7},{6,4},{7,5},{8,10},{9,11},{10,... | collective-permute-start | bytes 98312 | tf_op jit(solution)/shard_map/ppermute | solution.py:334
  2.9 0.0 collective-permute-start.10
  2.9 2.0 %shard_map.146 = (bf16[64,640]{1,0:T(8,128)(2,1)}, bf16[64,384]{1,0:T(8,128)(2,1)}, bf16[64,2304]{1,0:T(8,128)(2,1)}) custom-call(f32[6]{0:T(128)} %log_rate_ref.1, f32[6]{0:T(128)} %bias_ref.1, f32[6]{0:T(128)} %skip_ref.1, bf16[64,3072]{1,0:T(8,128)(2,1)} %x0_ref.3, bf16[64,512]{1,0:T(8,128)(2,1)} %maps_ref.1, bf16[24,64]{1,0:T(8,128)(2,1)} %bitcast.4, ...), custom_call_target="tpu_custom_call" | custom-call | tf_op jit(solution)/shard_map/pallas_call | solution.py:359
  5.0 0.5 %collective-permute-start.2 = (bf16[64,640]{1,0:T(8,128)(2,1)}, bf16[64,640]{1,0:T(8,128)(2,1)S(1)}, u32[]{:S(2)}, u32[]{:S(2)}) collective-permute-start(bf16[64,640]{1,0:T(8,128)(2,1)} %get-tuple-element.19.told0), channel_id=1, source_target_pairs={{0,1},{1,0},{2,3},{3,2},{4,5},{5,4},{6,7},{7,6},{8,9},{9,8},{10,11... | collective-permute-start | bytes 245768 | tf_op jit(solution)/shard_map/ppermute | solution.py:334
  5.5 0.1 collective-permute-start.11
  5.6 0.0 collective-permute-done.far_pool_ref
  5.6 2.1 %collective-permute-start.1 = (bf16[4,2,8,256]{3,2,1,0:T(8,128)(2,1)S(1)}, bf16[4,2,8,256]{3,2,1,0:T(8,128)(2,1)S(1)}, u32[]{:S(2)}, u32[]{:S(2)}) collective-permute-start(bf16[4,2,8,256]{3,2,1,0:T(8,128)(2,1)S(1)} %get-tuple-element.18), channel_id=1, source_target_pairs={{0,4},{4,0},{8,12},{12,8},{16,20},{20,16},{24,28},{28,24},{1,5},{5... | collective-permute-start | bytes 98312 | tf_op jit(solution)/shard_map/ppermute | solution.py:384
  7.7 2.1 %collective-permute-done.8.ahead2.told2 = bf16[64,384]{1,0:T(8,128)(2,1)S(1)} collective-permute-done((bf16[64,384]{1,0:T(8,128)(2,1)}, bf16[64,384]{1,0:T(8,128)(2,1)S(1)}, u32[]{:S(2)}, u32[]{:S(2)}) %collective-permute-start.8) | collective-permute-done | bytes 49184 | tf_op jit(solution)/shard_map/ppermute | solution.py:334
  9.8 0.0 collective-permute-start.7
  9.8 0.0 collective-permute-done.1
  9.8 0.0 collective-permute-start.9
  9.8 0.0 collective-permute-done.2.told1
  9.9 2.2 %collective-permute-start.3 = (bf16[4,2,8,256]{3,2,1,0:T(8,128)(2,1)S(1)}, bf16[4,2,8,256]{3,2,1,0:T(8,128)(2,1)S(1)}, u32[]{:S(2)}, u32[]{:S(2)}) collective-permute-start(bf16[4,2,8,256]{3,2,1,0:T(8,128)(2,1)S(1)} %pad_maximum_fusion), channel_id=1, source_target_pairs={{0,8},{4,12},{8,0},{12,4},{16,24},{20,28},{24,16},{28,20},{1,9},{5... | collective-permute-start | bytes 98312 | tf_op jit(solution)/shard_map/ppermute | solution.py:384
  12.0 2.0 %collective-permute-done.3 = bf16[4,2,8,256]{3,2,1,0:T(8,128)(2,1)S(1)} collective-permute-done((bf16[4,2,8,256]{3,2,1,0:T(8,128)(2,1)S(1)}, bf16[4,2,8,256]{3,2,1,0:T(8,128)(2,1)S(1)}, u32[]{:S(2)}, u32[]{:S(2)}) %collective-permute-start.3) | collective-permute-done | bytes 32800 | tf_op jit(solution)/shard_map/ppermute | solution.py:384
  14.1 0.0 collective-permute-done.9.ahead3.told3
  14.1 0.0 collective-permute-done.10.x1_ref
  14.1 0.0 copy-start.2
  14.1 1.3 %shard_map.147 = (bf16[128,768]{1,0:T(8,128)(2,1)S(1)}, f32[32,256]{1,0:T(8,128)S(1)}, f32[256,128]{1,0:T(8,128)S(1)}, f32[8,128]{1,0:T(8,128)S(1)}) custom-call(bf16[64,640]{1,0:T(8,128)(2,1)S(1)} %copy-done.1, bf16[64,640]{1,0:T(8,128)(2,1)S(1)} %collective-permute-done.2.told1, bf16[64,384]{1,0:T(8,128)(2,1)S(1)} %collective-permute-done.8.ahead2.told2, ...), custom_call_target="tpu_custom_call" | custom-call | tf_op jit(solution)/shard_map/pallas_call | solution.py:388
  15.4 1.6 %collective-permute-start.13 = (bf16[128,768]{1,0:T(8,128)(2,1)S(1)}, bf16[128,768]{1,0:T(8,128)(2,1)S(1)}, u32[]{:S(2)}, u32[]{:S(2)}) collective-permute-start(bf16[128,768]{1,0:T(8,128)(2,1)S(1)} %get-tuple-element.23), channel_id=1, source_target_pairs={{0,2},{1,3},{2,0},{3,1},{4,6},{5,7},{6,4},{7,5},{8,10},{9,11},{10,... | collective-permute-start | bytes 589832 | tf_op jit(solution)/shard_map/ppermute | solution.py:334
  17.0 0.7 %collective-permute-done.7.far_ref = bf16[64,2304]{1,0:T(8,128)(2,1)S(1)} collective-permute-done((bf16[64,2304]{1,0:T(8,128)(2,1)}, bf16[64,2304]{1,0:T(8,128)(2,1)S(1)}, u32[]{:S(2)}, u32[]{:S(2)}) %collective-permute-start.7) | collective-permute-done | bytes 294944 | tf_op jit(solution)/shard_map/ppermute | solution.py:334
  17.8 0.0 collective-permute-start.12
  17.8 2.7 %collective-permute-start.4 = (bf16[4,2,8,256]{3,2,1,0:T(8,128)(2,1)S(1)}, bf16[4,2,8,256]{3,2,1,0:T(8,128)(2,1)S(1)}, u32[]{:S(2)}, u32[]{:S(2)}) collective-permute-start(bf16[4,2,8,256]{3,2,1,0:T(8,128)(2,1)S(1)} %pad_maximum_fusion.1), channel_id=1, source_target_pairs={{0,16},{4,20},{8,24},{12,28},{16,0},{20,4},{24,8},{28,12},{1,17},{... | collective-permute-start | bytes 98312 | tf_op jit(solution)/shard_map/ppermute | solution.py:384
  20.5 0.9 %shard_map.149.y_ref = f32[64,3072]{1,0:T(8,128)S(1)} custom-call(f32[32,256]{1,0:T(8,128)S(1)} %get-tuple-element.25.shift_ref, f32[256,128]{1,0:T(8,128)S(1)} %get-tuple-element.26.total_ref, f32[8,128]{1,0:T(8,128)S(1)} %get-tuple-element.27.skip_ref, bf16[64,640]{1,0:T(8,128)(2,1)S(1)} %copy-done.1, bf16[64,640]{1,0:T(8,128)(2,1)S(1)} %collective-permute-done.2.told1, ...), custom_call_target="tpu_custom_call" | custom-call | tf_op jit(solution)/shard_map/pallas_call | solution.py:395
  21.4 0.8 %collective-permute-done.13.y2_ref = bf16[128,768]{1,0:T(8,128)(2,1)S(1)} collective-permute-done((bf16[128,768]{1,0:T(8,128)(2,1)S(1)}, bf16[128,768]{1,0:T(8,128)(2,1)S(1)}, u32[]{:S(2)}, u32[]{:S(2)}) %collective-permute-start.13) | collective-permute-done | bytes 196640 | tf_op jit(solution)/shard_map/ppermute | solution.py:334
  22.2 0.5 %collective-permute-start.6 = (bf16[64,512]{1,0:T(8,128)(2,1)S(1)}, bf16[64,512]{1,0:T(8,128)(2,1)S(1)}, u32[]{:S(2)}, u32[]{:S(2)}) collective-permute-start(bf16[64,512]{1,0:T(8,128)(2,1)S(1)} %copy-done.4), channel_id=1, source_target_pairs={{0,1},{1,0},{2,3},{3,2},{4,5},{5,4},{6,7},{7,6},{8,9},{9,8},{10,11... | collective-permute-start | bytes 196616 | tf_op jit(solution)/shard_map/ppermute | solution.py:334
  22.7 0.1 collective-permute-start.5
  23.5 0.0 copy-start.3
  23.5 0.0 copy-start.7
  23.5 0.2 collective-permute-done.6.kv1
  23.7 0.3 %collective-permute-done.5.pages1 = bf16[8,2,8,256]{3,2,1,0:T(8,128)(2,1)S(1)} collective-permute-done((bf16[8,2,8,256]{3,2,1,0:T(8,128)(2,1)S(1)}, bf16[8,2,8,256]{3,2,1,0:T(8,128)(2,1)S(1)}, u32[]{:S(2)}, u32[]{:S(2)}) %collective-permute-start.5) | collective-permute-done | bytes 65568 | tf_op jit(solution)/shard_map/ppermute | solution.py:334
  24.0 1.2 %shard_map.148.attended_ref = bf16[64,1536]{1,0:T(8,128)(2,1)S(1)} custom-call(s32[1,8]{1,0:T(1,128)S(1)} %copy-done.8, s32[1]{0:T(128)S(6)} %copy.20.length_ref, bf16[64,1536]{1,0:T(8,128)(2,1)S(1)} %copy-done.5, bf16[8,2,8,256]{3,2,1,0:T(8,128)(2,1)S(1)} %constant_dynamic-update-slice_fusion.pages0, ...), custom_call_target="tpu_custom_call" | custom-call | tf_op jit(solution)/shard_map/pallas_call | solution.py:401
  25.3 1.3 %shard_map.150 = bf16[64,4608]{1,0:T(8,128)(2,1)} custom-call(bf16[64,1536]{1,0:T(8,128)(2,1)S(1)} %shard_map.148.attended_ref, bf16[64,3072]{1,0:T(8,128)(2,1)S(1)} %copy-done.3, f32[1,3072]{1,0:T(1,128)S(1)} %bitcast.3, f32[64,3072]{1,0:T(8,128)S(1)} %shard_map.149.y_ref, bf16[128,768]{1,0:T(8,128)(2,1)S(1)} %collective-permute-done.13.y2_ref, ...), custom_call_target="tpu_custom_call" | custom-call | tf_op jit(solution)/shard_map/pallas_call | solution.py:405
  (31 shorter events, 0.1 us)
Async XLA Ops:
  0.0 5.6 %collective-permute-start = (bf16[8,8,256]{2,1,0:T(8,128)(2,1)}, bf16[8,8,256]{2,1,0:T(8,128)(2,1)S(1)}, u32[]{:S(2)}, u32[]{:S(2)}) collective-permute-start(bf16[8,8,256]{2,1,0:T(8,128)(2,1)} %pool_ref.1), channel_id=1, source_target_pairs={{0,2},{1,3},{2,0},{3,1},{4,6},{5,7},{6,4},{7,5},{8,10},{9,11},{10,... | collective-permute-start | bytes 98312 | tf_op jit(solution)/shard_map/ppermute | solution.py:334
  2.9 11.1 %collective-permute-start.10 = (bf16[64,3072]{1,0:T(8,128)(2,1)}, bf16[64,3072]{1,0:T(8,128)(2,1)S(1)}, u32[]{:S(2)}, u32[]{:S(2)}) collective-permute-start(bf16[64,3072]{1,0:T(8,128)(2,1)} %x0_ref.3), channel_id=1, source_target_pairs={{0,1},{1,0},{2,3},{3,2},{4,5},{5,4},{6,7},{7,6},{8,9},{9,8},{10,11... | collective-permute-start | bytes 1179656 | tf_op jit(solution)/shard_map/ppermute | solution.py:334
  2.9 2.6 %copy-start.6 = (bf16[8,8,256]{2,1,0:T(8,128)(2,1)S(1)}, bf16[8,8,256]{2,1,0:T(8,128)(2,1)}, u32[]{:S(2)}) copy-start(bf16[8,8,256]{2,1,0:T(8,128)(2,1)} %pool_ref.1) | copy-start | bytes 98308
  2.9 11.1 %copy-start = (bf16[64,3072]{1,0:T(8,128)(2,1)S(1)}, bf16[64,3072]{1,0:T(8,128)(2,1)}, u32[]{:S(2)}) copy-start(bf16[64,3072]{1,0:T(8,128)(2,1)} %x0_ref.3) | copy-start | bytes 1179652
  5.0 4.9 %collective-permute-start.2 = (bf16[64,640]{1,0:T(8,128)(2,1)}, bf16[64,640]{1,0:T(8,128)(2,1)S(1)}, u32[]{:S(2)}, u32[]{:S(2)}) collective-permute-start(bf16[64,640]{1,0:T(8,128)(2,1)} %get-tuple-element.19.told0), channel_id=1, source_target_pairs={{0,1},{1,0},{2,3},{3,2},{4,5},{5,4},{6,7},{7,6},{8,9},{9,8},{10,11... | collective-permute-start | bytes 245768 | tf_op jit(solution)/shard_map/ppermute | solution.py:334
  5.5 4.3 %collective-permute-start.8 = (bf16[64,384]{1,0:T(8,128)(2,1)}, bf16[64,384]{1,0:T(8,128)(2,1)S(1)}, u32[]{:S(2)}, u32[]{:S(2)}) collective-permute-start(bf16[64,384]{1,0:T(8,128)(2,1)} %get-tuple-element.22), channel_id=1, source_target_pairs={{0,2},{1,3},{2,0},{3,1},{4,6},{5,7},{6,4},{7,5},{8,10},{9,11},{10,... | collective-permute-start | bytes 147464 | tf_op jit(solution)/shard_map/ppermute | solution.py:334
  5.5 8.6 %collective-permute-start.11 = (bf16[1,6,128,256]{3,2,1,0:T(8,128)(2,1)}, bf16[1,6,128,256]{3,2,1,0:T(8,128)(2,1)S(1)}, u32[]{:S(2)}, u32[]{:S(2)}) collective-permute-start(bf16[1,6,128,256]{3,2,1,0:T(8,128)(2,1)} %prior0_ref.1), channel_id=1, source_target_pairs={{0,1},{1,0},{2,3},{3,2},{4,5},{5,4},{6,7},{7,6},{8,9},{9,8},{10,11... | collective-permute-start | bytes 1179656 | tf_op jit(solution)/shard_map/ppermute | solution.py:334
  5.6 4.2 %collective-permute-start.1 = (bf16[4,2,8,256]{3,2,1,0:T(8,128)(2,1)S(1)}, bf16[4,2,8,256]{3,2,1,0:T(8,128)(2,1)S(1)}, u32[]{:S(2)}, u32[]{:S(2)}) collective-permute-start(bf16[4,2,8,256]{3,2,1,0:T(8,128)(2,1)S(1)} %get-tuple-element.18), channel_id=1, source_target_pairs={{0,4},{4,0},{8,12},{12,8},{16,20},{20,16},{24,28},{28,24},{1,5},{5... | collective-permute-start | bytes 98312 | tf_op jit(solution)/shard_map/ppermute | solution.py:384
  7.7 6.4 %copy-start.1 = (bf16[64,640]{1,0:T(8,128)(2,1)S(1)}, bf16[64,640]{1,0:T(8,128)(2,1)}, u32[]{:S(2)}) copy-start(bf16[64,640]{1,0:T(8,128)(2,1)} %get-tuple-element.19.told0) | copy-start | bytes 245764
  9.8 8.0 %collective-permute-start.7 = (bf16[64,2304]{1,0:T(8,128)(2,1)}, bf16[64,2304]{1,0:T(8,128)(2,1)S(1)}, u32[]{:S(2)}, u32[]{:S(2)}) collective-permute-start(bf16[64,2304]{1,0:T(8,128)(2,1)} %get-tuple-element.21), channel_id=1, source_target_pairs={{0,2},{1,3},{2,0},{3,1},{4,6},{5,7},{6,4},{7,5},{8,10},{9,11},{10,... | collective-permute-start | bytes 884744 | tf_op jit(solution)/shard_map/ppermute | solution.py:334
  9.8 4.3 %collective-permute-start.9 = (bf16[64,384]{1,0:T(8,128)(2,1)S(1)}, bf16[64,384]{1,0:T(8,128)(2,1)S(1)}, u32[]{:S(2)}, u32[]{:S(2)}) collective-permute-start(bf16[64,384]{1,0:T(8,128)(2,1)S(1)} %collective-permute-done.8.ahead2.told2), channel_id=1, source_target_pairs={{0,1},{1,0},{2,3},{3,2},{4,5},{5,4},{6,7},{7,6},{8,9},{9,8},{10,11... | collective-permute-start | bytes 147464 | tf_op jit(solution)/shard_map/ppermute | solution.py:334
  9.9 4.2 %collective-permute-start.3 = (bf16[4,2,8,256]{3,2,1,0:T(8,128)(2,1)S(1)}, bf16[4,2,8,256]{3,2,1,0:T(8,128)(2,1)S(1)}, u32[]{:S(2)}, u32[]{:S(2)}) collective-permute-start(bf16[4,2,8,256]{3,2,1,0:T(8,128)(2,1)S(1)} %pad_maximum_fusion), channel_id=1, source_target_pairs={{0,8},{4,12},{8,0},{12,4},{16,24},{20,28},{24,16},{28,20},{1,9},{5... | collective-permute-start | bytes 98312 | tf_op jit(solution)/shard_map/ppermute | solution.py:384
  14.1 6.4 %copy-start.2 = (bf16[1,6,128,256]{3,2,1,0:T(8,128)(2,1)S(1)}, bf16[1,6,128,256]{3,2,1,0:T(8,128)(2,1)}, u32[]{:S(2)}) copy-start(bf16[1,6,128,256]{3,2,1,0:T(8,128)(2,1)} %prior0_ref.1) | copy-start | bytes 1179652
  15.4 6.8 %collective-permute-start.13 = (bf16[128,768]{1,0:T(8,128)(2,1)S(1)}, bf16[128,768]{1,0:T(8,128)(2,1)S(1)}, u32[]{:S(2)}, u32[]{:S(2)}) collective-permute-start(bf16[128,768]{1,0:T(8,128)(2,1)S(1)} %get-tuple-element.23), channel_id=1, source_target_pairs={{0,2},{1,3},{2,0},{3,1},{4,6},{5,7},{6,4},{7,5},{8,10},{9,11},{10,... | collective-permute-start | bytes 589832 | tf_op jit(solution)/shard_map/ppermute | solution.py:334
  17.8 2.7 %collective-permute-start.12 = (bf16[64,2304]{1,0:T(8,128)(2,1)S(1)}, bf16[64,2304]{1,0:T(8,128)(2,1)S(1)}, u32[]{:S(2)}, u32[]{:S(2)}) collective-permute-start(bf16[64,2304]{1,0:T(8,128)(2,1)S(1)} %collective-permute-done.7.far_ref), channel_id=1, source_target_pairs={{0,1},{1,0},{2,3},{3,2},{4,5},{5,4},{6,7},{7,6},{8,9},{9,8},{10,11... | collective-permute-start | bytes 884744 | tf_op jit(solution)/shard_map/ppermute | solution.py:334
  17.8 4.9 %collective-permute-start.4 = (bf16[4,2,8,256]{3,2,1,0:T(8,128)(2,1)S(1)}, bf16[4,2,8,256]{3,2,1,0:T(8,128)(2,1)S(1)}, u32[]{:S(2)}, u32[]{:S(2)}) collective-permute-start(bf16[4,2,8,256]{3,2,1,0:T(8,128)(2,1)S(1)} %pad_maximum_fusion.1), channel_id=1, source_target_pairs={{0,16},{4,20},{8,24},{12,28},{16,0},{20,4},{24,8},{28,12},{1,17},{... | collective-permute-start | bytes 98312 | tf_op jit(solution)/shard_map/ppermute | solution.py:384
  20.5 1.7 %copy-start.4 = (bf16[64,512]{1,0:T(8,128)(2,1)S(1)}, bf16[64,512]{1,0:T(8,128)(2,1)}, u32[]{:S(2)}) copy-start(bf16[64,512]{1,0:T(8,128)(2,1)} %kv0.1) | copy-start | bytes 196612
  20.5 3.6 %copy-start.5 = (bf16[64,1536]{1,0:T(8,128)(2,1)S(1)}, bf16[64,1536]{1,0:T(8,128)(2,1)}, u32[]{:S(2)}) copy-start(bf16[64,1536]{1,0:T(8,128)(2,1)} %query_ref.1) | copy-start | bytes 589828
  22.2 3.1 %collective-permute-start.14 = (bf16[128,768]{1,0:T(8,128)(2,1)S(1)}, bf16[128,768]{1,0:T(8,128)(2,1)S(1)}, u32[]{:S(2)}, u32[]{:S(2)}) collective-permute-start(bf16[128,768]{1,0:T(8,128)(2,1)S(1)} %collective-permute-done.13.y2_ref), channel_id=1, source_target_pairs={{0,1},{1,0},{2,3},{3,2},{4,5},{5,4},{6,7},{7,6},{8,9},{9,8},{10,11... | collective-permute-start | bytes 589832 | tf_op jit(solution)/shard_map/ppermute | solution.py:334
  22.2 1.5 %collective-permute-start.6 = (bf16[64,512]{1,0:T(8,128)(2,1)S(1)}, bf16[64,512]{1,0:T(8,128)(2,1)S(1)}, u32[]{:S(2)}, u32[]{:S(2)}) collective-permute-start(bf16[64,512]{1,0:T(8,128)(2,1)S(1)} %copy-done.4), channel_id=1, source_target_pairs={{0,1},{1,0},{2,3},{3,2},{4,5},{5,4},{6,7},{7,6},{8,9},{9,8},{10,11... | collective-permute-start | bytes 196616 | tf_op jit(solution)/shard_map/ppermute | solution.py:334
  22.7 1.3 %copy-start.8 = (s32[1,8]{1,0:T(1,128)S(1)}, s32[1,8]{1,0:T(1,128)}, u32[]{:S(2)}) copy-start(s32[1,8]{1,0:T(1,128)} %page_map_ref.1) | copy-start | bytes 100
  22.7 1.3 %collective-permute-start.5 = (bf16[8,2,8,256]{3,2,1,0:T(8,128)(2,1)S(1)}, bf16[8,2,8,256]{3,2,1,0:T(8,128)(2,1)S(1)}, u32[]{:S(2)}, u32[]{:S(2)}) collective-permute-start(bf16[8,2,8,256]{3,2,1,0:T(8,128)(2,1)S(1)} %constant_dynamic-update-slice_fusion.pages0), channel_id=1, source_target_pairs={{0,1},{1,0},{2,3},{3,2},{4,5},{5,4},{6,7},{7,6},{8,9},{9,8},{10,11... | collective-permute-start | bytes 196616 | tf_op jit(solution)/shard_map/ppermute | solution.py:334
  23.5 1.8 %copy-start.3 = (bf16[64,3072]{1,0:T(8,128)(2,1)S(1)}, bf16[64,3072]{1,0:T(8,128)(2,1)}, u32[]{:S(2)}) copy-start(bf16[64,3072]{1,0:T(8,128)(2,1)} %gate_ref.1) | copy-start | bytes 1179652
  23.5 1.8 %copy-start.7 = (f32[3072]{0:T(1024)S(1)}, f32[3072]{0:T(1024)}, u32[]{:S(2)}) copy-start(f32[3072]{0:T(1024)} %param.29) | copy-start | bytes 36868

commit v4 on v3

--- a/solution.py
+++ b/solution.py
@@ -253,14 +253,14 @@
     part = slots * half
     cached = 2 * part
     inv_scale = 1.0 / math.sqrt(HD)
+    square, wide = (slots, slots), (slots, cached)
+    holders = jnp.where(iota(square, 0) == iota(square, 1), jnp.broadcast_to(page_map_ref[...], square), 0)
+    holders = jnp.sum(holders.astype(F32), axis=1, keepdims=True).astype(jnp.int32)
+    page = jnp.where((holders ^ request) == iota(wide, 1) % part // half, iota(wide, 0), 0)
+    page = jnp.sum(page.astype(F32), axis=0, keepdims=True).astype(jnp.int32)
     lane = iota((1, cached), 1)
-
-    def place(page, base):
-        return jnp.where(lane % part // half == (page_map_ref[0, page] ^ request), page * PAGE, base)
-
-    position = lax.fori_loop(0, slots, place, jnp.zeros((1, cached), jnp.int32), unroll=slots <= 8)
-    position = position + ((me ^ (lane // part)) % 2) * half + lane % half
-    old_shut = jnp.broadcast_to(jnp.where(position < length_ref[0], 0.0, -jnp.inf), (rows, cached))
+    position = page * PAGE + ((me ^ (lane // part)) % 2) * half + lane % half
+    old_shut = jnp.broadcast_to(jnp.where(position < length_ref[...], 0.0, -jnp.inf), (rows, cached))
     ones = jnp.where(iota((8, LANES), 1) == MASK_LANE, 1.0, 0.0).astype(BF16)
     token, source = iota((rows, rows), 0), iota((rows, rows), 1)
     keep = told0[:, STATE + MASK_LANE : STATE + MASK_LANE + 1].astype(F32)
@@ -398,8 +398,8 @@
     y3 = hopped(behind(y2, y), 1)
     pages = jnp.concatenate(parts)
     pages1 = hopped(pages, 1)
-    (attended,) = call(attention_kernel, [((rows, QH * HD), BF16)], [SMEM] * 2 + [VMEM] * 11)(
-        page_map, cached_lengths, queries, pages, pages1,
+    (attended,) = call(attention_kernel, [((rows, QH * HD), BF16)], [VMEM] * 13)(
+        page_map, cached_lengths.reshape(1, 1), queries, pages, pages1,
         fresh_keyvals, kv1, far, relayed, told, told1, ahead2, ahead3,
     )
     (result,) = call(

time: 26.7 us -> 26.6 us (level)
  Pallas kernels: 6.75 us -> 6.29 us
  local copies, waits for them, and re-layouts: 0.06 us -> 0.4 us
    pallas_call x1, Pallas kernels: 1.21 us -> 0.75 us  [local(): call(attention_kernel, [((rows, QH * HD), BF16)], [VMEM] * 13)]
    unnamed x19, local copies, waits for them, and re-layouts: 0.04 us -> 0.39 us
  transfers between devices with their start and end apart: 15 -> 15, of which waited for: 6 -> 6; matrix products, arithmetic and copies ran while one was open for 0% -> 0% of each run, Pallas kernels for 20% -> 19%
where the time goes in v4:
time: 26.6 us; the launch traced here: 26.4 us
  starting transfers between devices  12.6 us (47%)
  Pallas kernels  6.29 us (24%)
  waiting for transfers between devices  6.27 us (24%)
  between operations  0.79 us (3%)
  local copies, waits for them, and re-layouts  0.4 us (2%)
    ppermute x3, starting transfers between devices, local(): came = lax.ppermute(sent, 'dp', [(i, i ^ bit) for i in range(slots)])  6.88 us
    ppermute x12, starting transfers between devices, hopped(): return lax.ppermute(block, 'head', [(i, i ^ hop) for i in range(4)])  5.76 us
    ppermute x12, waiting for transfers between devices, hopped(): return lax.ppermute(block, 'head', [(i, i ^ hop) for i in range(4)])  4.22 us
    ppermute x3, waiting for transfers between devices, local(): came = lax.ppermute(sent, 'dp', [(i, i ^ bit) for i in range(slots)])  2.05 us
    pallas_call x1, Pallas kernels, local(): call(pack_kernel, [((rows, TOLD), BF16), ((rows, AHEAD), BF16), ((rows, 2...  2.05 us
    pallas_call x1, Pallas kernels, local(): call(final_kernel, [((rows, QH * HD + MI), BF16)], [VMEM] * 6, [pltpu.VME...  1.3 us
    pallas_call x1, Pallas kernels, local(): call(remote_kernel, [((2 * rows, width), BF16), ((32, 4 * rows), F32), ((...  1.28 us
    pallas_call x1, Pallas kernels, local(): call(near_kernel, [((rows, MI), F32)], [VMEM] * 11)  0.9 us
  transfers between devices with their start and end apart: 15, of which 6 were waited for; matrix products, arithmetic and copies ran while one was open for 0% of the time, Pallas kernels for 19%

profile of v4, /device:TPU:0, one launch (start us, length us, event | category | flops | bytes accessed | tf_op | source)
XLA Modules:
  0.0 26.4 jit_solution(13029223966284123732)
XLA Ops:
  0.0 2.9 %collective-permute-start = (bf16[8,8,256]{2,1,0:T(8,128)(2,1)}, bf16[8,8,256]{2,1,0:T(8,128)(2,1)S(1)}, u32[]{:S(2)}, u32[]{:S(2)}) collective-permute-start(bf16[8,8,256]{2,1,0:T(8,128)(2,1)} %pool_ref.1), channel_id=1, source_target_pairs={{0,2},{1,3},{2,0},{3,1},{4,6},{5,7},{6,4},{7,5},{8,10},{9,11},{10,... | collective-permute-start | bytes 98312 | tf_op jit(solution)/shard_map/ppermute | solution.py:334
  2.9 2.0 %shard_map.146 = (bf16[64,640]{1,0:T(8,128)(2,1)}, bf16[64,384]{1,0:T(8,128)(2,1)}, bf16[64,2304]{1,0:T(8,128)(2,1)}) custom-call(f32[6]{0:T(128)} %log_rate_ref.1, f32[6]{0:T(128)} %bias_ref.1, f32[6]{0:T(128)} %skip_ref.1, bf16[64,3072]{1,0:T(8,128)(2,1)} %x0_ref.3, bf16[64,512]{1,0:T(8,128)(2,1)} %maps_ref.1, bf16[24,64]{1,0:T(8,128)(2,1)} %bitcast.6, ...), custom_call_target="tpu_custom_call" | custom-call | tf_op jit(solution)/shard_map/pallas_call | solution.py:359
  5.0 0.5 %collective-permute-start.2 = (bf16[64,640]{1,0:T(8,128)(2,1)}, bf16[64,640]{1,0:T(8,128)(2,1)S(1)}, u32[]{:S(2)}, u32[]{:S(2)}) collective-permute-start(bf16[64,640]{1,0:T(8,128)(2,1)} %get-tuple-element.19.told0), channel_id=1, source_target_pairs={{0,1},{1,0},{2,3},{3,2},{4,5},{5,4},{6,7},{7,6},{8,9},{9,8},{10,11... | collective-permute-start | bytes 245768 | tf_op jit(solution)/shard_map/ppermute | solution.py:334
  5.5 0.1 collective-permute-start.11
  5.6 2.1 %collective-permute-start.1 = (bf16[4,2,8,256]{3,2,1,0:T(8,128)(2,1)S(1)}, bf16[4,2,8,256]{3,2,1,0:T(8,128)(2,1)S(1)}, u32[]{:S(2)}, u32[]{:S(2)}) collective-permute-start(bf16[4,2,8,256]{3,2,1,0:T(8,128)(2,1)S(1)} %get-tuple-element.18), channel_id=1, source_target_pairs={{0,4},{4,0},{8,12},{12,8},{16,20},{20,16},{24,28},{28,24},{1,5},{5... | collective-permute-start | bytes 98312 | tf_op jit(solution)/shard_map/ppermute | solution.py:384
  7.7 2.1 %collective-permute-done.8.ahead2.told2 = bf16[64,384]{1,0:T(8,128)(2,1)S(1)} collective-permute-done((bf16[64,384]{1,0:T(8,128)(2,1)}, bf16[64,384]{1,0:T(8,128)(2,1)S(1)}, u32[]{:S(2)}, u32[]{:S(2)}) %collective-permute-start.8) | collective-permute-done | bytes 49184 | tf_op jit(solution)/shard_map/ppermute | solution.py:334
  9.8 0.0 collective-permute-start.7
  9.8 0.0 collective-permute-done.1
  9.8 0.0 collective-permute-start.9
  9.9 2.2 %collective-permute-start.3 = (bf16[4,2,8,256]{3,2,1,0:T(8,128)(2,1)S(1)}, bf16[4,2,8,256]{3,2,1,0:T(8,128)(2,1)S(1)}, u32[]{:S(2)}, u32[]{:S(2)}) collective-permute-start(bf16[4,2,8,256]{3,2,1,0:T(8,128)(2,1)S(1)} %pad_maximum_fusion), channel_id=1, source_target_pairs={{0,8},{4,12},{8,0},{12,4},{16,24},{20,28},{24,16},{28,20},{1,9},{5... | collective-permute-start | bytes 98312 | tf_op jit(solution)/shard_map/ppermute | solution.py:384
  12.0 2.0 %collective-permute-done.3 = bf16[4,2,8,256]{3,2,1,0:T(8,128)(2,1)S(1)} collective-permute-done((bf16[4,2,8,256]{3,2,1,0:T(8,128)(2,1)S(1)}, bf16[4,2,8,256]{3,2,1,0:T(8,128)(2,1)S(1)}, u32[]{:S(2)}, u32[]{:S(2)}) %collective-permute-start.3) | collective-permute-done | bytes 32800 | tf_op jit(solution)/shard_map/ppermute | solution.py:384
  14.1 0.0 collective-permute-done.9.ahead3.told3
  14.1 0.0 collective-permute-done.10.x1_ref
  14.1 0.0 collective-permute-done.11.prior1_ref
  14.1 0.0 copy-start.2
  14.1 1.3 %shard_map.147 = (bf16[128,768]{1,0:T(8,128)(2,1)S(1)}, f32[32,256]{1,0:T(8,128)S(1)}, f32[256,128]{1,0:T(8,128)S(1)}, f32[8,128]{1,0:T(8,128)S(1)}) custom-call(bf16[64,640]{1,0:T(8,128)(2,1)S(1)} %copy-done.1, bf16[64,640]{1,0:T(8,128)(2,1)S(1)} %collective-permute-done.2.told1, bf16[64,384]{1,0:T(8,128)(2,1)S(1)} %collective-permute-done.8.ahead2.told2, ...), custom_call_target="tpu_custom_call" | custom-call | tf_op jit(solution)/shard_map/pallas_call | solution.py:388
  15.4 1.6 %collective-permute-start.13 = (bf16[128,768]{1,0:T(8,128)(2,1)S(1)}, bf16[128,768]{1,0:T(8,128)(2,1)S(1)}, u32[]{:S(2)}, u32[]{:S(2)}) collective-permute-start(bf16[128,768]{1,0:T(8,128)(2,1)S(1)} %get-tuple-element.23), channel_id=1, source_target_pairs={{0,2},{1,3},{2,0},{3,1},{4,6},{5,7},{6,4},{7,5},{8,10},{9,11},{10,... | collective-permute-start | bytes 589832 | tf_op jit(solution)/shard_map/ppermute | solution.py:334
  17.0 0.7 %collective-permute-done.7.far_ref = bf16[64,2304]{1,0:T(8,128)(2,1)S(1)} collective-permute-done((bf16[64,2304]{1,0:T(8,128)(2,1)}, bf16[64,2304]{1,0:T(8,128)(2,1)S(1)}, u32[]{:S(2)}, u32[]{:S(2)}) %collective-permute-start.7) | collective-permute-done | bytes 294944 | tf_op jit(solution)/shard_map/ppermute | solution.py:334
  17.8 0.0 collective-permute-start.12
  17.8 2.7 %collective-permute-start.4 = (bf16[4,2,8,256]{3,2,1,0:T(8,128)(2,1)S(1)}, bf16[4,2,8,256]{3,2,1,0:T(8,128)(2,1)S(1)}, u32[]{:S(2)}, u32[]{:S(2)}) collective-permute-start(bf16[4,2,8,256]{3,2,1,0:T(8,128)(2,1)S(1)} %pad_maximum_fusion.1), channel_id=1, source_target_pairs={{0,16},{4,20},{8,24},{12,28},{16,0},{20,4},{24,8},{28,12},{1,17},{... | collective-permute-start | bytes 98312 | tf_op jit(solution)/shard_map/ppermute | solution.py:384
  20.5 0.0 collective-permute-done.12.relayed_ref
  20.5 0.9 %shard_map.149.y_ref = f32[64,3072]{1,0:T(8,128)S(1)} custom-call(f32[32,256]{1,0:T(8,128)S(1)} %get-tuple-element.25.shift_ref, f32[256,128]{1,0:T(8,128)S(1)} %get-tuple-element.26.total_ref, f32[8,128]{1,0:T(8,128)S(1)} %get-tuple-element.27.skip_ref, bf16[64,640]{1,0:T(8,128)(2,1)S(1)} %copy-done.1, bf16[64,640]{1,0:T(8,128)(2,1)S(1)} %collective-permute-done.2.told1, ...), custom_call_target="tpu_custom_call" | custom-call | tf_op jit(solution)/shard_map/pallas_call | solution.py:395
  21.4 0.8 %collective-permute-done.13.y2_ref = bf16[128,768]{1,0:T(8,128)(2,1)S(1)} collective-permute-done((bf16[128,768]{1,0:T(8,128)(2,1)S(1)}, bf16[128,768]{1,0:T(8,128)(2,1)S(1)}, u32[]{:S(2)}, u32[]{:S(2)}) %collective-permute-start.13) | collective-permute-done | bytes 196640 | tf_op jit(solution)/shard_map/ppermute | solution.py:334
  22.2 0.5 %collective-permute-start.6 = (bf16[64,512]{1,0:T(8,128)(2,1)S(1)}, bf16[64,512]{1,0:T(8,128)(2,1)S(1)}, u32[]{:S(2)}, u32[]{:S(2)}) collective-permute-start(bf16[64,512]{1,0:T(8,128)(2,1)S(1)} %copy-done.4), channel_id=1, source_target_pairs={{0,1},{1,0},{2,3},{3,2},{4,5},{5,4},{6,7},{7,6},{8,9},{9,8},{10,11... | collective-permute-start | bytes 196616 | tf_op jit(solution)/shard_map/ppermute | solution.py:334
  22.7 0.1 collective-permute-start.5
  23.4 0.0 copy-start.8
  23.5 0.3 %collective-permute-done.6.kv1 = bf16[64,512]{1,0:T(8,128)(2,1)S(1)} collective-permute-done((bf16[64,512]{1,0:T(8,128)(2,1)S(1)}, bf16[64,512]{1,0:T(8,128)(2,1)S(1)}, u32[]{:S(2)}, u32[]{:S(2)}) %collective-permute-start.6) | collective-permute-done | bytes 65568 | tf_op jit(solution)/shard_map/ppermute | solution.py:334
  23.7 0.2 collective-permute-done.5.pages1
  24.0 0.1 copy-done.8
  24.1 0.8 %shard_map.148.attended_ref = bf16[64,1536]{1,0:T(8,128)(2,1)S(1)} custom-call(s32[1,8]{1,0:T(1,128)S(1)} %copy-done.8, s32[1,1]{1,0:T(1,128)} %bitcast.4.length_ref, bf16[64,1536]{1,0:T(8,128)(2,1)S(1)} %copy-done.5, bf16[8,2,8,256]{3,2,1,0:T(8,128)(2,1)S(1)} %constant_dynamic-update-slice_fusion.pages0, ...), custom_call_target="tpu_custom_call" | custom-call | tf_op jit(solution)/shard_map/pallas_call | solution.py:401
  24.9 0.2 copy-done.3
  25.1 1.3 %shard_map.150 = bf16[64,4608]{1,0:T(8,128)(2,1)} custom-call(bf16[64,1536]{1,0:T(8,128)(2,1)S(1)} %shard_map.148.attended_ref, bf16[64,3072]{1,0:T(8,128)(2,1)S(1)} %copy-done.3, f32[1,3072]{1,0:T(1,128)S(1)} %bitcast.5, f32[64,3072]{1,0:T(8,128)S(1)} %shard_map.149.y_ref, bf16[128,768]{1,0:T(8,128)(2,1)S(1)} %collective-permute-done.13.y2_ref, ...), custom_call_target="tpu_custom_call" | custom-call | tf_op jit(solution)/shard_map/pallas_call | solution.py:405
  (31 shorter events, 0.1 us)
Async XLA Ops:
  0.0 5.6 %collective-permute-start = (bf16[8,8,256]{2,1,0:T(8,128)(2,1)}, bf16[8,8,256]{2,1,0:T(8,128)(2,1)S(1)}, u32[]{:S(2)}, u32[]{:S(2)}) collective-permute-start(bf16[8,8,256]{2,1,0:T(8,128)(2,1)} %pool_ref.1), channel_id=1, source_target_pairs={{0,2},{1,3},{2,0},{3,1},{4,6},{5,7},{6,4},{7,5},{8,10},{9,11},{10,... | collective-permute-start | bytes 98312 | tf_op jit(solution)/shard_map/ppermute | solution.py:334
  2.9 11.1 %collective-permute-start.10 = (bf16[64,3072]{1,0:T(8,128)(2,1)}, bf16[64,3072]{1,0:T(8,128)(2,1)S(1)}, u32[]{:S(2)}, u32[]{:S(2)}) collective-permute-start(bf16[64,3072]{1,0:T(8,128)(2,1)} %x0_ref.3), channel_id=1, source_target_pairs={{0,1},{1,0},{2,3},{3,2},{4,5},{5,4},{6,7},{7,6},{8,9},{9,8},{10,11... | collective-permute-start | bytes 1179656 | tf_op jit(solution)/shard_map/ppermute | solution.py:334
  2.9 2.6 %copy-start.6 = (bf16[8,8,256]{2,1,0:T(8,128)(2,1)S(1)}, bf16[8,8,256]{2,1,0:T(8,128)(2,1)}, u32[]{:S(2)}) copy-start(bf16[8,8,256]{2,1,0:T(8,128)(2,1)} %pool_ref.1) | copy-start | bytes 98308
  2.9 11.1 %copy-start = (bf16[64,3072]{1,0:T(8,128)(2,1)S(1)}, bf16[64,3072]{1,0:T(8,128)(2,1)}, u32[]{:S(2)}) copy-start(bf16[64,3072]{1,0:T(8,128)(2,1)} %x0_ref.3) | copy-start | bytes 1179652
  5.0 4.9 %collective-permute-start.2 = (bf16[64,640]{1,0:T(8,128)(2,1)}, bf16[64,640]{1,0:T(8,128)(2,1)S(1)}, u32[]{:S(2)}, u32[]{:S(2)}) collective-permute-start(bf16[64,640]{1,0:T(8,128)(2,1)} %get-tuple-element.19.told0), channel_id=1, source_target_pairs={{0,1},{1,0},{2,3},{3,2},{4,5},{5,4},{6,7},{7,6},{8,9},{9,8},{10,11... | collective-permute-start | bytes 245768 | tf_op jit(solution)/shard_map/ppermute | solution.py:334
  5.5 4.3 %collective-permute-start.8 = (bf16[64,384]{1,0:T(8,128)(2,1)}, bf16[64,384]{1,0:T(8,128)(2,1)S(1)}, u32[]{:S(2)}, u32[]{:S(2)}) collective-permute-start(bf16[64,384]{1,0:T(8,128)(2,1)} %get-tuple-element.22), channel_id=1, source_target_pairs={{0,2},{1,3},{2,0},{3,1},{4,6},{5,7},{6,4},{7,5},{8,10},{9,11},{10,... | collective-permute-start | bytes 147464 | tf_op jit(solution)/shard_map/ppermute | solution.py:334
  5.5 8.6 %collective-permute-start.11 = (bf16[1,6,128,256]{3,2,1,0:T(8,128)(2,1)}, bf16[1,6,128,256]{3,2,1,0:T(8,128)(2,1)S(1)}, u32[]{:S(2)}, u32[]{:S(2)}) collective-permute-start(bf16[1,6,128,256]{3,2,1,0:T(8,128)(2,1)} %prior0_ref.1), channel_id=1, source_target_pairs={{0,1},{1,0},{2,3},{3,2},{4,5},{5,4},{6,7},{7,6},{8,9},{9,8},{10,11... | collective-permute-start | bytes 1179656 | tf_op jit(solution)/shard_map/ppermute | solution.py:334
  5.6 4.2 %collective-permute-start.1 = (bf16[4,2,8,256]{3,2,1,0:T(8,128)(2,1)S(1)}, bf16[4,2,8,256]{3,2,1,0:T(8,128)(2,1)S(1)}, u32[]{:S(2)}, u32[]{:S(2)}) collective-permute-start(bf16[4,2,8,256]{3,2,1,0:T(8,128)(2,1)S(1)} %get-tuple-element.18), channel_id=1, source_target_pairs={{0,4},{4,0},{8,12},{12,8},{16,20},{20,16},{24,28},{28,24},{1,5},{5... | collective-permute-start | bytes 98312 | tf_op jit(solution)/shard_map/ppermute | solution.py:384
  7.7 6.4 %copy-start.1 = (bf16[64,640]{1,0:T(8,128)(2,1)S(1)}, bf16[64,640]{1,0:T(8,128)(2,1)}, u32[]{:S(2)}) copy-start(bf16[64,640]{1,0:T(8,128)(2,1)} %get-tuple-element.19.told0) | copy-start | bytes 245764
  9.8 8.0 %collective-permute-start.7 = (bf16[64,2304]{1,0:T(8,128)(2,1)}, bf16[64,2304]{1,0:T(8,128)(2,1)S(1)}, u32[]{:S(2)}, u32[]{:S(2)}) collective-permute-start(bf16[64,2304]{1,0:T(8,128)(2,1)} %get-tuple-element.21), channel_id=1, source_target_pairs={{0,2},{1,3},{2,0},{3,1},{4,6},{5,7},{6,4},{7,5},{8,10},{9,11},{10,... | collective-permute-start | bytes 884744 | tf_op jit(solution)/shard_map/ppermute | solution.py:334
  9.8 4.3 %collective-permute-start.9 = (bf16[64,384]{1,0:T(8,128)(2,1)S(1)}, bf16[64,384]{1,0:T(8,128)(2,1)S(1)}, u32[]{:S(2)}, u32[]{:S(2)}) collective-permute-start(bf16[64,384]{1,0:T(8,128)(2,1)S(1)} %collective-permute-done.8.ahead2.told2), channel_id=1, source_target_pairs={{0,1},{1,0},{2,3},{3,2},{4,5},{5,4},{6,7},{7,6},{8,9},{9,8},{10,11... | collective-permute-start | bytes 147464 | tf_op jit(solution)/shard_map/ppermute | solution.py:334
  9.9 4.2 %collective-permute-start.3 = (bf16[4,2,8,256]{3,2,1,0:T(8,128)(2,1)S(1)}, bf16[4,2,8,256]{3,2,1,0:T(8,128)(2,1)S(1)}, u32[]{:S(2)}, u32[]{:S(2)}) collective-permute-start(bf16[4,2,8,256]{3,2,1,0:T(8,128)(2,1)S(1)} %pad_maximum_fusion), channel_id=1, source_target_pairs={{0,8},{4,12},{8,0},{12,4},{16,24},{20,28},{24,16},{28,20},{1,9},{5... | collective-permute-start | bytes 98312 | tf_op jit(solution)/shard_map/ppermute | solution.py:384
  14.1 6.4 %copy-start.2 = (bf16[1,6,128,256]{3,2,1,0:T(8,128)(2,1)S(1)}, bf16[1,6,128,256]{3,2,1,0:T(8,128)(2,1)}, u32[]{:S(2)}) copy-start(bf16[1,6,128,256]{3,2,1,0:T(8,128)(2,1)} %prior0_ref.1) | copy-start | bytes 1179652
  15.4 6.8 %collective-permute-start.13 = (bf16[128,768]{1,0:T(8,128)(2,1)S(1)}, bf16[128,768]{1,0:T(8,128)(2,1)S(1)}, u32[]{:S(2)}, u32[]{:S(2)}) collective-permute-start(bf16[128,768]{1,0:T(8,128)(2,1)S(1)} %get-tuple-element.23), channel_id=1, source_target_pairs={{0,2},{1,3},{2,0},{3,1},{4,6},{5,7},{6,4},{7,5},{8,10},{9,11},{10,... | collective-permute-start | bytes 589832 | tf_op jit(solution)/shard_map/ppermute | solution.py:334
  17.8 2.7 %collective-permute-start.12 = (bf16[64,2304]{1,0:T(8,128)(2,1)S(1)}, bf16[64,2304]{1,0:T(8,128)(2,1)S(1)}, u32[]{:S(2)}, u32[]{:S(2)}) collective-permute-start(bf16[64,2304]{1,0:T(8,128)(2,1)S(1)} %collective-permute-done.7.far_ref), channel_id=1, source_target_pairs={{0,1},{1,0},{2,3},{3,2},{4,5},{5,4},{6,7},{7,6},{8,9},{9,8},{10,11... | collective-permute-start | bytes 884744 | tf_op jit(solution)/shard_map/ppermute | solution.py:334
  17.8 4.9 %collective-permute-start.4 = (bf16[4,2,8,256]{3,2,1,0:T(8,128)(2,1)S(1)}, bf16[4,2,8,256]{3,2,1,0:T(8,128)(2,1)S(1)}, u32[]{:S(2)}, u32[]{:S(2)}) collective-permute-start(bf16[4,2,8,256]{3,2,1,0:T(8,128)(2,1)S(1)} %pad_maximum_fusion.1), channel_id=1, source_target_pairs={{0,16},{4,20},{8,24},{12,28},{16,0},{20,4},{24,8},{28,12},{1,17},{... | collective-permute-start | bytes 98312 | tf_op jit(solution)/shard_map/ppermute | solution.py:384
  20.5 1.7 %copy-start.4 = (bf16[64,512]{1,0:T(8,128)(2,1)S(1)}, bf16[64,512]{1,0:T(8,128)(2,1)}, u32[]{:S(2)}) copy-start(bf16[64,512]{1,0:T(8,128)(2,1)} %kv0.1) | copy-start | bytes 196612
  20.5 3.5 %copy-start.5 = (bf16[64,1536]{1,0:T(8,128)(2,1)S(1)}, bf16[64,1536]{1,0:T(8,128)(2,1)}, u32[]{:S(2)}) copy-start(bf16[64,1536]{1,0:T(8,128)(2,1)} %query_ref.1) | copy-start | bytes 589828
  22.2 2.7 %collective-permute-start.14 = (bf16[128,768]{1,0:T(8,128)(2,1)S(1)}, bf16[128,768]{1,0:T(8,128)(2,1)S(1)}, u32[]{:S(2)}, u32[]{:S(2)}) collective-permute-start(bf16[128,768]{1,0:T(8,128)(2,1)S(1)} %collective-permute-done.13.y2_ref), channel_id=1, source_target_pairs={{0,1},{1,0},{2,3},{3,2},{4,5},{5,4},{6,7},{7,6},{8,9},{9,8},{10,11... | collective-permute-start | bytes 589832 | tf_op jit(solution)/shard_map/ppermute | solution.py:334
  22.2 1.5 %collective-permute-start.6 = (bf16[64,512]{1,0:T(8,128)(2,1)S(1)}, bf16[64,512]{1,0:T(8,128)(2,1)S(1)}, u32[]{:S(2)}, u32[]{:S(2)}) collective-permute-start(bf16[64,512]{1,0:T(8,128)(2,1)S(1)} %copy-done.4), channel_id=1, source_target_pairs={{0,1},{1,0},{2,3},{3,2},{4,5},{5,4},{6,7},{7,6},{8,9},{9,8},{10,11... | collective-permute-start | bytes 196616 | tf_op jit(solution)/shard_map/ppermute | solution.py:334
  22.7 1.3 %collective-permute-start.5 = (bf16[8,2,8,256]{3,2,1,0:T(8,128)(2,1)S(1)}, bf16[8,2,8,256]{3,2,1,0:T(8,128)(2,1)S(1)}, u32[]{:S(2)}, u32[]{:S(2)}) collective-permute-start(bf16[8,2,8,256]{3,2,1,0:T(8,128)(2,1)S(1)} %constant_dynamic-update-slice_fusion.pages0), channel_id=1, source_target_pairs={{0,1},{1,0},{2,3},{3,2},{4,5},{5,4},{6,7},{7,6},{8,9},{9,8},{10,11... | collective-permute-start | bytes 196616 | tf_op jit(solution)/shard_map/ppermute | solution.py:334
  23.4 0.7 %copy-start.8 = (s32[1,8]{1,0:T(1,128)S(1)}, s32[1,8]{1,0:T(1,128)}, u32[]{:S(2)}) copy-start(s32[1,8]{1,0:T(1,128)} %page_map_ref.1) | copy-start | bytes 100
  24.1 1.0 %copy-start.3 = (bf16[64,3072]{1,0:T(8,128)(2,1)S(1)}, bf16[64,3072]{1,0:T(8,128)(2,1)}, u32[]{:S(2)}) copy-start(bf16[64,3072]{1,0:T(8,128)(2,1)} %gate_ref.1) | copy-start | bytes 1179652
  24.1 1.0 %copy-start.7 = (f32[3072]{0:T(1024)S(1)}, f32[3072]{0:T(1024)}, u32[]{:S(2)}) copy-start(f32[3072]{0:T(1024)} %param.29) | copy-start | bytes 36868

commit v5 on v4

--- a/solution.py
+++ b/solution.py
@@ -16,12 +16,15 @@
 PAGE = 16
 LANES = 128
 EPSILON = 1e-05
+SCAN_COST = 3 * 10**8
+ATTEND_COST = 10**9
+PACK_COST = 3 * 10**9
+ORDER_COST = 3 * 10**8
 BF16 = jnp.bfloat16
 F32 = jnp.float32
 HIGHEST = lax.Precision.HIGHEST
 VMEM = pl.BlockSpec(memory_space=pltpu.VMEM)
 SMEM = pl.BlockSpec(memory_space=pltpu.SMEM)
-ANY = pl.BlockSpec(memory_space=pl.ANY)
 NOTES = slice(STATE, STATE + LANES)
 AHEAD = STATE + LANES
 IN_MAP = slice(AHEAD, AHEAD + STATE)
@@ -32,9 +35,11 @@
 ALL_HEADS = 24
 
 
-def call(kernel, outs, specs, scratch=(), limit=24):
+def call(kernel, outs, specs, scratch=(), limit=24, flops=0):
+    cost = pl.CostEstimate(flops=flops, bytes_accessed=0, transcendentals=0) if flops else None
     return pl.pallas_call(
         kernel,
+        cost_estimate=cost,
         out_shape=[jax.ShapeDtypeStruct(shape, dtype) for shape, dtype in outs],
         in_specs=specs,
         out_specs=[VMEM] * len(outs),
@@ -355,12 +360,13 @@
     width = MI // 4
     slots, half = cache_pool.shape[0], cache_pool.shape[1]
     far_pool = hopped(cache_pool, 2)
-    pages, sent = call(order_kernel, [((slots // 2, 2, half, 2 * HD), BF16)] * 2, [VMEM] * 2)(cache_pool, far_pool)
+    pages, sent = call(order_kernel, [((slots // 2, 2, half, 2 * HD), BF16)] * 2, [VMEM] * 2, flops=ORDER_COST)(cache_pool, far_pool)
     told, ahead, far = call(
         pack_kernel,
         [((rows, TOLD), BF16), ((rows, AHEAD), BF16), ((rows, 2 * width + STATE + KEYVALS), BF16)],
         [SMEM] * 3 + [VMEM] * 5,
         limit=60,
+        flops=PACK_COST,
     )(
         decay_log, step_bias, skip_gain,
         ssm_input, state_maps, step_logit.T, slot_mask.reshape(1, rows), fresh_keyvals,
@@ -389,6 +395,7 @@
         remote_kernel,
         [((2 * rows, width), BF16), ((32, 4 * rows), F32), ((4 * rows, LANES), F32), ((8, LANES), F32)],
         [VMEM] * 7,
+        flops=SCAN_COST,
     )(told, told1, ahead2, ahead3, ssm_input, x1, prior1)
     relayed = hopped(behind(far, y2), 1)
     y2 = hopped(y2, 2)
@@ -398,7 +405,7 @@
     y3 = hopped(behind(y2, y), 1)
     pages = jnp.concatenate(parts)
     pages1 = hopped(pages, 1)
-    (attended,) = call(attention_kernel, [((rows, QH * HD), BF16)], [VMEM] * 13)(
+    (attended,) = call(attention_kernel, [((rows, QH * HD), BF16)], [VMEM] * 13, flops=ATTEND_COST)(
         page_map, cached_lengths.reshape(1, 1), queries, pages, pages1,
         fresh_keyvals, kv1, far, relayed, told, told1, ahead2, ahead3,
     )

time: 26.6 us -> 26.3 us (0.989)
  starting transfers between devices: 12.6 us -> 12 us
  waiting for transfers between devices: 6.27 us -> 6.69 us
    ppermute x3, waiting for transfers between devices: 2.05 us -> 2.77 us  [local(): came = lax.ppermute(sent, 'dp', [(i, i ^ bit) for i in range(slots)])]
    ppermute x3, starting transfers between devices: 6.88 us -> 6.34 us  [local(): came = lax.ppermute(sent, 'dp', [(i, i ^ bit) for i in range(slots)])]
    ppermute x12, waiting for transfers between devices: 4.22 us -> 3.93 us  [hopped(): return lax.ppermute(block, 'head', [(i, i ^ hop) for i in range(4)])]
where the time goes in v5:
time: 26.3 us; the launch traced here: 26.1 us
  starting transfers between devices  12 us (46%)
  waiting for transfers between devices  6.69 us (25%)
  Pallas kernels  6.28 us (24%)
  between operations  0.79 us (3%)
  local copies, waits for them, and re-layouts  0.33 us (1%)
    ppermute x3, starting transfers between devices, local(): came = lax.ppermute(sent, 'dp', [(i, i ^ bit) for i in range(slots)])  6.34 us
    ppermute x12, starting transfers between devices, hopped(): return lax.ppermute(block, 'head', [(i, i ^ hop) for i in range(4)])  5.64 us
    ppermute x12, waiting for transfers between devices, hopped(): return lax.ppermute(block, 'head', [(i, i ^ hop) for i in range(4)])  3.93 us
    ppermute x3, waiting for transfers between devices, local(): came = lax.ppermute(sent, 'dp', [(i, i ^ bit) for i in range(slots)])  2.77 us
    pallas_call x1, Pallas kernels, local(): call(pack_kernel, [((rows, TOLD), BF16), ((rows, AHEAD), BF16), ((rows, 2...  2.05 us
    pallas_call x1, Pallas kernels, local(): call(final_kernel, [((rows, QH * HD + MI), BF16)], [VMEM] * 6, [pltpu.VME...  1.3 us
    pallas_call x1, Pallas kernels, local(): call(remote_kernel, [((2 * rows, width), BF16), ((32, 4 * rows), F32), ((...  1.28 us
    pallas_call x1, Pallas kernels, local(): call(near_kernel, [((rows, MI), F32)], [VMEM] * 11)  0.9 us
  transfers between devices with their start and end apart: 15, of which 6 were waited for; matrix products, arithmetic and copies ran while one was open for 0% of the time, Pallas kernels for 19%

profile of v5, /device:TPU:0, one launch (start us, length us, event | category | flops | bytes accessed | tf_op | source)
XLA Modules:
  0.0 26.1 jit_solution(16038727865103343477)
XLA Ops:
  0.0 0.5 %collective-permute-start.10 = (bf16[64,3072]{1,0:T(8,128)(2,1)}, bf16[64,3072]{1,0:T(8,128)(2,1)S(1)}, u32[]{:S(2)}, u32[]{:S(2)}) collective-permute-start(bf16[64,3072]{1,0:T(8,128)(2,1)} %x0_ref.3), channel_id=1, source_target_pairs={{0,1},{1,0},{2,3},{3,2},{4,5},{5,4},{6,7},{7,6},{8,9},{9,8},{10,11... | collective-permute-start | bytes 1179656 | tf_op jit(solution)/shard_map/ppermute | solution.py:339
  0.5 2.5 %collective-permute-start = (bf16[8,8,256]{2,1,0:T(8,128)(2,1)}, bf16[8,8,256]{2,1,0:T(8,128)(2,1)S(1)}, u32[]{:S(2)}, u32[]{:S(2)}) collective-permute-start(bf16[8,8,256]{2,1,0:T(8,128)(2,1)} %pool_ref.1), channel_id=1, source_target_pairs={{0,2},{1,3},{2,0},{3,1},{4,6},{5,7},{6,4},{7,5},{8,10},{9,11},{10,... | collective-permute-start | bytes 98312 | tf_op jit(solution)/shard_map/ppermute | solution.py:339
  2.9 2.0 %shard_map.146 = (bf16[64,640]{1,0:T(8,128)(2,1)}, bf16[64,384]{1,0:T(8,128)(2,1)}, bf16[64,2304]{1,0:T(8,128)(2,1)}) custom-call(f32[6]{0:T(128)} %log_rate_ref.1, f32[6]{0:T(128)} %bias_ref.1, f32[6]{0:T(128)} %skip_ref.1, bf16[64,3072]{1,0:T(8,128)(2,1)} %x0_ref.3, bf16[64,512]{1,0:T(8,128)(2,1)} %maps_ref.1, bf16[24,64]{1,0:T(8,128)(2,1)} %bitcast.6, ...), custom_call_target="tpu_custom_call" | custom-call | flops 3000000000 | tf_op jit(solution)/shard_map/pallas_call | solution.py:364
  5.0 0.2 collective-permute-start.2
  5.2 0.3 %collective-permute-start.8 = (bf16[64,384]{1,0:T(8,128)(2,1)}, bf16[64,384]{1,0:T(8,128)(2,1)S(1)}, u32[]{:S(2)}, u32[]{:S(2)}) collective-permute-start(bf16[64,384]{1,0:T(8,128)(2,1)} %get-tuple-element.22), channel_id=1, source_target_pairs={{0,2},{1,3},{2,0},{3,1},{4,6},{5,7},{6,4},{7,5},{8,10},{9,11},{10,... | collective-permute-start | bytes 147464 | tf_op jit(solution)/shard_map/ppermute | solution.py:339
  5.5 0.1 collective-permute-start.11
  5.6 0.0 collective-permute-done.far_pool_ref
  5.6 1.8 %collective-permute-start.1 = (bf16[4,2,8,256]{3,2,1,0:T(8,128)(2,1)S(1)}, bf16[4,2,8,256]{3,2,1,0:T(8,128)(2,1)S(1)}, u32[]{:S(2)}, u32[]{:S(2)}) collective-permute-start(bf16[4,2,8,256]{3,2,1,0:T(8,128)(2,1)S(1)} %get-tuple-element.18), channel_id=1, source_target_pairs={{0,4},{4,0},{8,12},{12,8},{16,20},{20,16},{24,28},{28,24},{1,5},{5... | collective-permute-start | bytes 98312 | tf_op jit(solution)/shard_map/ppermute | solution.py:390
  7.4 2.1 %collective-permute-done.8.ahead2.told2 = bf16[64,384]{1,0:T(8,128)(2,1)S(1)} collective-permute-done((bf16[64,384]{1,0:T(8,128)(2,1)}, bf16[64,384]{1,0:T(8,128)(2,1)S(1)}, u32[]{:S(2)}, u32[]{:S(2)}) %collective-permute-start.8) | collective-permute-done | bytes 49184 | tf_op jit(solution)/shard_map/ppermute | solution.py:339
  9.5 0.3 %collective-permute-start.7 = (bf16[64,2304]{1,0:T(8,128)(2,1)S(1)}, bf16[64,2304]{1,0:T(8,128)(2,1)S(1)}, u32[]{:S(2)}, u32[]{:S(2)}) collective-permute-start(bf16[64,2304]{1,0:T(8,128)(2,1)S(1)} %copy-done.9), channel_id=1, source_target_pairs={{0,2},{1,3},{2,0},{3,1},{4,6},{5,7},{6,4},{7,5},{8,10},{9,11},{10,... | collective-permute-start | bytes 884744 | tf_op jit(solution)/shard_map/ppermute | solution.py:339
  9.8 0.0 collective-permute-done.1
  9.8 0.0 collective-permute-done.2.told1
  9.8 1.9 %collective-permute-start.3 = (bf16[4,2,8,256]{3,2,1,0:T(8,128)(2,1)S(1)}, bf16[4,2,8,256]{3,2,1,0:T(8,128)(2,1)S(1)}, u32[]{:S(2)}, u32[]{:S(2)}) collective-permute-start(bf16[4,2,8,256]{3,2,1,0:T(8,128)(2,1)S(1)} %pad_maximum_fusion), channel_id=1, source_target_pairs={{0,8},{4,12},{8,0},{12,4},{16,24},{20,28},{24,16},{28,20},{1,9},{5... | collective-permute-start | bytes 98312 | tf_op jit(solution)/shard_map/ppermute | solution.py:390
  11.7 2.1 %collective-permute-done.3 = bf16[4,2,8,256]{3,2,1,0:T(8,128)(2,1)S(1)} collective-permute-done((bf16[4,2,8,256]{3,2,1,0:T(8,128)(2,1)S(1)}, bf16[4,2,8,256]{3,2,1,0:T(8,128)(2,1)S(1)}, u32[]{:S(2)}, u32[]{:S(2)}) %collective-permute-start.3) | collective-permute-done | bytes 32800 | tf_op jit(solution)/shard_map/ppermute | solution.py:390
  13.8 0.0 collective-permute-done.9.ahead3.told3
  13.8 0.0 collective-permute-done.10.x1_ref
  13.9 1.3 %shard_map.147 = (bf16[128,768]{1,0:T(8,128)(2,1)S(1)}, f32[32,256]{1,0:T(8,128)S(1)}, f32[256,128]{1,0:T(8,128)S(1)}, f32[8,128]{1,0:T(8,128)S(1)}) custom-call(bf16[64,640]{1,0:T(8,128)(2,1)S(1)} %copy-done.3, bf16[64,640]{1,0:T(8,128)(2,1)S(1)} %collective-permute-done.2.told1, bf16[64,384]{1,0:T(8,128)(2,1)S(1)} %collective-permute-done.8.ahead2.told2, ...), custom_call_target="tpu_custom_call" | custom-call | flops 300000000 | tf_op jit(solution)/shard_map/pallas_call | solution.py:394
  15.2 0.0 copy-start.6
  15.2 1.6 %collective-permute-start.13 = (bf16[128,768]{1,0:T(8,128)(2,1)S(1)}, bf16[128,768]{1,0:T(8,128)(2,1)S(1)}, u32[]{:S(2)}, u32[]{:S(2)}) collective-permute-start(bf16[128,768]{1,0:T(8,128)(2,1)S(1)} %get-tuple-element.23), channel_id=1, source_target_pairs={{0,2},{1,3},{2,0},{3,1},{4,6},{5,7},{6,4},{7,5},{8,10},{9,11},{10,... | collective-permute-start | bytes 589832 | tf_op jit(solution)/shard_map/ppermute | solution.py:339
  16.8 0.8 %collective-permute-done.7.far_ref = bf16[64,2304]{1,0:T(8,128)(2,1)S(1)} collective-permute-done((bf16[64,2304]{1,0:T(8,128)(2,1)S(1)}, bf16[64,2304]{1,0:T(8,128)(2,1)S(1)}, u32[]{:S(2)}, u32[]{:S(2)}) %collective-permute-start.7) | collective-permute-done | bytes 294944 | tf_op jit(solution)/shard_map/ppermute | solution.py:339
  17.6 2.7 %collective-permute-start.4 = (bf16[4,2,8,256]{3,2,1,0:T(8,128)(2,1)S(1)}, bf16[4,2,8,256]{3,2,1,0:T(8,128)(2,1)S(1)}, u32[]{:S(2)}, u32[]{:S(2)}) collective-permute-start(bf16[4,2,8,256]{3,2,1,0:T(8,128)(2,1)S(1)} %pad_maximum_fusion.1), channel_id=1, source_target_pairs={{0,16},{4,20},{8,24},{12,28},{16,0},{20,4},{24,8},{28,12},{1,17},{... | collective-permute-start | bytes 98312 | tf_op jit(solution)/shard_map/ppermute | solution.py:390
  20.3 0.2 collective-permute-start.6
  20.5 0.9 %shard_map.149.y_ref = f32[64,3072]{1,0:T(8,128)S(1)} custom-call(f32[32,256]{1,0:T(8,128)S(1)} %get-tuple-element.25.shift_ref, f32[256,128]{1,0:T(8,128)S(1)} %get-tuple-element.26.total_ref, f32[8,128]{1,0:T(8,128)S(1)} %get-tuple-element.27.skip_ref, bf16[64,640]{1,0:T(8,128)(2,1)S(1)} %copy-done.3, bf16[64,640]{1,0:T(8,128)(2,1)S(1)} %collective-permute-done.2.told1, ...), custom_call_target="tpu_custom_call" | custom-call | tf_op jit(solution)/shard_map/pallas_call | solution.py:402
  21.4 0.4 %collective-permute-done.13.y2_ref = bf16[128,768]{1,0:T(8,128)(2,1)S(1)} collective-permute-done((bf16[128,768]{1,0:T(8,128)(2,1)S(1)}, bf16[128,768]{1,0:T(8,128)(2,1)S(1)}, u32[]{:S(2)}, u32[]{:S(2)}) %collective-permute-start.13) | collective-permute-done | bytes 196640 | tf_op jit(solution)/shard_map/ppermute | solution.py:339
  21.8 0.0 collective-permute-start.14
  21.8 0.7 %collective-permute-done.4 = bf16[4,2,8,256]{3,2,1,0:T(8,128)(2,1)S(1)} collective-permute-done((bf16[4,2,8,256]{3,2,1,0:T(8,128)(2,1)S(1)}, bf16[4,2,8,256]{3,2,1,0:T(8,128)(2,1)S(1)}, u32[]{:S(2)}, u32[]{:S(2)}) %collective-permute-start.4) | collective-permute-done | bytes 32800 | tf_op jit(solution)/shard_map/ppermute | solution.py:390
  23.1 0.0 copy-start.8
  23.2 0.6 %collective-permute-done.5.pages1 = bf16[8,2,8,256]{3,2,1,0:T(8,128)(2,1)S(1)} collective-permute-done((bf16[8,2,8,256]{3,2,1,0:T(8,128)(2,1)S(1)}, bf16[8,2,8,256]{3,2,1,0:T(8,128)(2,1)S(1)}, u32[]{:S(2)}, u32[]{:S(2)}) %collective-permute-start.5) | collective-permute-done | bytes 65568 | tf_op jit(solution)/shard_map/ppermute | solution.py:339
  23.7 0.1 copy-done.8
  23.8 0.8 %shard_map.148.attended_ref = bf16[64,1536]{1,0:T(8,128)(2,1)S(1)} custom-call(s32[1,8]{1,0:T(1,128)S(1)} %copy-done.8, s32[1,1]{1,0:T(1,128)} %bitcast.4.length_ref, bf16[64,1536]{1,0:T(8,128)(2,1)S(1)} %copy-done.5, bf16[8,2,8,256]{3,2,1,0:T(8,128)(2,1)S(1)} %constant_dynamic-update-slice_fusion.pages0, ...), custom_call_target="tpu_custom_call" | custom-call | flops 1000000000 | tf_op jit(solution)/shard_map/pallas_call | solution.py:408
  24.6 0.2 copy-done.2
  24.8 1.3 %shard_map.150 = bf16[64,4608]{1,0:T(8,128)(2,1)} custom-call(bf16[64,1536]{1,0:T(8,128)(2,1)S(1)} %shard_map.148.attended_ref, bf16[64,3072]{1,0:T(8,128)(2,1)S(1)} %copy-done.2, f32[1,3072]{1,0:T(1,128)S(1)} %bitcast.5, f32[64,3072]{1,0:T(8,128)S(1)} %shard_map.149.y_ref, bf16[128,768]{1,0:T(8,128)(2,1)S(1)} %collective-permute-done.13.y2_ref, ...), custom_call_target="tpu_custom_call" | custom-call | tf_op jit(solution)/shard_map/pallas_call | solution.py:412
  (33 shorter events, 0.1 us)
Async XLA Ops:
  0.0 13.8 %collective-permute-start.10 = (bf16[64,3072]{1,0:T(8,128)(2,1)}, bf16[64,3072]{1,0:T(8,128)(2,1)S(1)}, u32[]{:S(2)}, u32[]{:S(2)}) collective-permute-start(bf16[64,3072]{1,0:T(8,128)(2,1)} %x0_ref.3), channel_id=1, source_target_pairs={{0,1},{1,0},{2,3},{3,2},{4,5},{5,4},{6,7},{7,6},{8,9},{9,8},{10,11... | collective-permute-start | bytes 1179656 | tf_op jit(solution)/shard_map/ppermute | solution.py:339
  0.5 5.1 %collective-permute-start = (bf16[8,8,256]{2,1,0:T(8,128)(2,1)}, bf16[8,8,256]{2,1,0:T(8,128)(2,1)S(1)}, u32[]{:S(2)}, u32[]{:S(2)}) collective-permute-start(bf16[8,8,256]{2,1,0:T(8,128)(2,1)} %pool_ref.1), channel_id=1, source_target_pairs={{0,2},{1,3},{2,0},{3,1},{4,6},{5,7},{6,4},{7,5},{8,10},{9,11},{10,... | collective-permute-start | bytes 98312 | tf_op jit(solution)/shard_map/ppermute | solution.py:339
  2.9 2.6 %copy-start.1 = (bf16[1,6,128,256]{3,2,1,0:T(8,128)(2,1)S(1)}, bf16[1,6,128,256]{3,2,1,0:T(8,128)(2,1)}, u32[]{:S(2)}) copy-start(bf16[1,6,128,256]{3,2,1,0:T(8,128)(2,1)} %prior0_ref.1) | copy-start | bytes 1179652
  2.9 2.6 %copy-start.7 = (bf16[8,8,256]{2,1,0:T(8,128)(2,1)S(1)}, bf16[8,8,256]{2,1,0:T(8,128)(2,1)}, u32[]{:S(2)}) copy-start(bf16[8,8,256]{2,1,0:T(8,128)(2,1)} %pool_ref.1) | copy-start | bytes 98308
  5.0 4.8 %collective-permute-start.2 = (bf16[64,640]{1,0:T(8,128)(2,1)}, bf16[64,640]{1,0:T(8,128)(2,1)S(1)}, u32[]{:S(2)}, u32[]{:S(2)}) collective-permute-start(bf16[64,640]{1,0:T(8,128)(2,1)} %get-tuple-element.19.told0), channel_id=1, source_target_pairs={{0,1},{1,0},{2,3},{3,2},{4,5},{5,4},{6,7},{7,6},{8,9},{9,8},{10,11... | collective-permute-start | bytes 245768 | tf_op jit(solution)/shard_map/ppermute | solution.py:339
  5.2 4.3 %copy-start.9 = (bf16[64,2304]{1,0:T(8,128)(2,1)S(1)}, bf16[64,2304]{1,0:T(8,128)(2,1)}, u32[]{:S(2)}) copy-start(bf16[64,2304]{1,0:T(8,128)(2,1)} %get-tuple-element.21) | copy-start | bytes 884740
  5.2 8.6 %copy-start = (bf16[64,3072]{1,0:T(8,128)(2,1)S(1)}, bf16[64,3072]{1,0:T(8,128)(2,1)}, u32[]{:S(2)}) copy-start(bf16[64,3072]{1,0:T(8,128)(2,1)} %x0_ref.3) | copy-start | bytes 1179652
  5.2 4.3 %collective-permute-start.8 = (bf16[64,384]{1,0:T(8,128)(2,1)}, bf16[64,384]{1,0:T(8,128)(2,1)S(1)}, u32[]{:S(2)}, u32[]{:S(2)}) collective-permute-start(bf16[64,384]{1,0:T(8,128)(2,1)} %get-tuple-element.22), channel_id=1, source_target_pairs={{0,2},{1,3},{2,0},{3,1},{4,6},{5,7},{6,4},{7,5},{8,10},{9,11},{10,... | collective-permute-start | bytes 147464 | tf_op jit(solution)/shard_map/ppermute | solution.py:339
  5.5 8.3 %collective-permute-start.11 = (bf16[1,6,128,256]{3,2,1,0:T(8,128)(2,1)S(1)}, bf16[1,6,128,256]{3,2,1,0:T(8,128)(2,1)S(1)}, u32[]{:S(2)}, u32[]{:S(2)}) collective-permute-start(bf16[1,6,128,256]{3,2,1,0:T(8,128)(2,1)S(1)} %copy-done.1), channel_id=1, source_target_pairs={{0,1},{1,0},{2,3},{3,2},{4,5},{5,4},{6,7},{7,6},{8,9},{9,8},{10,11... | collective-permute-start | bytes 1179656 | tf_op jit(solution)/shard_map/ppermute | solution.py:339
  5.6 4.2 %collective-permute-start.1 = (bf16[4,2,8,256]{3,2,1,0:T(8,128)(2,1)S(1)}, bf16[4,2,8,256]{3,2,1,0:T(8,128)(2,1)S(1)}, u32[]{:S(2)}, u32[]{:S(2)}) collective-permute-start(bf16[4,2,8,256]{3,2,1,0:T(8,128)(2,1)S(1)} %get-tuple-element.18), channel_id=1, source_target_pairs={{0,4},{4,0},{8,12},{12,8},{16,20},{20,16},{24,28},{28,24},{1,5},{5... | collective-permute-start | bytes 98312 | tf_op jit(solution)/shard_map/ppermute | solution.py:390
  7.4 6.5 %copy-start.3 = (bf16[64,640]{1,0:T(8,128)(2,1)S(1)}, bf16[64,640]{1,0:T(8,128)(2,1)}, u32[]{:S(2)}) copy-start(bf16[64,640]{1,0:T(8,128)(2,1)} %get-tuple-element.19.told0) | copy-start | bytes 245764
  9.5 8.0 %collective-permute-start.7 = (bf16[64,2304]{1,0:T(8,128)(2,1)S(1)}, bf16[64,2304]{1,0:T(8,128)(2,1)S(1)}, u32[]{:S(2)}, u32[]{:S(2)}) collective-permute-start(bf16[64,2304]{1,0:T(8,128)(2,1)S(1)} %copy-done.9), channel_id=1, source_target_pairs={{0,2},{1,3},{2,0},{3,1},{4,6},{5,7},{6,4},{7,5},{8,10},{9,11},{10,... | collective-permute-start | bytes 884744 | tf_op jit(solution)/shard_map/ppermute | solution.py:339
  9.8 4.0 %collective-permute-start.9 = (bf16[64,384]{1,0:T(8,128)(2,1)S(1)}, bf16[64,384]{1,0:T(8,128)(2,1)S(1)}, u32[]{:S(2)}, u32[]{:S(2)}) collective-permute-start(bf16[64,384]{1,0:T(8,128)(2,1)S(1)} %collective-permute-done.8.ahead2.told2), channel_id=1, source_target_pairs={{0,1},{1,0},{2,3},{3,2},{4,5},{5,4},{6,7},{7,6},{8,9},{9,8},{10,11... | collective-permute-start | bytes 147464 | tf_op jit(solution)/shard_map/ppermute | solution.py:339
  9.8 4.0 %collective-permute-start.3 = (bf16[4,2,8,256]{3,2,1,0:T(8,128)(2,1)S(1)}, bf16[4,2,8,256]{3,2,1,0:T(8,128)(2,1)S(1)}, u32[]{:S(2)}, u32[]{:S(2)}) collective-permute-start(bf16[4,2,8,256]{3,2,1,0:T(8,128)(2,1)S(1)} %pad_maximum_fusion), channel_id=1, source_target_pairs={{0,8},{4,12},{8,0},{12,4},{16,24},{20,28},{24,16},{28,20},{1,9},{5... | collective-permute-start | bytes 98312 | tf_op jit(solution)/shard_map/ppermute | solution.py:390
  15.2 5.1 %copy-start.6 = (bf16[64,512]{1,0:T(8,128)(2,1)S(1)}, bf16[64,512]{1,0:T(8,128)(2,1)}, u32[]{:S(2)}) copy-start(bf16[64,512]{1,0:T(8,128)(2,1)} %kv0.1) | copy-start | bytes 196612
  15.2 6.6 %collective-permute-start.13 = (bf16[128,768]{1,0:T(8,128)(2,1)S(1)}, bf16[128,768]{1,0:T(8,128)(2,1)S(1)}, u32[]{:S(2)}, u32[]{:S(2)}) collective-permute-start(bf16[128,768]{1,0:T(8,128)(2,1)S(1)} %get-tuple-element.23), channel_id=1, source_target_pairs={{0,2},{1,3},{2,0},{3,1},{4,6},{5,7},{6,4},{7,5},{8,10},{9,11},{10,... | collective-permute-start | bytes 589832 | tf_op jit(solution)/shard_map/ppermute | solution.py:339
  17.6 2.9 %collective-permute-start.12 = (bf16[64,2304]{1,0:T(8,128)(2,1)S(1)}, bf16[64,2304]{1,0:T(8,128)(2,1)S(1)}, u32[]{:S(2)}, u32[]{:S(2)}) collective-permute-start(bf16[64,2304]{1,0:T(8,128)(2,1)S(1)} %collective-permute-done.7.far_ref), channel_id=1, source_target_pairs={{0,1},{1,0},{2,3},{3,2},{4,5},{5,4},{6,7},{7,6},{8,9},{9,8},{10,11... | collective-permute-start | bytes 884744 | tf_op jit(solution)/shard_map/ppermute | solution.py:339
  17.6 4.9 %collective-permute-start.4 = (bf16[4,2,8,256]{3,2,1,0:T(8,128)(2,1)S(1)}, bf16[4,2,8,256]{3,2,1,0:T(8,128)(2,1)S(1)}, u32[]{:S(2)}, u32[]{:S(2)}) collective-permute-start(bf16[4,2,8,256]{3,2,1,0:T(8,128)(2,1)S(1)} %pad_maximum_fusion.1), channel_id=1, source_target_pairs={{0,16},{4,20},{8,24},{12,28},{16,0},{20,4},{24,8},{28,12},{1,17},{... | collective-permute-start | bytes 98312 | tf_op jit(solution)/shard_map/ppermute | solution.py:390
  20.3 2.9 %collective-permute-start.6 = (bf16[64,512]{1,0:T(8,128)(2,1)S(1)}, bf16[64,512]{1,0:T(8,128)(2,1)S(1)}, u32[]{:S(2)}, u32[]{:S(2)}) collective-permute-start(bf16[64,512]{1,0:T(8,128)(2,1)S(1)} %copy-done.6), channel_id=1, source_target_pairs={{0,1},{1,0},{2,3},{3,2},{4,5},{5,4},{6,7},{7,6},{8,9},{9,8},{10,11... | collective-permute-start | bytes 196616 | tf_op jit(solution)/shard_map/ppermute | solution.py:339
  20.5 3.3 %copy-start.5 = (bf16[64,1536]{1,0:T(8,128)(2,1)S(1)}, bf16[64,1536]{1,0:T(8,128)(2,1)}, u32[]{:S(2)}) copy-start(bf16[64,1536]{1,0:T(8,128)(2,1)} %query_ref.1) | copy-start | bytes 589828
  21.8 2.8 %collective-permute-start.14 = (bf16[128,768]{1,0:T(8,128)(2,1)S(1)}, bf16[128,768]{1,0:T(8,128)(2,1)S(1)}, u32[]{:S(2)}, u32[]{:S(2)}) collective-permute-start(bf16[128,768]{1,0:T(8,128)(2,1)S(1)} %collective-permute-done.13.y2_ref), channel_id=1, source_target_pairs={{0,1},{1,0},{2,3},{3,2},{4,5},{5,4},{6,7},{7,6},{8,9},{9,8},{10,11... | collective-permute-start | bytes 589832 | tf_op jit(solution)/shard_map/ppermute | solution.py:339
  22.5 1.3 %collective-permute-start.5 = (bf16[8,2,8,256]{3,2,1,0:T(8,128)(2,1)S(1)}, bf16[8,2,8,256]{3,2,1,0:T(8,128)(2,1)S(1)}, u32[]{:S(2)}, u32[]{:S(2)}) collective-permute-start(bf16[8,2,8,256]{3,2,1,0:T(8,128)(2,1)S(1)} %constant_dynamic-update-slice_fusion.pages0), channel_id=1, source_target_pairs={{0,1},{1,0},{2,3},{3,2},{4,5},{5,4},{6,7},{7,6},{8,9},{9,8},{10,11... | collective-permute-start | bytes 196616 | tf_op jit(solution)/shard_map/ppermute | solution.py:339
  23.1 0.7 %copy-start.8 = (s32[1,8]{1,0:T(1,128)S(1)}, s32[1,8]{1,0:T(1,128)}, u32[]{:S(2)}) copy-start(s32[1,8]{1,0:T(1,128)} %page_map_ref.1) | copy-start | bytes 100
  23.8 1.0 %copy-start.2 = (bf16[64,3072]{1,0:T(8,128)(2,1)S(1)}, bf16[64,3072]{1,0:T(8,128)(2,1)}, u32[]{:S(2)}) copy-start(bf16[64,3072]{1,0:T(8,128)(2,1)} %gate_ref.1) | copy-start | bytes 1179652
  23.8 1.0 %copy-start.4 = (f32[3072]{0:T(1024)S(1)}, f32[3072]{0:T(1024)}, u32[]{:S(2)}) copy-start(f32[3072]{0:T(1024)} %param.29) | copy-start | bytes 36868

commit v6 on v5

--- a/solution.py
+++ b/solution.py
@@ -25,6 +25,7 @@
 HIGHEST = lax.Precision.HIGHEST
 VMEM = pl.BlockSpec(memory_space=pltpu.VMEM)
 SMEM = pl.BlockSpec(memory_space=pltpu.SMEM)
+ANY = pl.BlockSpec(memory_space=pl.ANY)
 NOTES = slice(STATE, STATE + LANES)
 AHEAD = STATE + LANES
 IN_MAP = slice(AHEAD, AHEAD + STATE)
@@ -35,14 +36,14 @@
 ALL_HEADS = 24
 
 
-def call(kernel, outs, specs, scratch=(), limit=24, flops=0):
+def call(kernel, outs, specs, scratch=(), limit=24, flops=0, out_spec=VMEM):
     cost = pl.CostEstimate(flops=flops, bytes_accessed=0, transcendentals=0) if flops else None
     return pl.pallas_call(
         kernel,
         cost_estimate=cost,
         out_shape=[jax.ShapeDtypeStruct(shape, dtype) for shape, dtype in outs],
         in_specs=specs,
-        out_specs=[VMEM] * len(outs),
+        out_specs=[out_spec] * len(outs),
         scratch_shapes=list(scratch),
         compiler_params=pltpu.CompilerParams(vmem_limit_bytes=limit << 20),
     )
@@ -309,11 +310,12 @@
         write(4)
 
 
-def final_kernel(attended_ref, gate_ref, gain_ref, y_ref, y2_ref, y3_ref, out_ref, gated):
+def final_kernel(attended_ref, gate_ref, gain_ref, y_ref, y2_ref, y3_ref, out_ref, gated, normed, sems):
     me = lax.axis_index("head")
     rows, width = y_ref.shape[0], y2_ref.shape[1]
     heads_width = attended_ref.shape[1]
-    out_ref[:, :heads_width] = attended_ref[...]
+    first = pltpu.make_async_copy(attended_ref, out_ref.at[:, pl.ds(0, heads_width)], sems.at[4])
+    first.start()
     squares = jnp.zeros((rows, 1), F32)
     for hop, far in enumerate((None, None, y3_ref[rows:, :], y2_ref[:rows, :])):
         gate = columns(gate_ref, me ^ hop, width).astype(F32)
@@ -324,11 +326,16 @@
         gated[:, hop * width : (hop + 1) * width] = part
         squares = squares + jnp.sum(part * part, axis=1, keepdims=True)
     scale = lax.rsqrt(squares / MI + EPSILON)
+    copies = [first]
     for hop in range(4):
         gain = columns(gain_ref, me ^ hop, width)
-        part = gated[:, hop * width : (hop + 1) * width] * scale * gain
+        normed[hop] = (gated[:, hop * width : (hop + 1) * width] * scale * gain).astype(BF16)
         start = pl.multiple_of(heads_width + (me ^ hop) * width, LANES)
-        out_ref[:, pl.ds(start, width)] = part.astype(BF16)
+        copy = pltpu.make_async_copy(normed.at[hop], out_ref.at[:, pl.ds(start, width)], sems.at[hop])
+        copy.start()
+        copies.append(copy)
+    for copy in copies:
+        copy.wait()
 
 
 def behind(block, earlier):
@@ -413,7 +420,12 @@
         final_kernel,
         [((rows, QH * HD + MI), BF16)],
         [VMEM] * 6,
-        [pltpu.VMEM((rows, MI), F32)],
+        [
+            pltpu.VMEM((rows, MI), F32),
+            pltpu.VMEM((4, rows, width), BF16),
+            pltpu.SemaphoreType.DMA((5,)),
+        ],
+        out_spec=ANY,
     )(attended, gate_input, norm_gain.reshape(1, MI), y, y2, y3)
     return result
 

time: 26.3 us -> 26.3 us (level)
  no operation moved by 1% of the time
where the time goes in v6:
time: 26.3 us; the launch traced here: 26 us
  starting transfers between devices  12 us (46%)
  waiting for transfers between devices  6.69 us (25%)
  Pallas kernels  6.22 us (24%)
  between operations  0.79 us (3%)
  local copies, waits for them, and re-layouts  0.33 us (1%)
    ppermute x3, starting transfers between devices, local(): came = lax.ppermute(sent, 'dp', [(i, i ^ bit) for i in range(slots)])  6.34 us
    ppermute x12, starting transfers between devices, hopped(): return lax.ppermute(block, 'head', [(i, i ^ hop) for i in range(4)])  5.64 us
    ppermute x12, waiting for transfers between devices, hopped(): return lax.ppermute(block, 'head', [(i, i ^ hop) for i in range(4)])  3.93 us
    ppermute x3, waiting for transfers between devices, local(): came = lax.ppermute(sent, 'dp', [(i, i ^ bit) for i in range(slots)])  2.77 us
    pallas_call x1, Pallas kernels, local(): call(pack_kernel, [((rows, TOLD), BF16), ((rows, AHEAD), BF16), ((rows, 2...  2.05 us
    pallas_call x1, Pallas kernels, local(): call(remote_kernel, [((2 * rows, width), BF16), ((32, 4 * rows), F32), ((...  1.28 us
    pallas_call x1, Pallas kernels, local(): call(final_kernel, [((rows, QH * HD + MI), BF16)], [VMEM] * 6, [pltpu.VME...  1.24 us
    pallas_call x1, Pallas kernels, local(): call(near_kernel, [((rows, MI), F32)], [VMEM] * 11)  0.9 us
  transfers between devices with their start and end apart: 15, of which 6 were waited for; matrix products, arithmetic and copies ran while one was open for 0% of the time, Pallas kernels for 19%

profile of v6, /device:TPU:0, one launch (start us, length us, event | category | flops | bytes accessed | tf_op | source)
XLA Modules:
  0.0 26.0 jit_solution(2248751266045797716)
XLA Ops:
  0.0 0.5 %collective-permute-start.10 = (bf16[64,3072]{1,0:T(8,128)(2,1)}, bf16[64,3072]{1,0:T(8,128)(2,1)S(1)}, u32[]{:S(2)}, u32[]{:S(2)}) collective-permute-start(bf16[64,3072]{1,0:T(8,128)(2,1)} %x0_ref.3), channel_id=1, source_target_pairs={{0,1},{1,0},{2,3},{3,2},{4,5},{5,4},{6,7},{7,6},{8,9},{9,8},{10,11... | collective-permute-start | bytes 1179656 | tf_op jit(solution)/shard_map/ppermute | solution.py:346
  0.5 2.5 %collective-permute-start = (bf16[8,8,256]{2,1,0:T(8,128)(2,1)}, bf16[8,8,256]{2,1,0:T(8,128)(2,1)S(1)}, u32[]{:S(2)}, u32[]{:S(2)}) collective-permute-start(bf16[8,8,256]{2,1,0:T(8,128)(2,1)} %pool_ref.1), channel_id=1, source_target_pairs={{0,2},{1,3},{2,0},{3,1},{4,6},{5,7},{6,4},{7,5},{8,10},{9,11},{10,... | collective-permute-start | bytes 98312 | tf_op jit(solution)/shard_map/ppermute | solution.py:346
  2.9 2.0 %shard_map.146 = (bf16[64,640]{1,0:T(8,128)(2,1)}, bf16[64,384]{1,0:T(8,128)(2,1)}, bf16[64,2304]{1,0:T(8,128)(2,1)}) custom-call(f32[6]{0:T(128)} %log_rate_ref.1, f32[6]{0:T(128)} %bias_ref.1, f32[6]{0:T(128)} %skip_ref.1, bf16[64,3072]{1,0:T(8,128)(2,1)} %x0_ref.3, bf16[64,512]{1,0:T(8,128)(2,1)} %maps_ref.1, bf16[24,64]{1,0:T(8,128)(2,1)} %bitcast.6, ...), custom_call_target="tpu_custom_call" | custom-call | flops 3000000000 | tf_op jit(solution)/shard_map/pallas_call | solution.py:371
  5.0 0.2 collective-permute-start.2
  5.2 0.3 %collective-permute-start.8 = (bf16[64,384]{1,0:T(8,128)(2,1)}, bf16[64,384]{1,0:T(8,128)(2,1)S(1)}, u32[]{:S(2)}, u32[]{:S(2)}) collective-permute-start(bf16[64,384]{1,0:T(8,128)(2,1)} %get-tuple-element.22), channel_id=1, source_target_pairs={{0,2},{1,3},{2,0},{3,1},{4,6},{5,7},{6,4},{7,5},{8,10},{9,11},{10,... | collective-permute-start | bytes 147464 | tf_op jit(solution)/shard_map/ppermute | solution.py:346
  5.5 0.1 collective-permute-start.11
  5.6 1.8 %collective-permute-start.1 = (bf16[4,2,8,256]{3,2,1,0:T(8,128)(2,1)S(1)}, bf16[4,2,8,256]{3,2,1,0:T(8,128)(2,1)S(1)}, u32[]{:S(2)}, u32[]{:S(2)}) collective-permute-start(bf16[4,2,8,256]{3,2,1,0:T(8,128)(2,1)S(1)} %get-tuple-element.18), channel_id=1, source_target_pairs={{0,4},{4,0},{8,12},{12,8},{16,20},{20,16},{24,28},{28,24},{1,5},{5... | collective-permute-start | bytes 98312 | tf_op jit(solution)/shard_map/ppermute | solution.py:397
  7.4 2.1 %collective-permute-done.8.ahead2.told2 = bf16[64,384]{1,0:T(8,128)(2,1)S(1)} collective-permute-done((bf16[64,384]{1,0:T(8,128)(2,1)}, bf16[64,384]{1,0:T(8,128)(2,1)S(1)}, u32[]{:S(2)}, u32[]{:S(2)}) %collective-permute-start.8) | collective-permute-done | bytes 49184 | tf_op jit(solution)/shard_map/ppermute | solution.py:346
  9.5 0.3 %collective-permute-start.7 = (bf16[64,2304]{1,0:T(8,128)(2,1)S(1)}, bf16[64,2304]{1,0:T(8,128)(2,1)S(1)}, u32[]{:S(2)}, u32[]{:S(2)}) collective-permute-start(bf16[64,2304]{1,0:T(8,128)(2,1)S(1)} %copy-done.9), channel_id=1, source_target_pairs={{0,2},{1,3},{2,0},{3,1},{4,6},{5,7},{6,4},{7,5},{8,10},{9,11},{10,... | collective-permute-start | bytes 884744 | tf_op jit(solution)/shard_map/ppermute | solution.py:346
  9.8 0.0 collective-permute-done.1
  9.8 0.0 collective-permute-start.9
  9.8 1.9 %collective-permute-start.3 = (bf16[4,2,8,256]{3,2,1,0:T(8,128)(2,1)S(1)}, bf16[4,2,8,256]{3,2,1,0:T(8,128)(2,1)S(1)}, u32[]{:S(2)}, u32[]{:S(2)}) collective-permute-start(bf16[4,2,8,256]{3,2,1,0:T(8,128)(2,1)S(1)} %pad_maximum_fusion), channel_id=1, source_target_pairs={{0,8},{4,12},{8,0},{12,4},{16,24},{20,28},{24,16},{28,20},{1,9},{5... | collective-permute-start | bytes 98312 | tf_op jit(solution)/shard_map/ppermute | solution.py:397
  11.7 2.1 %collective-permute-done.3 = bf16[4,2,8,256]{3,2,1,0:T(8,128)(2,1)S(1)} collective-permute-done((bf16[4,2,8,256]{3,2,1,0:T(8,128)(2,1)S(1)}, bf16[4,2,8,256]{3,2,1,0:T(8,128)(2,1)S(1)}, u32[]{:S(2)}, u32[]{:S(2)}) %collective-permute-start.3) | collective-permute-done | bytes 32800 | tf_op jit(solution)/shard_map/ppermute | solution.py:397
  13.8 0.0 collective-permute-done.11.prior1_ref
  13.9 1.3 %shard_map.147 = (bf16[128,768]{1,0:T(8,128)(2,1)S(1)}, f32[32,256]{1,0:T(8,128)S(1)}, f32[256,128]{1,0:T(8,128)S(1)}, f32[8,128]{1,0:T(8,128)S(1)}) custom-call(bf16[64,640]{1,0:T(8,128)(2,1)S(1)} %copy-done.3, bf16[64,640]{1,0:T(8,128)(2,1)S(1)} %collective-permute-done.2.told1, bf16[64,384]{1,0:T(8,128)(2,1)S(1)} %collective-permute-done.8.ahead2.told2, ...), custom_call_target="tpu_custom_call" | custom-call | flops 300000000 | tf_op jit(solution)/shard_map/pallas_call | solution.py:401
  15.2 0.0 copy-start.6
  15.2 1.6 %collective-permute-start.13 = (bf16[128,768]{1,0:T(8,128)(2,1)S(1)}, bf16[128,768]{1,0:T(8,128)(2,1)S(1)}, u32[]{:S(2)}, u32[]{:S(2)}) collective-permute-start(bf16[128,768]{1,0:T(8,128)(2,1)S(1)} %get-tuple-element.23), channel_id=1, source_target_pairs={{0,2},{1,3},{2,0},{3,1},{4,6},{5,7},{6,4},{7,5},{8,10},{9,11},{10,... | collective-permute-start | bytes 589832 | tf_op jit(solution)/shard_map/ppermute | solution.py:346
  16.8 0.8 %collective-permute-done.7.far_ref = bf16[64,2304]{1,0:T(8,128)(2,1)S(1)} collective-permute-done((bf16[64,2304]{1,0:T(8,128)(2,1)S(1)}, bf16[64,2304]{1,0:T(8,128)(2,1)S(1)}, u32[]{:S(2)}, u32[]{:S(2)}) %collective-permute-start.7) | collective-permute-done | bytes 294944 | tf_op jit(solution)/shard_map/ppermute | solution.py:346
  17.6 0.0 collective-permute-start.12
  17.6 2.7 %collective-permute-start.4 = (bf16[4,2,8,256]{3,2,1,0:T(8,128)(2,1)S(1)}, bf16[4,2,8,256]{3,2,1,0:T(8,128)(2,1)S(1)}, u32[]{:S(2)}, u32[]{:S(2)}) collective-permute-start(bf16[4,2,8,256]{3,2,1,0:T(8,128)(2,1)S(1)} %pad_maximum_fusion.1), channel_id=1, source_target_pairs={{0,16},{4,20},{8,24},{12,28},{16,0},{20,4},{24,8},{28,12},{1,17},{... | collective-permute-start | bytes 98312 | tf_op jit(solution)/shard_map/ppermute | solution.py:397
  20.3 0.2 collective-permute-start.6
  20.5 0.0 collective-permute-done.12.relayed_ref
  20.5 0.9 %shard_map.149.y_ref = f32[64,3072]{1,0:T(8,128)S(1)} custom-call(f32[32,256]{1,0:T(8,128)S(1)} %get-tuple-element.25.shift_ref, f32[256,128]{1,0:T(8,128)S(1)} %get-tuple-element.26.total_ref, f32[8,128]{1,0:T(8,128)S(1)} %get-tuple-element.27.skip_ref, bf16[64,640]{1,0:T(8,128)(2,1)S(1)} %copy-done.3, bf16[64,640]{1,0:T(8,128)(2,1)S(1)} %collective-permute-done.2.told1, ...), custom_call_target="tpu_custom_call" | custom-call | tf_op jit(solution)/shard_map/pallas_call | solution.py:409
  21.4 0.4 %collective-permute-done.13.y2_ref = bf16[128,768]{1,0:T(8,128)(2,1)S(1)} collective-permute-done((bf16[128,768]{1,0:T(8,128)(2,1)S(1)}, bf16[128,768]{1,0:T(8,128)(2,1)S(1)}, u32[]{:S(2)}, u32[]{:S(2)}) %collective-permute-start.13) | collective-permute-done | bytes 196640 | tf_op jit(solution)/shard_map/ppermute | solution.py:346
  21.8 0.0 collective-permute-start.14
  21.8 0.7 %collective-permute-done.4 = bf16[4,2,8,256]{3,2,1,0:T(8,128)(2,1)S(1)} collective-permute-done((bf16[4,2,8,256]{3,2,1,0:T(8,128)(2,1)S(1)}, bf16[4,2,8,256]{3,2,1,0:T(8,128)(2,1)S(1)}, u32[]{:S(2)}, u32[]{:S(2)}) %collective-permute-start.4) | collective-permute-done | bytes 32800 | tf_op jit(solution)/shard_map/ppermute | solution.py:397
  23.1 0.0 copy-start.8
  23.2 0.6 %collective-permute-done.5.pages1 = bf16[8,2,8,256]{3,2,1,0:T(8,128)(2,1)S(1)} collective-permute-done((bf16[8,2,8,256]{3,2,1,0:T(8,128)(2,1)S(1)}, bf16[8,2,8,256]{3,2,1,0:T(8,128)(2,1)S(1)}, u32[]{:S(2)}, u32[]{:S(2)}) %collective-permute-start.5) | collective-permute-done | bytes 65568 | tf_op jit(solution)/shard_map/ppermute | solution.py:346
  23.7 0.1 copy-done.8
  23.8 0.8 %shard_map.148.attended_ref = bf16[64,1536]{1,0:T(8,128)(2,1)S(1)} custom-call(s32[1,8]{1,0:T(1,128)S(1)} %copy-done.8, s32[1,1]{1,0:T(1,128)} %bitcast.4.length_ref, bf16[64,1536]{1,0:T(8,128)(2,1)S(1)} %copy-done.5, bf16[8,2,8,256]{3,2,1,0:T(8,128)(2,1)S(1)} %constant_dynamic-update-slice_fusion.pages0, ...), custom_call_target="tpu_custom_call" | custom-call | flops 1000000000 | tf_op jit(solution)/shard_map/pallas_call | solution.py:415
  24.6 0.2 copy-done.2
  24.8 1.2 %shard_map.150 = bf16[64,4608]{1,0:T(8,128)(2,1)} custom-call(bf16[64,1536]{1,0:T(8,128)(2,1)S(1)} %shard_map.148.attended_ref, bf16[64,3072]{1,0:T(8,128)(2,1)S(1)} %copy-done.2, f32[1,3072]{1,0:T(1,128)S(1)} %bitcast.5, f32[64,3072]{1,0:T(8,128)S(1)} %shard_map.149.y_ref, bf16[128,768]{1,0:T(8,128)(2,1)S(1)} %collective-permute-done.13.y2_ref, ...), custom_call_target="tpu_custom_call" | custom-call | tf_op jit(solution)/shard_map/pallas_call | solution.py:419
  (33 shorter events, 0.1 us)
Async XLA Ops:
  0.0 13.8 %collective-permute-start.10 = (bf16[64,3072]{1,0:T(8,128)(2,1)}, bf16[64,3072]{1,0:T(8,128)(2,1)S(1)}, u32[]{:S(2)}, u32[]{:S(2)}) collective-permute-start(bf16[64,3072]{1,0:T(8,128)(2,1)} %x0_ref.3), channel_id=1, source_target_pairs={{0,1},{1,0},{2,3},{3,2},{4,5},{5,4},{6,7},{7,6},{8,9},{9,8},{10,11... | collective-permute-start | bytes 1179656 | tf_op jit(solution)/shard_map/ppermute | solution.py:346
  0.5 5.1 %collective-permute-start = (bf16[8,8,256]{2,1,0:T(8,128)(2,1)}, bf16[8,8,256]{2,1,0:T(8,128)(2,1)S(1)}, u32[]{:S(2)}, u32[]{:S(2)}) collective-permute-start(bf16[8,8,256]{2,1,0:T(8,128)(2,1)} %pool_ref.1), channel_id=1, source_target_pairs={{0,2},{1,3},{2,0},{3,1},{4,6},{5,7},{6,4},{7,5},{8,10},{9,11},{10,... | collective-permute-start | bytes 98312 | tf_op jit(solution)/shard_map/ppermute | solution.py:346
  2.9 2.6 %copy-start.1 = (bf16[1,6,128,256]{3,2,1,0:T(8,128)(2,1)S(1)}, bf16[1,6,128,256]{3,2,1,0:T(8,128)(2,1)}, u32[]{:S(2)}) copy-start(bf16[1,6,128,256]{3,2,1,0:T(8,128)(2,1)} %prior0_ref.1) | copy-start | bytes 1179652
  2.9 2.6 %copy-start.7 = (bf16[8,8,256]{2,1,0:T(8,128)(2,1)S(1)}, bf16[8,8,256]{2,1,0:T(8,128)(2,1)}, u32[]{:S(2)}) copy-start(bf16[8,8,256]{2,1,0:T(8,128)(2,1)} %pool_ref.1) | copy-start | bytes 98308
  5.0 4.8 %collective-permute-start.2 = (bf16[64,640]{1,0:T(8,128)(2,1)}, bf16[64,640]{1,0:T(8,128)(2,1)S(1)}, u32[]{:S(2)}, u32[]{:S(2)}) collective-permute-start(bf16[64,640]{1,0:T(8,128)(2,1)} %get-tuple-element.19.told0), channel_id=1, source_target_pairs={{0,1},{1,0},{2,3},{3,2},{4,5},{5,4},{6,7},{7,6},{8,9},{9,8},{10,11... | collective-permute-start | bytes 245768 | tf_op jit(solution)/shard_map/ppermute | solution.py:346
  5.2 4.3 %copy-start.9 = (bf16[64,2304]{1,0:T(8,128)(2,1)S(1)}, bf16[64,2304]{1,0:T(8,128)(2,1)}, u32[]{:S(2)}) copy-start(bf16[64,2304]{1,0:T(8,128)(2,1)} %get-tuple-element.21) | copy-start | bytes 884740
  5.2 8.6 %copy-start = (bf16[64,3072]{1,0:T(8,128)(2,1)S(1)}, bf16[64,3072]{1,0:T(8,128)(2,1)}, u32[]{:S(2)}) copy-start(bf16[64,3072]{1,0:T(8,128)(2,1)} %x0_ref.3) | copy-start | bytes 1179652
  5.2 4.3 %collective-permute-start.8 = (bf16[64,384]{1,0:T(8,128)(2,1)}, bf16[64,384]{1,0:T(8,128)(2,1)S(1)}, u32[]{:S(2)}, u32[]{:S(2)}) collective-permute-start(bf16[64,384]{1,0:T(8,128)(2,1)} %get-tuple-element.22), channel_id=1, source_target_pairs={{0,2},{1,3},{2,0},{3,1},{4,6},{5,7},{6,4},{7,5},{8,10},{9,11},{10,... | collective-permute-start | bytes 147464 | tf_op jit(solution)/shard_map/ppermute | solution.py:346
  5.5 8.3 %collective-permute-start.11 = (bf16[1,6,128,256]{3,2,1,0:T(8,128)(2,1)S(1)}, bf16[1,6,128,256]{3,2,1,0:T(8,128)(2,1)S(1)}, u32[]{:S(2)}, u32[]{:S(2)}) collective-permute-start(bf16[1,6,128,256]{3,2,1,0:T(8,128)(2,1)S(1)} %copy-done.1), channel_id=1, source_target_pairs={{0,1},{1,0},{2,3},{3,2},{4,5},{5,4},{6,7},{7,6},{8,9},{9,8},{10,11... | collective-permute-start | bytes 1179656 | tf_op jit(solution)/shard_map/ppermute | solution.py:346
  5.6 4.2 %collective-permute-start.1 = (bf16[4,2,8,256]{3,2,1,0:T(8,128)(2,1)S(1)}, bf16[4,2,8,256]{3,2,1,0:T(8,128)(2,1)S(1)}, u32[]{:S(2)}, u32[]{:S(2)}) collective-permute-start(bf16[4,2,8,256]{3,2,1,0:T(8,128)(2,1)S(1)} %get-tuple-element.18), channel_id=1, source_target_pairs={{0,4},{4,0},{8,12},{12,8},{16,20},{20,16},{24,28},{28,24},{1,5},{5... | collective-permute-start | bytes 98312 | tf_op jit(solution)/shard_map/ppermute | solution.py:397
  7.4 6.5 %copy-start.3 = (bf16[64,640]{1,0:T(8,128)(2,1)S(1)}, bf16[64,640]{1,0:T(8,128)(2,1)}, u32[]{:S(2)}) copy-start(bf16[64,640]{1,0:T(8,128)(2,1)} %get-tuple-element.19.told0) | copy-start | bytes 245764
  9.5 8.0 %collective-permute-start.7 = (bf16[64,2304]{1,0:T(8,128)(2,1)S(1)}, bf16[64,2304]{1,0:T(8,128)(2,1)S(1)}, u32[]{:S(2)}, u32[]{:S(2)}) collective-permute-start(bf16[64,2304]{1,0:T(8,128)(2,1)S(1)} %copy-done.9), channel_id=1, source_target_pairs={{0,2},{1,3},{2,0},{3,1},{4,6},{5,7},{6,4},{7,5},{8,10},{9,11},{10,... | collective-permute-start | bytes 884744 | tf_op jit(solution)/shard_map/ppermute | solution.py:346
  9.8 4.0 %collective-permute-start.9 = (bf16[64,384]{1,0:T(8,128)(2,1)S(1)}, bf16[64,384]{1,0:T(8,128)(2,1)S(1)}, u32[]{:S(2)}, u32[]{:S(2)}) collective-permute-start(bf16[64,384]{1,0:T(8,128)(2,1)S(1)} %collective-permute-done.8.ahead2.told2), channel_id=1, source_target_pairs={{0,1},{1,0},{2,3},{3,2},{4,5},{5,4},{6,7},{7,6},{8,9},{9,8},{10,11... | collective-permute-start | bytes 147464 | tf_op jit(solution)/shard_map/ppermute | solution.py:346
  9.8 4.0 %collective-permute-start.3 = (bf16[4,2,8,256]{3,2,1,0:T(8,128)(2,1)S(1)}, bf16[4,2,8,256]{3,2,1,0:T(8,128)(2,1)S(1)}, u32[]{:S(2)}, u32[]{:S(2)}) collective-permute-start(bf16[4,2,8,256]{3,2,1,0:T(8,128)(2,1)S(1)} %pad_maximum_fusion), channel_id=1, source_target_pairs={{0,8},{4,12},{8,0},{12,4},{16,24},{20,28},{24,16},{28,20},{1,9},{5... | collective-permute-start | bytes 98312 | tf_op jit(solution)/shard_map/ppermute | solution.py:397
  15.2 5.1 %copy-start.6 = (bf16[64,512]{1,0:T(8,128)(2,1)S(1)}, bf16[64,512]{1,0:T(8,128)(2,1)}, u32[]{:S(2)}) copy-start(bf16[64,512]{1,0:T(8,128)(2,1)} %kv0.1) | copy-start | bytes 196612
  15.2 6.6 %collective-permute-start.13 = (bf16[128,768]{1,0:T(8,128)(2,1)S(1)}, bf16[128,768]{1,0:T(8,128)(2,1)S(1)}, u32[]{:S(2)}, u32[]{:S(2)}) collective-permute-start(bf16[128,768]{1,0:T(8,128)(2,1)S(1)} %get-tuple-element.23), channel_id=1, source_target_pairs={{0,2},{1,3},{2,0},{3,1},{4,6},{5,7},{6,4},{7,5},{8,10},{9,11},{10,... | collective-permute-start | bytes 589832 | tf_op jit(solution)/shard_map/ppermute | solution.py:346
  17.6 2.9 %collective-permute-start.12 = (bf16[64,2304]{1,0:T(8,128)(2,1)S(1)}, bf16[64,2304]{1,0:T(8,128)(2,1)S(1)}, u32[]{:S(2)}, u32[]{:S(2)}) collective-permute-start(bf16[64,2304]{1,0:T(8,128)(2,1)S(1)} %collective-permute-done.7.far_ref), channel_id=1, source_target_pairs={{0,1},{1,0},{2,3},{3,2},{4,5},{5,4},{6,7},{7,6},{8,9},{9,8},{10,11... | collective-permute-start | bytes 884744 | tf_op jit(solution)/shard_map/ppermute | solution.py:346
  17.6 4.9 %collective-permute-start.4 = (bf16[4,2,8,256]{3,2,1,0:T(8,128)(2,1)S(1)}, bf16[4,2,8,256]{3,2,1,0:T(8,128)(2,1)S(1)}, u32[]{:S(2)}, u32[]{:S(2)}) collective-permute-start(bf16[4,2,8,256]{3,2,1,0:T(8,128)(2,1)S(1)} %pad_maximum_fusion.1), channel_id=1, source_target_pairs={{0,16},{4,20},{8,24},{12,28},{16,0},{20,4},{24,8},{28,12},{1,17},{... | collective-permute-start | bytes 98312 | tf_op jit(solution)/shard_map/ppermute | solution.py:397
  20.3 2.9 %collective-permute-start.6 = (bf16[64,512]{1,0:T(8,128)(2,1)S(1)}, bf16[64,512]{1,0:T(8,128)(2,1)S(1)}, u32[]{:S(2)}, u32[]{:S(2)}) collective-permute-start(bf16[64,512]{1,0:T(8,128)(2,1)S(1)} %copy-done.6), channel_id=1, source_target_pairs={{0,1},{1,0},{2,3},{3,2},{4,5},{5,4},{6,7},{7,6},{8,9},{9,8},{10,11... | collective-permute-start | bytes 196616 | tf_op jit(solution)/shard_map/ppermute | solution.py:346
  20.5 3.3 %copy-start.5 = (bf16[64,1536]{1,0:T(8,128)(2,1)S(1)}, bf16[64,1536]{1,0:T(8,128)(2,1)}, u32[]{:S(2)}) copy-start(bf16[64,1536]{1,0:T(8,128)(2,1)} %query_ref.1) | copy-start | bytes 589828
  21.8 2.8 %collective-permute-start.14 = (bf16[128,768]{1,0:T(8,128)(2,1)S(1)}, bf16[128,768]{1,0:T(8,128)(2,1)S(1)}, u32[]{:S(2)}, u32[]{:S(2)}) collective-permute-start(bf16[128,768]{1,0:T(8,128)(2,1)S(1)} %collective-permute-done.13.y2_ref), channel_id=1, source_target_pairs={{0,1},{1,0},{2,3},{3,2},{4,5},{5,4},{6,7},{7,6},{8,9},{9,8},{10,11... | collective-permute-start | bytes 589832 | tf_op jit(solution)/shard_map/ppermute | solution.py:346
  22.5 1.3 %collective-permute-start.5 = (bf16[8,2,8,256]{3,2,1,0:T(8,128)(2,1)S(1)}, bf16[8,2,8,256]{3,2,1,0:T(8,128)(2,1)S(1)}, u32[]{:S(2)}, u32[]{:S(2)}) collective-permute-start(bf16[8,2,8,256]{3,2,1,0:T(8,128)(2,1)S(1)} %constant_dynamic-update-slice_fusion.pages0), channel_id=1, source_target_pairs={{0,1},{1,0},{2,3},{3,2},{4,5},{5,4},{6,7},{7,6},{8,9},{9,8},{10,11... | collective-permute-start | bytes 196616 | tf_op jit(solution)/shard_map/ppermute | solution.py:346
  23.1 0.7 %copy-start.8 = (s32[1,8]{1,0:T(1,128)S(1)}, s32[1,8]{1,0:T(1,128)}, u32[]{:S(2)}) copy-start(s32[1,8]{1,0:T(1,128)} %page_map_ref.1) | copy-start | bytes 100
  23.8 1.0 %copy-start.2 = (bf16[64,3072]{1,0:T(8,128)(2,1)S(1)}, bf16[64,3072]{1,0:T(8,128)(2,1)}, u32[]{:S(2)}) copy-start(bf16[64,3072]{1,0:T(8,128)(2,1)} %gate_ref.1) | copy-start | bytes 1179652
  23.8 1.0 %copy-start.4 = (f32[3072]{0:T(1024)S(1)}, f32[3072]{0:T(1024)}, u32[]{:S(2)}) copy-start(f32[3072]{0:T(1024)} %param.29) | copy-start | bytes 36868
